TPU v7x, 256 devices: a whole 4x4x8 slice. The times are simulated.
256 devices in a mesh: outer: 16 (over z, y_lo), inner: 16 (over y_hi, x, core).
Axes of the slice: x: 4, y: 4 (y_hi: 2, y_lo: 2; y = y_hi * 2 + y_lo), z: 8, core: 2. Of those that a mesh axis runs over, the one named last changes fastest.
Arguments:
- tokens: bfloat16 [65536, 8192], P(('outer', 'inner')), may hold values from -6 to 6
- norm_gain: float32 [8192], replicated, may hold values from 0.25 to 1.75
- weight_codes: bfloat16 [8192, 512], P('inner'), may hold values from -1 to 1
- weight_scales: float32 [64, 512], P('inner'), may hold values from 0.006 to 0.04
- key_grad: bfloat16 [65536, 512], P(('outer', 'inner')), may hold values from -24 to 24
Outputs:
- key_out: bfloat16 [65536, 512], P(('outer', 'inner'))
- token_grad: bfloat16 [65536, 8192], P(('outer', 'inner'))
- weight_grad: float32 [8192, 512], P('inner', 'outer')
All inputs are finite; a program needn't handle non-finite values. Where the computation divides by a largest or mean magnitude, that divisor is 1e-20 or more.
Results may differ from a plain program's by a relative error of at most 0.015.
Values may be sent and summed in bfloat16 or wider, within the bound.
No kernel may reach another device: no remote copies, remote signals or barrier semaphores. Data moves between devices by JAX's collectives and lax.ppermute only.
A program may use at most 192 MiB of HBM per device.

v0:
```python
import jax
import jax.numpy as jnp
from jax import lax
from jax.sharding import PartitionSpec as P


def gathered_then(shard, axis, dim, work):
    return work(lax.all_gather(shard, axis, axis=dim, tiled=True), jnp.int32(0))


def quantize(matrix, group_rows):
    groups = matrix.reshape(-1, group_rows, matrix.shape[-1])
    group_scale = jnp.max(jnp.abs(groups), axis=1) + 1e-06
    code_vals = (groups / group_scale[:, None, :]).astype(jnp.bfloat16)
    return (code_vals, group_scale)


def unpack(code_vals, group_scale):
    values = code_vals.astype(jnp.float32) * group_scale[:, None, :]
    return values.astype(jnp.bfloat16).reshape(-1, code_vals.shape[-1])


def on_device(tokens, norm_gain, weight_codes, weight_scales, key_grad):
    group_rows = weight_codes.shape[0] // weight_scales.shape[0]
    width_cols = weight_codes.shape[1]
    values = tokens.astype(jnp.float32)
    mean_square = jnp.mean(values * values, axis=-1, keepdims=True)
    inverse = lax.rsqrt(mean_square + 1e-05)
    normed = (values * inverse * norm_gain).astype(jnp.bfloat16)
    coded = weight_codes.reshape(-1, group_rows, width_cols)
    contract = (((1,), (1,)), ((), ()))
    pieces = (
        lax.all_gather(coded, "inner", axis=0, tiled=True),
        lax.all_gather(weight_scales.astype(jnp.bfloat16), "inner", axis=0, tiled=True).astype(
            jnp.float32
        ),
    )
    weight = unpack(pieces[0], pieces[1])
    key_sum = jnp.dot(normed, weight, preferred_element_type=jnp.float32)

    def project(pieces):
        weight = unpack(pieces[0], pieces[1])
        return lax.dot_general(key_grad, weight, contract, preferred_element_type=jnp.float32)

    back_grad = gathered_then(
        (coded, weight_scales.astype(jnp.bfloat16)),
        "inner",
        0,
        lambda piece, start: project((piece[0], piece[1].astype(jnp.float32))),
    )
    key_out = key_sum.astype(jnp.bfloat16)
    scaled = back_grad * norm_gain
    average = jnp.mean(values * scaled, axis=-1, keepdims=True)
    token_grad = (inverse * scaled - values * inverse**3 * average).astype(jnp.bfloat16)
    n_inner = lax.axis_size("inner")
    n_outer = lax.axis_size("outer")
    partial_value = lax.dot_general(
        normed, key_grad, (((0,), (0,)), ((), ())), preferred_element_type=jnp.float32
    )
    code_vals, group_scale = quantize(partial_value, group_rows)
    code_vals = code_vals.reshape(n_inner, -1, group_rows, width_cols)
    group_scale = group_scale.reshape(n_inner, -1, width_cols)
    got_codes, got_scale = (
        lax.all_to_all(code_vals, "inner", split_axis=0, concat_axis=0, tiled=True),
        lax.all_to_all(
            group_scale.astype(jnp.bfloat16), "inner", split_axis=0, concat_axis=0, tiled=True
        ).astype(group_scale.dtype),
    )
    summed = jnp.sum(got_codes.astype(jnp.float32) * got_scale[:, :, None, :], axis=0).reshape(
        -1, width_cols
    )
    second_codes, second_scale = quantize(summed, group_rows)
    group_count = second_codes.shape[0]
    owned_cols = width_cols // n_outer
    second_codes = second_codes.reshape(group_count, group_rows, n_outer, owned_cols)
    second_scale = second_scale.reshape(group_count, 1, n_outer, owned_cols)
    final_codes, final_scale = (
        lax.all_to_all(second_codes, "outer", split_axis=2, concat_axis=2, tiled=True),
        lax.all_to_all(
            second_scale.astype(jnp.bfloat16), "outer", split_axis=2, concat_axis=2, tiled=True
        ).astype(second_scale.dtype),
    )
    weight_grad = jnp.sum(final_codes.astype(jnp.float32) * final_scale, axis=2).reshape(
        -1, owned_cols
    )
    return (key_out, token_grad, weight_grad)


def solution(mesh):
    in_specs = (
        P(("outer", "inner"), None),
        P(),
        P("inner", None),
        P("inner", None),
        P(("outer", "inner"), None),
    )
    out_specs = (P(("outer", "inner"), None), P(("outer", "inner"), None), P("inner", "outer"))
    return jax.shard_map(
        on_device, mesh=mesh, in_specs=in_specs, out_specs=out_specs, check_vma=False
    )
```

profile of v0, /device:TPU:6, one launch (start us, length us, event | category | flops | bytes accessed | tf_op | source)
XLA Modules:
  0.0 297.2 jit_solution(703245106358528413)
XLA Ops:
  7.2 0.0 copy-start
  7.2 0.0 all-gather.3.cloned.1.call-start
  7.2 0.7 all-gather.3.cloned.1.call-update
  7.9 0.7 convert_bitcast_fusion
  8.6 18.6 %all-gather = bf16[16,4,512]{2,1,0:T(4,128)(2,1)S(1)} all-gather(bf16[1,4,512]{2,1,0:T(4,128)(2,1)S(1)} %convert_bitcast_fusion), channel_id=1, replica_groups=mesh['outer'=16,'inner'=16] {'inner'}, dimensions={0}, use_global_device_ids=true | all-gather | bytes 69632 | tf_op jit(solution)/shard_map/all_gather | solution.py:34
  27.2 6.4 %copy.17 = bf16[256,8192]{0,1:T(8,128)(2,1)} copy(bf16[256,8192]{1,0:T(8,128)(2,1)} %param.5) | data formatting | bytes 8388608 | tf_op args[0]
  33.6 0.0 copy-start.3
  33.6 56.0 %all-gather.3.cloned.1.call-done = bf16[64,128,512]{2,1,0:T(8,128)(2,1)} async-done(((bf16[4,128,512]{2,1,0:T(8,128)(2,1)}), bf16[64,128,512]{2,1,0:T(8,128)(2,1)}) %all-gather.3.cloned.1.call-update) | async-done | bytes 8388624 | tf_op jit(solution)/shard_map/all_gather | solution.py:33
  89.7 0.0 copy-start.2
  89.7 9.8 %multiply_convert_fusion = bf16[64,128,512]{2,1,0:T(8,128)(2,1)} fusion(bf16[64,128,512]{2,1,0:T(8,128)(2,1)} %all-gather.3.cloned.1.call-done, f32[64,512]{1,0:T(8,128)S(1)} %reshape.90), kind=kLoop, calls=%fused_computation.3 | loop fusion | flops 12582912 | bytes 16908288 | tf_op jit(solution)/shard_map/convert_element_type | solution.py:20
  99.5 0.0 copy-done
  99.5 0.0 copy-done.3
  99.5 0.0 copy-done.2
  99.5 6.9 %fusion.7 = (f32[256]{0:T(256)S(1)}, f32[256]{0:T(256)S(1)}, f32[256,8192]{0,1:T(8,128)}) fusion(bf16[256,8192]{0,1:T(8,128)(2,1)S(1)} %copy-done.2, f32[8192]{0:T(1024)S(1)} %copy-done.3, bf16[8192,512]{1,0:T(8,128)(2,1)} %bitcast.23, bf16[256,512]{1,0:T(8,128)(2,1)S(1)} %copy-done), kind=kOutput, calls=%fused_computation.16 | convolution fusion | flops 2160066048 | bytes 21268480 | tf_op jit(solution)/shard_map/dot_general | solution.py:43
  106.4 7.2 %bitcast_reduce_fusion = (f32[64,512]{1,0:T(8,128)S(1)}, f32[8192,512]{1,0:T(8,128)}) fusion(bf16[256,512]{1,0:T(8,128)(2,1)S(1)} %copy-done, bf16[256,8192]{0,1:T(8,128)(2,1)S(1)} %copy-done.2, f32[8192]{0:T(1024)S(1)} %copy-done.3, f32[256]{0:T(256)S(1)} %get-tuple-element.20), kind=kOutput, calls=%fused_computation | convolution fusion | flops 2164228096 | bytes 21398528 | tf_op jit(solution)/shard_map/dot_general | solution.py:57
  113.7 0.7 convert_element_type.73
  114.3 5.7 %all-to-all-start.1 = ((bf16[16,4,512]{2,1,0:T(4,128)(2,1)}), bf16[16,4,512]{2,1,0:T(4,128)(2,1)S(1)}, u32[]{:S(2)}, u32[]{:S(2)}) async-start(bf16[16,4,512]{2,1,0:T(4,128)(2,1)} %convert_element_type.73), calls=%async_computation.1 | async-start | bytes 131072 | tf_op jit(solution)/shard_map/all_to_all | solution.py:65
  120.1 9.7 %divide_convert_fusion = bf16[16,4,128,512]{3,2,1,0:T(8,128)(2,1)} fusion(f32[16,4,128,512]{3,2,1,0:T(8,128)} %bitcast.22, f32[16,4,512]{2,1,0:T(4,128)S(1)} %add.54), kind=kLoop, calls=%fused_computation.2 | loop fusion | flops 8388608 | bytes 25296896 | tf_op jit(solution)/shard_map/convert_element_type | solution.py:14
  129.7 0.0 all-to-all-done.1
  129.7 7.3 %all-to-all-start = ((bf16[16,4,128,512]{3,2,1,0:T(8,128)(2,1)}), bf16[16,4,128,512]{3,2,1,0:T(8,128)(2,1)}, u32[]{:S(2)}, u32[]{:S(2)}) async-start(bf16[16,4,128,512]{3,2,1,0:T(8,128)(2,1)} %divide_convert_fusion), calls=%async_computation | async-start | bytes 16777216 | tf_op jit(solution)/shard_map/all_to_all | solution.py:64
  137.0 8.1 %fusion.6 = bf16[256,8192]{0,1:T(8,128)(2,1)} fusion(bf16[256,8192]{0,1:T(8,128)(2,1)} %copy.17, f32[256,8192]{0,1:T(8,128)} %get-tuple-element.21, f32[256]{0:T(256)S(1)} %get-tuple-element.24, f32[256]{0:T(256)S(1)} %get-tuple-element.19, f32[256]{0:T(256)S(1)} %get-tuple-element.20), kind=kLoop, calls=%fused_computation.15 | loop fusion | flops 12582912 | bytes 16780288 | tf_op jit(solution)/shard_map/convert_element_type | solution.py:54
  145.1 6.3 %copy.23 = bf16[256,8192]{1,0:T(8,128)(2,1)} copy(bf16[256,8192]{0,1:T(8,128)(2,1)} %fusion.6) | data formatting | bytes 8388608
  151.5 95.5 %all-to-all-done = bf16[16,4,128,512]{3,2,1,0:T(8,128)(2,1)} async-done(((bf16[16,4,128,512]{3,2,1,0:T(8,128)(2,1)}), bf16[16,4,128,512]{3,2,1,0:T(8,128)(2,1)}, u32[]{:S(2)}, u32[]{:S(2)}) %all-to-all-start) | async-done | bytes 8388640 | tf_op jit(solution)/shard_map/all_to_all | solution.py:64
  247.0 5.6 %multiply_reduce_fusion = f32[4,128,512]{2,1,0:T(8,128)S(1)} fusion(bf16[16,4,128,512]{3,2,1,0:T(8,128)(2,1)} %all-to-all-done, f32[16,4,512]{2,1,0:T(4,128)S(1)} %convert_element_type.74), kind=kLoop, calls=%fused_computation.1 | loop fusion | flops 12320768 | bytes 9568256 | tf_op jit(solution)/shard_map/reduce_sum | solution.py:69
  252.5 0.1 abs_reduce_fusion
  252.6 0.3 copy.18
  253.0 0.1 convert_element_type.78
  253.1 0.6 copy.20
  253.7 7.4 %all-to-all-start.3 = ((bf16[4,1,16,32]{3,0,1,2:T(4,128)(2,1)}), bf16[4,1,16,32]{3,0,1,2:T(4,128)(2,1)S(1)}, u32[]{:S(2)}, u32[]{:S(2)}) async-start(bf16[4,1,16,32]{3,0,1,2:T(4,128)(2,1)} %copy.20), calls=%async_computation.3 | async-start | bytes 32768 | tf_op jit(solution)/shard_map/all_to_all | solution.py:79
  261.1 0.1 add.57
  261.2 0.3 divide_convert_fusion.1
  261.5 0.8 copy.19
  262.3 7.3 %all-to-all-done.3 = bf16[4,1,16,32]{3,0,1,2:T(4,128)(2,1)S(1)} async-done(((bf16[4,1,16,32]{3,0,1,2:T(4,128)(2,1)}), bf16[4,1,16,32]{3,0,1,2:T(4,128)(2,1)S(1)}, u32[]{:S(2)}, u32[]{:S(2)}) %all-to-all-start.3) | async-done | bytes 4128 | tf_op jit(solution)/shard_map/all_to_all | solution.py:79
  269.6 3.6 %all-to-all-start.2 = ((bf16[4,128,16,32]{1,3,0,2:T(8,128)(2,1)}), bf16[4,128,16,32]{1,3,0,2:T(8,128)(2,1)S(1)}, u32[]{:S(2)}, u32[]{:S(2)}) async-start(bf16[4,128,16,32]{1,3,0,2:T(8,128)(2,1)} %copy.19), calls=%async_computation.2 | async-start | bytes 1048576 | tf_op jit(solution)/shard_map/all_to_all | solution.py:78
  273.2 0.0 copy-start.1
  273.2 10.0 %convolution_convert_fusion = bf16[256,512]{1,0:T(8,128)(2,1)} fusion(bf16[8192,512]{1,0:T(8,128)(2,1)} %bitcast.24, bf16[256,8192]{0,1:T(8,128)(2,1)} %copy.17, f32[8192]{0:T(1024)S(1)} %copy-done.3, f32[256]{0:T(256)S(1)} %get-tuple-element.20), kind=kOutput, calls=%fused_computation.17 | convolution fusion | flops 2156003328 | bytes 12878848 | tf_op jit(solution)/shard_map/dot_general | solution.py:39
  283.2 6.2 %all-to-all-done.2 = bf16[4,128,16,32]{1,3,0,2:T(8,128)(2,1)S(1)} async-done(((bf16[4,128,16,32]{1,3,0,2:T(8,128)(2,1)}), bf16[4,128,16,32]{1,3,0,2:T(8,128)(2,1)S(1)}, u32[]{:S(2)}, u32[]{:S(2)}) %all-to-all-start.2) | async-done | bytes 524320 | tf_op jit(solution)/shard_map/all_to_all | solution.py:78
  289.4 0.3 multiply_reduce_fusion.1
  289.7 0.6 copy_bitcast_fusion
  290.4 0.0 copy-done.1
  (7 shorter events, 0.1 us)
Async XLA Ops:
  7.2 92.3 %copy-start = (bf16[256,512]{1,0:T(8,128)(2,1)S(1)}, bf16[256,512]{1,0:T(8,128)(2,1)}, u32[]{:S(2)}) copy-start(bf16[256,512]{1,0:T(8,128)(2,1)} %param.9) | copy-start | bytes 786436
  7.2 82.5 %all-gather.3.cloned.1.call-start = ((), (), s32[]{:S(2)}) async-start(), calls=%async_computation.4 | async-start | bytes 8912896 | tf_op jit(solution)/shard_map/all_gather | solution.py:33
  33.6 65.8 %copy-start.3 = (f32[8192]{0:T(1024)S(1)}, f32[8192]{0:T(1024)}, u32[]{:S(2)}) copy-start(f32[8192]{0:T(1024)} %param.6) | copy-start | bytes 98308
  89.7 9.8 %copy-start.2 = (bf16[256,8192]{0,1:T(8,128)(2,1)S(1)}, bf16[256,8192]{0,1:T(8,128)(2,1)}, u32[]{:S(2)}) copy-start(bf16[256,8192]{0,1:T(8,128)(2,1)} %copy.17) | copy-start | bytes 12582916
  114.3 15.4 %all-to-all-start.1 = ((bf16[16,4,512]{2,1,0:T(4,128)(2,1)}), bf16[16,4,512]{2,1,0:T(4,128)(2,1)S(1)}, u32[]{:S(2)}, u32[]{:S(2)}) async-start(bf16[16,4,512]{2,1,0:T(4,128)(2,1)} %convert_element_type.73), calls=%async_computation.1 | async-start | bytes 131072 | tf_op jit(solution)/shard_map/all_to_all | solution.py:65
  129.7 117.2 %all-to-all-start = ((bf16[16,4,128,512]{3,2,1,0:T(8,128)(2,1)}), bf16[16,4,128,512]{3,2,1,0:T(8,128)(2,1)}, u32[]{:S(2)}, u32[]{:S(2)}) async-start(bf16[16,4,128,512]{3,2,1,0:T(8,128)(2,1)} %divide_convert_fusion), calls=%async_computation | async-start | bytes 16777216 | tf_op jit(solution)/shard_map/all_to_all | solution.py:64
  253.7 15.9 %all-to-all-start.3 = ((bf16[4,1,16,32]{3,0,1,2:T(4,128)(2,1)}), bf16[4,1,16,32]{3,0,1,2:T(4,128)(2,1)S(1)}, u32[]{:S(2)}, u32[]{:S(2)}) async-start(bf16[4,1,16,32]{3,0,1,2:T(4,128)(2,1)} %copy.20), calls=%async_computation.3 | async-start | bytes 32768 | tf_op jit(solution)/shard_map/all_to_all | solution.py:79
  269.6 19.7 %all-to-all-start.2 = ((bf16[4,128,16,32]{1,3,0,2:T(8,128)(2,1)}), bf16[4,128,16,32]{1,3,0,2:T(8,128)(2,1)S(1)}, u32[]{:S(2)}, u32[]{:S(2)}) async-start(bf16[4,128,16,32]{1,3,0,2:T(8,128)(2,1)} %copy.19), calls=%async_computation.2 | async-start | bytes 1048576 | tf_op jit(solution)/shard_map/all_to_all | solution.py:78
  273.2 17.1 %copy-start.1 = (bf16[256,512]{1,0:T(8,128)(2,1)S(1)}, bf16[256,512]{1,0:T(8,128)(2,1)}, u32[]{:S(2)}) copy-start(bf16[256,512]{1,0:T(8,128)(2,1)} %param.9) | copy-start | bytes 786436
Sparse Core Ops, SparseCore 0:
  10.7 78.8 all-gather.2
where the time goes:
time: 302 us; the launch traced here: 297 us
  waiting for transfers between devices  166 us (55%)
  other arithmetic  35.4 us (12%)
  matrix products  24.1 us (8%)
  starting transfers between devices  24 us (8%)
  blocking collectives  18.6 us (6%)
  local copies, waits for them, and re-layouts  15.4 us (5%)
  between operations  14.1 us (5%)
    all_to_all x1, waiting for transfers between devices, on_device(): lax.all_to_all(code_vals, 'inner', split_axis=0, concat_axis=0, tiled=True)  95.5 us
    all_gather x1, waiting for transfers between devices, on_device(): lax.all_gather(coded, 'inner', axis=0, tiled=True)  56 us
    all_gather x1, blocking collectives, on_device(): lax.all_gather(weight_scales.astype(jnp.bfloat16), 'inner', axis=0, tiled...  18.6 us
    unnamed x10, local copies, waits for them, and re-layouts  12.8 us
    convert_element_type x2, other arithmetic, quantize(): code_vals = (groups / group_scale[:, None, :]).astype(jnp.bfloat16)  10 us
    dot_general x1, matrix products, on_device(): key_sum = jnp.dot(normed, weight, preferred_element_type=jnp.float32)  9.95 us
    convert_element_type x1, other arithmetic, unpack(): return values.astype(jnp.bfloat16).reshape(-1, code_vals.shape[-1])  9.77 us
    convert_element_type x1, other arithmetic, on_device(): (inverse * scaled - values * inverse ** 3 * average).astype(jnp.bfloat16)  8.14 us
  transfers between devices with their start and end apart: 5, of which 4 were waited for; matrix products, arithmetic and copies ran while one was open for 14% of the time, Pallas kernels for 0%

commit v1 on v0

v1 whole, which is shorter than its diff:
```python
import functools

import jax
import jax.numpy as jnp
import numpy as np
from jax import lax
from jax.experimental import pallas as pl
from jax.experimental.pallas import tpu as pltpu
from jax.sharding import Mesh, PartitionSpec as P

BF, F32 = jnp.bfloat16, jnp.float32
NZ, NYL, NYH, NX, NC = 8, 2, 2, 4, 2
BLK, HALF = 512, 256
ROWS = (((0,), (0,)), ((), ()))
COLS = (((1,), (1,)), ((), ()))


def around(axis, size, step):
    return functools.partial(
        lax.ppermute, axis_name=axis, perm=[(i, (i + step) % size) for i in range(size)]
    )


def y_rank(y):
    return (y % 2) * 2 + (y // 2) % 2


def along_y(step):
    return functools.partial(
        lax.ppermute,
        axis_name=("yl", "yh"),
        perm=[(y_rank(y), y_rank((y + step) % 4)) for y in range(4)],
    )


swap_core = around("c", NC, 1)
swap_yh = around("yh", NYH, 1)


def vmem():
    return pl.BlockSpec(memory_space=pltpu.VMEM)


def smem():
    return pl.BlockSpec(memory_space=pltpu.SMEM)


def partial_kernel(where, tok_own, tok_far, kgt, *outs):
    x, yl, yh, c = where[0], where[1], where[2], where[3]

    def product(row0, rows, block, offset):
        own_col = pl.multiple_of((block * NC + c) * BLK + offset, HALF)
        far_col = pl.multiple_of(block * BLK + offset, HALF)
        left = kgt[pl.ds(row0, rows), :]
        return jnp.dot(
            left[:, :256], tok_own[:, pl.ds(own_col, HALF)], preferred_element_type=F32
        ) + jnp.dot(left[:, 256:], tok_far[:, pl.ds(far_col, HALF)], preferred_element_type=F32)

    for step in range(4):
        to = (x + step) % NX
        for h in range(NYH):
            outs[step][:, h * HALF : (h + 1) * HALF] = product(0, 512, h * NX + to, 0).astype(BF)
    y = yh * 2 + yl
    for step in range(4):
        to = (y + step) % 4
        row0 = pl.multiple_of((to % 2) * 256, 256)
        for q in range(NX):
            outs[4 + step][:, q * HALF : (q + 1) * HALF] = product(
                row0, 256, (to // 2) * NX + q, HALF
            ).astype(BF)


def partials(where, tok_own, tok_far, kgt):
    shapes = [jax.ShapeDtypeStruct((512, 512), BF)] * 4 + [
        jax.ShapeDtypeStruct((256, 1024), BF)
    ] * 4
    return pl.pallas_call(
        partial_kernel,
        out_shape=shapes,
        in_specs=[smem()] + [vmem()] * 3,
        out_specs=[vmem()] * 8,
        compiler_params=pltpu.CompilerParams(vmem_limit_bytes=40 * 2**20),
        cost_estimate=pl.CostEstimate(
            flops=2 * 512 * 512 * 4096, bytes_accessed=11 * 2**20, transcendentals=0
        ),
    )(where, tok_own, tok_far, kgt)


def project_kernel(where, tok_own, tok_far, kg, *refs):
    pieces, (key_own, key_far, grad_own, grad_far) = refs[:-4], refs[-4:]
    x, yh, c = where[0], where[2], where[3]
    key_own[...] = jnp.zeros_like(key_own)
    key_far[...] = jnp.zeros_like(key_far)
    for index in range(16):
        kind, hop, flip = index // 8, (index // 2) % 4, index % 2
        block = (yh + flip) % NYH * NX + (x + NX - hop) % NX
        offset = kind * HALF
        own_col = pl.multiple_of((block * NC + c) * BLK + offset, HALF)
        far_col = pl.multiple_of(block * BLK + offset, HALF)
        if kind == 0:
            weight = pieces[flip][hop * HALF : (hop + 1) * HALF, :]
        else:
            weight = pieces[2 + hop][flip * HALF : (flip + 1) * HALF, :]
        key_own[...] += jnp.dot(
            tok_own[:, pl.ds(own_col, HALF)], weight, preferred_element_type=F32
        )
        key_far[...] += jnp.dot(
            tok_far[:, pl.ds(far_col, HALF)], weight, preferred_element_type=F32
        )
        grads = lax.dot_general(kg[...], weight, COLS, preferred_element_type=F32).astype(BF)
        grad_own[:, pl.ds(far_col, HALF)] = grads[:256]
        grad_far[:, pl.ds(far_col, HALF)] = grads[256:]


def project(where, tok_own, tok_far, kg, pieces):
    return pl.pallas_call(
        project_kernel,
        out_shape=[jax.ShapeDtypeStruct((256, 512), F32)] * 2
        + [jax.ShapeDtypeStruct((256, 4096), BF)] * 2,
        in_specs=[smem()] + [vmem()] * (3 + len(pieces)),
        out_specs=[vmem()] * 4,
        compiler_params=pltpu.CompilerParams(vmem_limit_bytes=40 * 2**20),
        cost_estimate=pl.CostEstimate(
            flops=4 * 512 * 512 * 4096, bytes_accessed=16 * 2**20, transcendentals=0
        ),
    )(where, tok_own, tok_far, kg, *pieces)


def finish_kernel(where, tokens, grad_a, grad_b, slope, out):
    c = where[3]
    for block in range(NYH * NX):
        for refs, parity in ((grad_a, c), (grad_b, 1 - c)):
            col = pl.multiple_of((block * NC + parity) * BLK, BLK)
            part = refs[:, block * BLK : (block + 1) * BLK].astype(F32)
            values = tokens[:, pl.ds(col, BLK)].astype(F32)
            out[:, pl.ds(col, BLK)] = (part - values * slope[...]).astype(BF)


def finish(where, tokens, grad_a, grad_b, slope):
    return pl.pallas_call(
        finish_kernel,
        out_shape=jax.ShapeDtypeStruct((256, 8192), BF),
        in_specs=[smem()] + [vmem()] * 4,
        out_specs=vmem(),
        compiler_params=pltpu.CompilerParams(vmem_limit_bytes=40 * 2**20),
        cost_estimate=pl.CostEstimate(
            flops=2 * 256 * 8192, bytes_accessed=12 * 2**20, transcendentals=0
        ),
    )(where, tokens, grad_a, grad_b, slope)


def total(parts):
    out = parts[0].astype(F32)
    for part in parts[1:]:
        out = out + part.astype(F32)
    return out


def on_device(tokens, norm_gain, weight_codes, weight_scales, key_grad):
    x, yl, yh, c, z = [lax.axis_index(name) for name in ("x", "yl", "yh", "c", "z")]
    where = jnp.stack([x, yl, yh, c]).astype(jnp.int32)
    y = yh * 2 + yl
    shard = (yh * NX + x) * NC + c

    gain = lax.dynamic_slice(norm_gain, (shard * BLK,), (BLK,))
    weight = (
        weight_codes.reshape(4, 128, 512).astype(F32)
        * weight_scales[:, None, :]
        * gain.reshape(4, 128, 1)
    ).astype(BF).reshape(BLK, 512)
    w_a, w_b = weight[:HALF], weight[HALF:]
    a_parts = [w_a] + [around("x", NX, s)(w_a) for s in (1, 2, 3)]
    b_pair = jnp.concatenate([w_b, swap_yh(w_b)], axis=0)
    a_row = jnp.concatenate(a_parts, axis=0)
    pieces = [a_row, swap_yh(a_row), b_pair] + [around("x", NX, s)(b_pair) for s in (1, 2, 3)]

    blocks = tokens.reshape(256, NYH * NX, NC, BLK)
    send = lax.dynamic_index_in_dim(blocks, 1 - c, axis=2, keepdims=False).reshape(256, 4096)
    tok_far = swap_core(send)
    values = tokens.astype(F32)
    inverse = lax.rsqrt(jnp.mean(values * values, axis=-1, keepdims=True) + 1e-05)
    kg = (key_grad.astype(F32) * inverse).astype(BF)
    kg_both = jnp.concatenate([kg, swap_core(kg)], axis=0)
    kgt = (
        kg_both.T.reshape(NZ, NYL, 32, 512).transpose(1, 0, 2, 3).reshape(512, 512)
    )

    outs = partials(where, tokens, tok_far, kgt)
    a_sum = total([outs[0]] + [around("x", NX, s)(outs[s]) for s in (1, 2, 3)])
    b_sum = total([outs[4]] + [along_y(s)(outs[4 + s]) for s in (1, 2, 3)])
    a_sum = a_sum.astype(BF).reshape(NYL, 256, NYH, HALF)
    b_sum = b_sum.astype(BF).reshape(256, NX, HALF)

    def a_piece(step):
        to = (y + step) % 4
        return lax.dynamic_slice(a_sum, (to % 2, 0, to // 2, 0), (1, 256, 1, HALF)).reshape(256, HALF)

    def b_piece(step):
        to = (x + step) % NX
        return lax.dynamic_slice(b_sum, (0, to, 0), (256, 1, HALF)).reshape(256, HALF)

    a_done = total([a_piece(0)] + [along_y(s)(a_piece(s)) for s in (1, 2, 3)])
    b_done = total([b_piece(0)] + [around("x", NX, s)(b_piece(s)) for s in (1, 2, 3)])
    plane = jnp.concatenate([a_done, b_done], axis=1).astype(BF).reshape(NZ, 32, BLK)
    over_z = lax.all_to_all(plane, "z", split_axis=0, concat_axis=0, tiled=True)
    weight_grad = (jnp.sum(over_z.astype(F32), axis=0) * gain[None, :]).T

    key_own, key_far, grad_own, grad_far = project(where, tokens, tok_far, kg_both, pieces)
    key_sum = key_own + swap_core(key_far)
    key_out = (key_sum * inverse).astype(BF)
    dotted = jnp.sum(key_grad.astype(F32) * key_sum, axis=-1, keepdims=True) / 8192.0
    slope = inverse * inverse * inverse * dotted
    token_grad = finish(where, tokens, grad_own, swap_core(grad_far), slope)
    return key_out, token_grad, weight_grad


def solution(mesh):
    fine = Mesh(
        np.asarray(mesh.devices).reshape(NZ, NYL, NYH, NX, NC), ("z", "yl", "yh", "x", "c")
    )
    outer, inner = ("z", "yl"), ("yh", "x", "c")
    in_specs = (P(outer + inner, None), P(), P(inner, None), P(inner, None), P(outer + inner, None))
    out_specs = (P(outer + inner, None), P(outer + inner, None), P(inner, outer))
    return jax.shard_map(
        on_device, mesh=fine, in_specs=in_specs, out_specs=out_specs, check_vma=False
    )
```

time: 302 us -> 160 us (0.53); the launches traced: 297 us -> 159 us
  waiting for transfers between devices: 166 us -> 30.9 us
  local copies, waits for them, and re-layouts: 15.4 us -> 49.5 us
  matrix products: 24.1 us -> 0 us
  Pallas kernels: 0 us -> 19.5 us
  blocking collectives: 18.6 us -> 0 us
  other arithmetic: 35.4 us -> 16.8 us
  starting transfers between devices: 24 us -> 41.2 us
  between operations: 14.1 us -> 0.87 us
    all_to_all x4 -> x1, waiting for transfers between devices: 109 us -> 11.4 us  [on_device(): over_z = lax.all_to_all(plane, 'z', split_axis=0, concat_axis=0, tiled=True)]
    all_gather x1 -> x0, waiting for transfers between devices: 56 us -> none  [on_device(): lax.all_gather(coded, 'inner', axis=0, tiled=True)]
    ppermute x0 -> x24, starting transfers between devices: none -> 32.8 us  [the longest x3 9.76 us: on_device(): a_sum = total([outs[0]] + [around('x', NX, s)(outs[s]) for s in (1, 2, 3)])]
    dot_general x3 -> x0, matrix products: 24.1 us -> none  [the longest x1 9.95 us: on_device(): key_sum = jnp.dot(normed, weight, preferred_element_type=jnp.float32)]
    convert_element_type x7 -> x4, other arithmetic: 28.6 us -> 5.99 us  [the longest x1 2.52 us: on_device(): b_sum = b_sum.astype(BF).reshape(256, NX, HALF)]
    ppermute x0 -> x24, waiting for transfers between devices: none -> 19.6 us  [the longest x3 7.74 us: on_device(): a_parts = [w_a] + [around('x', NX, s)(w_a) for s in (1, 2, 3)]]
    pallas_call x0 -> x3, Pallas kernels: none -> 19.5 us  [the longest x1 9.15 us: project(): pl.pallas_call(project_kernel, out_shape=[jax.ShapeDtypeStruct((256, 512)...]
    all_gather x1 -> x0, blocking collectives: 18.6 us -> none  [on_device(): lax.all_gather(weight_scales.astype(jnp.bfloat16), 'inner', axis=0, tiled...]
  transfers between devices with their start and end apart: 5 -> 25, of which waited for: 4 -> 7; matrix products, arithmetic and copies ran while one was open for 14% -> 19% of each run, Pallas kernels for 0% -> 9%
where the time goes in v1:
time: 160 us; the launch traced here: 159 us
  local copies, waits for them, and re-layouts  49.5 us (31%)
  starting transfers between devices  41.2 us (26%)
  waiting for transfers between devices  30.9 us (19%)
  Pallas kernels  19.5 us (12%)
  other arithmetic  16.8 us (10%)
    unnamed x47, local copies, waits for them, and re-layouts  16.5 us
    dynamic_slice x1, local copies, waits for them, and re-layouts, on_device(): lax.dynamic_index_in_dim(blocks, 1 - c, axis=2, keepdims=False)  13.9 us
    all_to_all x1, waiting for transfers between devices, on_device(): over_z = lax.all_to_all(plane, 'z', split_axis=0, concat_axis=0, tiled=True)  11.4 us
    ppermute x3, starting transfers between devices, on_device(): a_sum = total([outs[0]] + [around('x', NX, s)(outs[s]) for s in (1, 2, 3)])  9.76 us
    pallas_call x1, Pallas kernels, project(): pl.pallas_call(project_kernel, out_shape=[jax.ShapeDtypeStruct((256, 512)...  9.15 us
    all_to_all x1, starting transfers between devices, on_device(): over_z = lax.all_to_all(plane, 'z', split_axis=0, concat_axis=0, tiled=True)  8.47 us
    reshape x1, local copies, waits for them, and re-layouts, on_device(): blocks = tokens.reshape(256, NYH * NX, NC, BLK)  7.79 us
    ppermute x3, waiting for transfers between devices, on_device(): a_parts = [w_a] + [around('x', NX, s)(w_a) for s in (1, 2, 3)]  7.74 us
  transfers between devices with their start and end apart: 25, of which 7 were waited for; matrix products, arithmetic and copies ran while one was open for 19% of the time, Pallas kernels for 9%

profile of v1, /device:TPU:6, one launch (start us, length us, event | category | flops | bytes accessed | tf_op | source)
XLA Modules:
  0.0 158.8 jit_solution(1311952820122380131)
XLA Ops:
  0.6 7.8 %reshape.109 = bf16[256,8,2,512]{3,2,1,0:T(2,128)(2,1)} reshape(bf16[256,8192]{1,0:T(8,128)(2,1)} %tok_own.3) | data formatting | bytes 8388608 | tf_op jit(solution)/shard_map/reshape | solution.py:177
  8.4 13.9 %dynamic-slice_reduce_fusion = bf16[256,8,512]{2,1,0:T(8,128)(2,1)S(1)} fusion(bf16[256,8,2,512]{3,2,1,0:T(2,128)(2,1)} %reshape.109, s32[]{:T(128)S(6)} %select_n.107), kind=kLoop, calls=%fused_computation.1 | loop fusion | bytes 4194308 | tf_op jit(solution)/shard_map/jit(dynamic_index_in_dim)/dynamic_slice | solution.py:178
  22.3 2.2 %copy.48 = bf16[32,8,8,512]{3,1,2,0:T(8,128)(2,1)} copy(bf16[32,8,8,512]{3,2,1,0:T(8,128)(2,1)S(1)} %bitcast.53) | data formatting | bytes 4194304
  25.5 2.3 %collective-permute-start.2 = (bf16[256,512]{1,0:T(8,128)(2,1)S(1)}, bf16[256,512]{1,0:T(8,128)(2,1)S(1)}, u32[]{:S(2)}, u32[]{:S(2)}) collective-permute-start(bf16[256,512]{1,0:T(8,128)(2,1)S(1)} %bitcast.57), channel_id=1, source_target_pairs={{0,2},{2,4},{4,6},{6,0},{1,3},{3,5},{5,7},{7,1},{8,10},{10,12},{12... | collective-permute-start | bytes 786440 | tf_op jit(solution)/shard_map/ppermute | solution.py:172
  28.7 2.9 %collective-permute-start.6 = (bf16[256,512]{1,0:T(8,128)(2,1)S(1)}, bf16[256,512]{1,0:T(8,128)(2,1)}, u32[]{:S(2)}, u32[]{:S(2)}) collective-permute-start(bf16[256,512]{1,0:T(8,128)(2,1)S(1)} %bitcast.55), channel_id=1, source_target_pairs={{0,8},{8,0},{1,9},{9,1},{2,10},{10,2},{3,11},{11,3},{4,12},{12,4},... | collective-permute-start | bytes 786440 | tf_op jit(solution)/shard_map/ppermute | solution.py:173
  31.7 3.1 %multiply_reduce_fusion = f32[256]{0:T(256)S(1)} fusion(bf16[256,8192]{1,0:T(8,128)(2,1)} %tok_own.3), kind=kLoop, calls=%fused_computation | loop fusion | flops 6291200 | bytes 4195328 | tf_op jit(solution)/shard_map/reduce_sum | solution.py:181
  35.6 4.1 %collective-permute-done.2 = bf16[256,512]{1,0:T(8,128)(2,1)S(1)} collective-permute-done((bf16[256,512]{1,0:T(8,128)(2,1)S(1)}, bf16[256,512]{1,0:T(8,128)(2,1)S(1)}, u32[]{:S(2)}, u32[]{:S(2)}) %collective-permute-start.2) | collective-permute-done | bytes 262176 | tf_op jit(solution)/shard_map/ppermute | solution.py:172
  39.7 3.7 %collective-permute-done.4 = bf16[256,512]{1,0:T(8,128)(2,1)S(1)} collective-permute-done((bf16[256,512]{1,0:T(8,128)(2,1)S(1)}, bf16[256,512]{1,0:T(8,128)(2,1)S(1)}, u32[]{:S(2)}, u32[]{:S(2)}) %collective-permute-start.4) | collective-permute-done | bytes 262176 | tf_op jit(solution)/shard_map/ppermute | solution.py:172
  43.4 1.5 collective-permute-start.5
  45.0 1.0 pad_maximum_fusion.2.refs_2_
  46.0 1.1 collective-permute-start.7
  47.1 2.1 %collective-permute-start.8 = (bf16[512,512]{1,0:T(8,128)(2,1)S(1)}, bf16[512,512]{1,0:T(8,128)(2,1)}, u32[]{:S(2)}, u32[]{:S(2)}) collective-permute-start(bf16[512,512]{1,0:T(8,128)(2,1)S(1)} %pad_maximum_fusion.2.refs_2_), channel_id=1, source_target_pairs={{0,4},{2,6},{4,0},{6,2},{1,5},{3,7},{5,1},{7,3},{8,12},{10,14},{12... | collective-permute-start | bytes 1572872 | tf_op jit(solution)/shard_map/ppermute | solution.py:175
  49.3 2.0 %fusion.10 = (bf16[512,512]{0,1:T(8,128)(2,1)}, bf16[512,512]{1,0:T(8,128)(2,1)}) fusion(bf16[256,512]{1,0:T(8,128)(2,1)S(1)} %collective-permute-done.1, bf16[256,512]{1,0:T(8,128)(2,1)} %fusion.2), kind=kLoop, calls=%fused_computation.46 | loop fusion | flops 1048576 | bytes 1572864 | tf_op jit(solution)/shard_map/transpose | solution.py:185
  51.3 2.1 %copy.29 = bf16[512,512]{1,0:T(8,128)(2,1)} copy(bf16[512,512]{0,1:T(8,128)(2,1)} %get-tuple-element.37) | data formatting | bytes 1048576 | tf_op jit(solution)/shard_map/transpose | solution.py:185
  53.4 1.1 copy.30
  54.5 2.2 %copy-done = bf16[256,8192]{1,0:T(8,128)(2,1)S(1)} copy-done((bf16[256,8192]{1,0:T(8,128)(2,1)S(1)}, bf16[256,8192]{1,0:T(8,128)(2,1)}, u32[]{:S(2)}) %copy-start) | copy-done | bytes 4194328
  56.7 5.4 %shard_map.78 = (bf16[512,512]{1,0:T(8,128)(2,1)S(1)}, bf16[512,512]{1,0:T(8,128)(2,1)}, bf16[512,512]{1,0:T(8,128)(2,1)}, bf16[512,512]{1,0:T(8,128)(2,1)}, bf1...) custom-call(s32[4]{0:T(128)S(1)} %pad_add_fusion.where, ...), custom_call_target="tpu_custom_call" | custom-call | flops 2147483648 | bytes 11534336 | tf_op jit(solution)/shard_map/pallas_call | solution.py:77
  63.7 3.1 %collective-permute-start.12 = (bf16[512,512]{1,0:T(8,128)(2,1)}, bf16[512,512]{1,0:T(8,128)(2,1)}, u32[]{:S(2)}, u32[]{:S(2)}) collective-permute-start(bf16[512,512]{1,0:T(8,128)(2,1)} %get-tuple-element.20), channel_id=1, source_target_pairs={{0,2},{2,4},{4,6},{6,0},{1,3},{3,5},{5,7},{7,1},{8,10},{10,12},{12... | collective-permute-start | bytes 1572872 | tf_op jit(solution)/shard_map/ppermute | solution.py:189
  67.1 6.4 %collective-permute-start.14 = (bf16[512,512]{1,0:T(8,128)(2,1)}, bf16[512,512]{1,0:T(8,128)(2,1)}, u32[]{:S(2)}, u32[]{:S(2)}) collective-permute-start(bf16[512,512]{1,0:T(8,128)(2,1)} %get-tuple-element.22), channel_id=1, source_target_pairs={{0,6},{2,0},{4,2},{6,4},{1,7},{3,1},{5,3},{7,5},{8,14},{10,8},{12,... | collective-permute-start | bytes 1572872 | tf_op jit(solution)/shard_map/ppermute | solution.py:189
  75.9 1.0 copy-done.11
  76.9 1.8 %collective-permute-start.19 = (bf16[256,1024]{1,0:T(8,128)(2,1)}, bf16[256,1024]{1,0:T(8,128)(2,1)}, u32[]{:S(2)}, u32[]{:S(2)}) collective-permute-start(bf16[256,1024]{1,0:T(8,128)(2,1)} %get-tuple-element.25), channel_id=1, source_target_pairs={{0,8},{16,24},{8,0},{24,16},{1,9},{17,25},{9,1},{25,17},{2,10},{18... | collective-permute-start | bytes 1572872 | tf_op jit(solution)/shard_map/ppermute | solution.py:190
  78.7 4.9 %collective-permute-done.12 = bf16[512,512]{1,0:T(8,128)(2,1)} collective-permute-done((bf16[512,512]{1,0:T(8,128)(2,1)}, bf16[512,512]{1,0:T(8,128)(2,1)}, u32[]{:S(2)}, u32[]{:S(2)}) %collective-permute-start.12) | collective-permute-done | bytes 524320 | tf_op jit(solution)/shard_map/ppermute | solution.py:189
  83.6 1.1 collective-permute-start.20
  84.6 1.0 copy-done.6
  85.7 1.0 copy-done.8
  86.7 1.2 copy-done.12
  87.9 1.0 copy-done.14
  89.0 9.1 %shard_map.76 = (f32[256,512]{1,0:T(8,128)S(1)}, f32[256,512]{1,0:T(8,128)}, bf16[256,4096]{1,0:T(8,128)(2,1)S(1)}, bf16[256,4096]{1,0:T(8,128)(2,1)}) custom-call(s32[4]{0:T(128)S(1)} %pad_add_fusion.where, bf16[256,8192]{1,0:T(8,128)(2,1)} %tok_own.3, bf16[256,4096]{1,0:T(8,128)(2,1)} %collective-permute-done.tok_far, bf16[512,512]{1,0:T(8,128)(2,1)S(1)} %copy-done.6, ...), custom_call_target="tpu_custom_call" | custom-call | flops 4294967296 | bytes 16777216 | tf_op jit(solution)/shard_map/pallas_call | solution.py:116
  98.1 0.8 copy-done.9
  99.5 2.5 %add_convert_fusion.1 = bf16[512,512]{1,0:T(8,128)(2,1)} fusion(bf16[512,512]{1,0:T(8,128)(2,1)} %collective-permute-done.14, bf16[512,512]{1,0:T(8,128)(2,1)} %collective-permute-done.13, bf16[512,512]{1,0:T(8,128)(2,1)} %collective-permute-done.12, bf16[512,512]{1,0:T(8,128)(2,1)S(1)} %copy-done.5), kind=kLoop, calls=%fused_computation.7 | loop fusion | flops 2097152 | bytes 2621440 | tf_op jit(solution)/shard_map/convert_element_type | solution.py:191
  102.0 1.2 reshape.113
  103.2 1.8 %constant_dynamic-slice_fusion.7 = (bf16[1,256,1,256]{3,2,1,0:T(2,128)(2,1)}, bf16[1,256,1,256]{3,2,1,0:T(2,128)(2,1)S(1)}, bf16[1,256,1,256]{3,2,1,0:T(2,128)(2,1)S(1)}, bf16[1,256,1,256]{3,2,1,0:T(2,128)(2,1)S(1)}) fusion(bf16[2,256,2,256]{3,2,1,0:T(2,128)(2,1)S(1)} %reshape.113, s32[]{:T(128)S(6)} %select_n.111, s32[]{:T(128)S(6)} %select_n.113, ...), kind=kLoop, calls=%fused_computation.42 | loop fusion | bytes 1048608 | tf_op jit(solution)/shard_map/dynamic_slice | solution.py:196
  107.0 1.0 collective-permute-start.15
  108.0 2.1 %collective-permute-start.16 = (bf16[256,256]{1,0:T(8,128)(2,1)}, bf16[256,256]{1,0:T(8,128)(2,1)}, u32[]{:S(2)}, u32[]{:S(2)}) collective-permute-start(bf16[256,256]{1,0:T(8,128)(2,1)} %bitcast.50), channel_id=1, source_target_pairs={{0,8},{16,24},{8,0},{24,16},{1,9},{17,25},{9,1},{25,17},{2,10},{18... | collective-permute-start | bytes 393224 | tf_op jit(solution)/shard_map/ppermute | solution.py:202
  110.1 1.3 collective-permute-start.17
  111.4 2.5 %add_convert_fusion = bf16[256,1024]{1,0:T(8,128)(2,1)} fusion(bf16[256,1024]{1,0:T(8,128)(2,1)} %collective-permute-done.20, bf16[256,1024]{1,0:T(8,128)(2,1)} %collective-permute-done.19, bf16[256,1024]{1,0:T(8,128)(2,1)} %collective-permute-done.18, bf16[256,1024]{1,0:T(8,128)(2,1)S(1)} %copy-done.3), kind=kLoop, calls=%fused_computation.6 | loop fusion | flops 2097152 | bytes 2621440 | tf_op jit(solution)/shard_map/convert_element_type | solution.py:192
  113.9 1.5 reshape.117
  115.4 1.1 constant_dynamic-slice_fusion.3
  116.5 2.7 %collective-permute-start.21 = (bf16[256,256]{1,0:T(8,128)(2,1)S(1)}, bf16[256,256]{1,0:T(8,128)(2,1)S(1)}, u32[]{:S(2)}, u32[]{:S(2)}) collective-permute-start(bf16[256,256]{1,0:T(8,128)(2,1)S(1)} %bitcast.64), channel_id=1, source_target_pairs={{0,2},{2,4},{4,6},{6,0},{1,3},{3,5},{5,7},{7,1},{8,10},{10,12},{12... | collective-permute-start | bytes 393224 | tf_op jit(solution)/shard_map/ppermute | solution.py:203
  119.2 1.9 %fusion.3 = (f32[256]{0:T(256)S(1)}, bf16[256,512]{1,0:T(8,128)(2,1)}) fusion(bf16[256,512]{1,0:T(8,128)(2,1)S(1)} %copy-done.15, f32[256,512]{1,0:T(8,128)S(1)} %copy-done.10, f32[256,512]{1,0:T(8,128)} %collective-permute-done.10, f32[256]{0:T(256)S(1)} %add_rsqrt_fusion), kind=kLoop, calls=%fused_computation.11 | loop fusion | flops 786176 | bytes 1574912 | tf_op jit(solution)/shard_map/reduce_sum | solution.py:211
  122.2 1.1 fusion.9
  123.3 1.3 collective-permute-done.21
  124.5 4.3 %collective-permute-done.22 = bf16[256,256]{1,0:T(8,128)(2,1)S(1)} collective-permute-done((bf16[256,256]{1,0:T(8,128)(2,1)S(1)}, bf16[256,256]{1,0:T(8,128)(2,1)S(1)}, u32[]{:S(2)}, u32[]{:S(2)}) %collective-permute-start.22) | collective-permute-done | bytes 131104 | tf_op jit(solution)/shard_map/ppermute | solution.py:203
  128.9 1.3 collective-permute-done.23
  131.0 8.5 %all-to-all-start = ((bf16[8,32,512]{2,1,0:T(8,128)(2,1)}), bf16[8,32,512]{2,1,0:T(8,128)(2,1)S(1)}, u32[]{:S(2)}, u32[]{:S(2)}) async-start(bf16[8,32,512]{2,1,0:T(8,128)(2,1)} %pad_maximum_fusion.3), calls=%async_computation | async-start | bytes 524288 | tf_op jit(solution)/shard_map/all_to_all | solution.py:205
  139.6 11.4 %all-to-all-done = bf16[8,32,512]{2,1,0:T(8,128)(2,1)S(1)} async-done(((bf16[8,32,512]{2,1,0:T(8,128)(2,1)}), bf16[8,32,512]{2,1,0:T(8,128)(2,1)S(1)}, u32[]{:S(2)}, u32[]{:S(2)}) %all-to-all-start) | async-done | bytes 262176 | tf_op jit(solution)/shard_map/all_to_all | solution.py:205
  151.7 2.2 %copy-done.1 = bf16[256,8192]{1,0:T(8,128)(2,1)S(1)} copy-done((bf16[256,8192]{1,0:T(8,128)(2,1)S(1)}, bf16[256,8192]{1,0:T(8,128)(2,1)}, u32[]{:S(2)}) %copy-start.1) | copy-done | bytes 4194328
  153.9 5.0 %shard_map.77 = bf16[256,8192]{1,0:T(8,128)(2,1)} custom-call(s32[4]{0:T(128)S(1)} %pad_add_fusion.where, bf16[256,8192]{1,0:T(8,128)(2,1)S(1)} %copy-done.1, bf16[256,4096]{1,0:T(8,128)(2,1)S(1)} %get-tuple-element.17.grad_a, bf16[256,4096]{1,0:T(8,128)(2,1)} %collective-permute-done.11.grad_b, f32[256,1]{1,0:T(8,128)S(1)} %multiply_multiply_fusion.slope), custom_call_target="tpu_custom_call" | custom-call | flops 4194304 | bytes 12582912 | tf_op jit(solution)/shard_map/pallas_call | solution.py:140
  (85 shorter events, 12.6 us)
Async XLA Ops:
  22.3 3.0 %copy-start.17 = (bf16[512,512]{1,0:T(8,128)(2,1)S(1)}, bf16[512,512]{1,0:T(8,128)(2,1)}, u32[]{:S(2)}) copy-start(bf16[512,512]{1,0:T(8,128)(2,1)} %param.7) | copy-start | bytes 1572868
  22.3 3.0 %copy-start.19 = (f32[4,512]{1,0:T(4,128)S(1)}, f32[4,512]{1,0:T(4,128)}, u32[]{:S(2)}) copy-start(f32[4,512]{1,0:T(4,128)} %param.8) | copy-start | bytes 24580
  24.5 30.0 %collective-permute-start = (bf16[256,4096]{1,0:T(8,128)(2,1)}, bf16[256,4096]{1,0:T(8,128)(2,1)}, u32[]{:S(2)}, u32[]{:S(2)}) collective-permute-start(bf16[256,4096]{1,0:T(8,128)(2,1)} %bitcast.30), channel_id=1, source_target_pairs={{0,1},{1,0},{2,3},{3,2},{4,5},{5,4},{6,7},{7,6},{8,9},{9,8},{10,11... | collective-permute-start | bytes 6291464 | tf_op jit(solution)/shard_map/ppermute | solution.py:179
  25.5 14.2 %collective-permute-start.2 = (bf16[256,512]{1,0:T(8,128)(2,1)S(1)}, bf16[256,512]{1,0:T(8,128)(2,1)S(1)}, u32[]{:S(2)}, u32[]{:S(2)}) collective-permute-start(bf16[256,512]{1,0:T(8,128)(2,1)S(1)} %bitcast.57), channel_id=1, source_target_pairs={{0,2},{2,4},{4,6},{6,0},{1,3},{3,5},{5,7},{7,1},{8,10},{10,12},{12... | collective-permute-start | bytes 786440 | tf_op jit(solution)/shard_map/ppermute | solution.py:172
  27.8 11.9 %collective-permute-start.3 = (bf16[256,512]{1,0:T(8,128)(2,1)S(1)}, bf16[256,512]{1,0:T(8,128)(2,1)S(1)}, u32[]{:S(2)}, u32[]{:S(2)}) collective-permute-start(bf16[256,512]{1,0:T(8,128)(2,1)S(1)} %bitcast.58), channel_id=1, source_target_pairs={{0,4},{2,6},{4,0},{6,2},{1,5},{3,7},{5,1},{7,3},{8,12},{10,14},{12... | collective-permute-start | bytes 786440 | tf_op jit(solution)/shard_map/ppermute | solution.py:172
  28.5 14.9 %collective-permute-start.4 = (bf16[256,512]{1,0:T(8,128)(2,1)S(1)}, bf16[256,512]{1,0:T(8,128)(2,1)S(1)}, u32[]{:S(2)}, u32[]{:S(2)}) collective-permute-start(bf16[256,512]{1,0:T(8,128)(2,1)S(1)} %bitcast.59), channel_id=1, source_target_pairs={{0,6},{2,0},{4,2},{6,4},{1,7},{3,1},{5,3},{7,5},{8,14},{10,8},{12,... | collective-permute-start | bytes 786440 | tf_op jit(solution)/shard_map/ppermute | solution.py:172
  28.7 6.0 %copy-start.15 = (bf16[256,512]{1,0:T(8,128)(2,1)S(1)}, bf16[256,512]{1,0:T(8,128)(2,1)}, u32[]{:S(2)}) copy-start(bf16[256,512]{1,0:T(8,128)(2,1)} %param.9) | copy-start | bytes 786436
  28.7 16.3 %collective-permute-start.6 = (bf16[256,512]{1,0:T(8,128)(2,1)S(1)}, bf16[256,512]{1,0:T(8,128)(2,1)}, u32[]{:S(2)}, u32[]{:S(2)}) collective-permute-start(bf16[256,512]{1,0:T(8,128)(2,1)S(1)} %bitcast.55), channel_id=1, source_target_pairs={{0,8},{8,0},{1,9},{9,1},{2,10},{10,2},{3,11},{11,3},{4,12},{12,4},... | collective-permute-start | bytes 786440 | tf_op jit(solution)/shard_map/ppermute | solution.py:173
  39.7 9.5 %collective-permute-start.1 = (bf16[256,512]{1,0:T(8,128)(2,1)}, bf16[256,512]{1,0:T(8,128)(2,1)S(1)}, u32[]{:S(2)}, u32[]{:S(2)}) collective-permute-start(bf16[256,512]{1,0:T(8,128)(2,1)} %fusion.2), channel_id=1, source_target_pairs={{0,1},{1,0},{2,3},{3,2},{4,5},{5,4},{6,7},{7,6},{8,9},{9,8},{10,11... | collective-permute-start | bytes 786440 | tf_op jit(solution)/shard_map/ppermute | solution.py:183
  43.4 32.5 %collective-permute-start.5 = (bf16[1024,512]{1,0:T(8,128)(2,1)S(1)}, bf16[1024,512]{1,0:T(8,128)(2,1)S(1)}, u32[]{:S(2)}, u32[]{:S(2)}) collective-permute-start(bf16[1024,512]{1,0:T(8,128)(2,1)S(1)} %pad_maximum_fusion.refs_0_), channel_id=1, source_target_pairs={{0,8},{8,0},{1,9},{9,1},{2,10},{10,2},{3,11},{11,3},{4,12},{12,4},... | collective-permute-start | bytes 3145736 | tf_op jit(solution)/shard_map/ppermute | solution.py:175
  46.0 16.1 %copy-start.7 = (bf16[512,512]{1,0:T(8,128)(2,1)}, bf16[512,512]{1,0:T(8,128)(2,1)S(1)}, u32[]{:S(2)}) copy-start(bf16[512,512]{1,0:T(8,128)(2,1)S(1)} %pad_maximum_fusion.2.refs_2_) | copy-start | bytes 1572868
  46.0 20.8 %collective-permute-start.7 = (bf16[512,512]{1,0:T(8,128)(2,1)S(1)}, bf16[512,512]{1,0:T(8,128)(2,1)S(1)}, u32[]{:S(2)}, u32[]{:S(2)}) collective-permute-start(bf16[512,512]{1,0:T(8,128)(2,1)S(1)} %pad_maximum_fusion.2.refs_2_), channel_id=1, source_target_pairs={{0,2},{2,4},{4,6},{6,0},{1,3},{3,5},{5,7},{7,1},{8,10},{10,12},{12... | collective-permute-start | bytes 1572872 | tf_op jit(solution)/shard_map/ppermute | solution.py:175
  47.1 20.0 %collective-permute-start.8 = (bf16[512,512]{1,0:T(8,128)(2,1)S(1)}, bf16[512,512]{1,0:T(8,128)(2,1)}, u32[]{:S(2)}, u32[]{:S(2)}) collective-permute-start(bf16[512,512]{1,0:T(8,128)(2,1)S(1)} %pad_maximum_fusion.2.refs_2_), channel_id=1, source_target_pairs={{0,4},{2,6},{4,0},{6,2},{1,5},{3,7},{5,1},{7,3},{8,12},{10,14},{12... | collective-permute-start | bytes 1572872 | tf_op jit(solution)/shard_map/ppermute | solution.py:175
  49.1 26.1 %collective-permute-start.9 = (bf16[512,512]{1,0:T(8,128)(2,1)S(1)}, bf16[512,512]{1,0:T(8,128)(2,1)}, u32[]{:S(2)}, u32[]{:S(2)}) collective-permute-start(bf16[512,512]{1,0:T(8,128)(2,1)S(1)} %pad_maximum_fusion.2.refs_2_), channel_id=1, source_target_pairs={{0,6},{2,0},{4,2},{6,4},{1,7},{3,1},{5,3},{7,5},{8,14},{10,8},{12,... | collective-permute-start | bytes 1572872 | tf_op jit(solution)/shard_map/ppermute | solution.py:175
  54.5 2.2 %copy-start = (bf16[256,8192]{1,0:T(8,128)(2,1)S(1)}, bf16[256,8192]{1,0:T(8,128)(2,1)}, u32[]{:S(2)}) copy-start(bf16[256,8192]{1,0:T(8,128)(2,1)} %tok_own.3) | copy-start | bytes 12582916
  62.1 0.8 copy-start.2
  62.9 0.8 copy-start.4
  63.7 19.8 %collective-permute-start.12 = (bf16[512,512]{1,0:T(8,128)(2,1)}, bf16[512,512]{1,0:T(8,128)(2,1)}, u32[]{:S(2)}, u32[]{:S(2)}) collective-permute-start(bf16[512,512]{1,0:T(8,128)(2,1)} %get-tuple-element.20), channel_id=1, source_target_pairs={{0,2},{2,4},{4,6},{6,0},{1,3},{3,5},{5,7},{7,1},{8,10},{10,12},{12... | collective-permute-start | bytes 1572872 | tf_op jit(solution)/shard_map/ppermute | solution.py:189
  66.8 17.8 %copy-start.13 = (bf16[512,512]{1,0:T(8,128)(2,1)}, bf16[512,512]{1,0:T(8,128)(2,1)S(1)}, u32[]{:S(2)}) copy-start(bf16[512,512]{1,0:T(8,128)(2,1)S(1)} %collective-permute-done.7.refs_3_) | copy-start | bytes 1572868
  66.8 32.1 %collective-permute-start.13 = (bf16[512,512]{1,0:T(8,128)(2,1)}, bf16[512,512]{1,0:T(8,128)(2,1)}, u32[]{:S(2)}, u32[]{:S(2)}) collective-permute-start(bf16[512,512]{1,0:T(8,128)(2,1)} %get-tuple-element.21), channel_id=1, source_target_pairs={{0,4},{2,6},{4,0},{6,2},{1,5},{3,7},{5,1},{7,3},{8,12},{10,14},{12... | collective-permute-start | bytes 1572872 | tf_op jit(solution)/shard_map/ppermute | solution.py:189
  67.1 31.8 %collective-permute-start.14 = (bf16[512,512]{1,0:T(8,128)(2,1)}, bf16[512,512]{1,0:T(8,128)(2,1)}, u32[]{:S(2)}, u32[]{:S(2)}) collective-permute-start(bf16[512,512]{1,0:T(8,128)(2,1)} %get-tuple-element.22), channel_id=1, source_target_pairs={{0,6},{2,0},{4,2},{6,4},{1,7},{3,1},{5,3},{7,5},{8,14},{10,8},{12,... | collective-permute-start | bytes 1572872 | tf_op jit(solution)/shard_map/ppermute | solution.py:189
  75.2 31.8 %collective-permute-start.18 = (bf16[256,1024]{1,0:T(8,128)(2,1)}, bf16[256,1024]{1,0:T(8,128)(2,1)}, u32[]{:S(2)}, u32[]{:S(2)}) collective-permute-start(bf16[256,1024]{1,0:T(8,128)(2,1)} %get-tuple-element.24), channel_id=1, source_target_pairs={{0,16},{16,8},{8,24},{24,0},{1,17},{17,9},{9,25},{25,1},{2,18},{18... | collective-permute-start | bytes 1572872 | tf_op jit(solution)/shard_map/ppermute | solution.py:190
  75.9 1.0 copy-start.11
  76.9 31.2 %collective-permute-start.19 = (bf16[256,1024]{1,0:T(8,128)(2,1)}, bf16[256,1024]{1,0:T(8,128)(2,1)}, u32[]{:S(2)}, u32[]{:S(2)}) collective-permute-start(bf16[256,1024]{1,0:T(8,128)(2,1)} %get-tuple-element.25), channel_id=1, source_target_pairs={{0,8},{16,24},{8,0},{24,16},{1,9},{17,25},{9,1},{25,17},{2,10},{18... | collective-permute-start | bytes 1572872 | tf_op jit(solution)/shard_map/ppermute | solution.py:190
  83.6 26.5 %collective-permute-start.20 = (bf16[256,1024]{1,0:T(8,128)(2,1)}, bf16[256,1024]{1,0:T(8,128)(2,1)}, u32[]{:S(2)}, u32[]{:S(2)}) collective-permute-start(bf16[256,1024]{1,0:T(8,128)(2,1)} %get-tuple-element.26), channel_id=1, source_target_pairs={{0,24},{16,0},{8,16},{24,8},{1,25},{17,1},{9,17},{25,9},{2,26},{18... | collective-permute-start | bytes 1572872 | tf_op jit(solution)/shard_map/ppermute | solution.py:190
  84.6 1.0 copy-start.6
  85.7 1.0 copy-start.8
  86.7 1.2 copy-start.12
  87.9 1.0 copy-start.14
  89.0 10.5 %copy-start.5 = (bf16[512,512]{1,0:T(8,128)(2,1)S(1)}, bf16[512,512]{1,0:T(8,128)(2,1)}, u32[]{:S(2)}) copy-start(bf16[512,512]{1,0:T(8,128)(2,1)} %copy-done.4) | copy-start | bytes 1572868
  98.1 0.8 copy-start.9
  98.9 52.7 %collective-permute-start.11 = (bf16[256,4096]{1,0:T(8,128)(2,1)}, bf16[256,4096]{1,0:T(8,128)(2,1)}, u32[]{:S(2)}, u32[]{:S(2)}) collective-permute-start(bf16[256,4096]{1,0:T(8,128)(2,1)} %get-tuple-element.18), channel_id=1, source_target_pairs={{0,1},{1,0},{2,3},{3,2},{4,5},{5,4},{6,7},{7,6},{8,9},{9,8},{10,11... | collective-permute-start | bytes 6291464 | tf_op jit(solution)/shard_map/ppermute | solution.py:213
  99.0 17.6 %collective-permute-start.10 = (f32[256,512]{1,0:T(8,128)}, f32[256,512]{1,0:T(8,128)}, u32[]{:S(2)}, u32[]{:S(2)}) collective-permute-start(f32[256,512]{1,0:T(8,128)} %get-tuple-element.16), channel_id=1, source_target_pairs={{0,1},{1,0},{2,3},{3,2},{4,5},{5,4},{6,7},{7,6},{8,9},{9,8},{10,11... | collective-permute-start | bytes 1572872 | tf_op jit(solution)/shard_map/ppermute | solution.py:209
  102.0 9.4 %copy-start.3 = (bf16[256,1024]{1,0:T(8,128)(2,1)S(1)}, bf16[256,1024]{1,0:T(8,128)(2,1)}, u32[]{:S(2)}) copy-start(bf16[256,1024]{1,0:T(8,128)(2,1)} %copy-done.2) | copy-start | bytes 1572868
  107.0 14.2 %collective-permute-start.15 = (bf16[256,256]{1,0:T(8,128)(2,1)}, bf16[256,256]{1,0:T(8,128)(2,1)}, u32[]{:S(2)}, u32[]{:S(2)}) collective-permute-start(bf16[256,256]{1,0:T(8,128)(2,1)} %bitcast.51), channel_id=1, source_target_pairs={{0,16},{16,8},{8,24},{24,0},{1,17},{17,9},{9,25},{25,1},{2,18},{18... | collective-permute-start | bytes 393224 | tf_op jit(solution)/shard_map/ppermute | solution.py:202
  108.0 13.8 %collective-permute-start.16 = (bf16[256,256]{1,0:T(8,128)(2,1)}, bf16[256,256]{1,0:T(8,128)(2,1)}, u32[]{:S(2)}, u32[]{:S(2)}) collective-permute-start(bf16[256,256]{1,0:T(8,128)(2,1)} %bitcast.50), channel_id=1, source_target_pairs={{0,8},{16,24},{8,0},{24,16},{1,9},{17,25},{9,1},{25,17},{2,10},{18... | collective-permute-start | bytes 393224 | tf_op jit(solution)/shard_map/ppermute | solution.py:202
  110.1 12.1 %collective-permute-start.17 = (bf16[256,256]{1,0:T(8,128)(2,1)}, bf16[256,256]{1,0:T(8,128)(2,1)}, u32[]{:S(2)}, u32[]{:S(2)}) collective-permute-start(bf16[256,256]{1,0:T(8,128)(2,1)} %bitcast.49), channel_id=1, source_target_pairs={{0,24},{16,0},{8,16},{24,8},{1,25},{17,1},{9,17},{25,9},{2,26},{18... | collective-permute-start | bytes 393224 | tf_op jit(solution)/shard_map/ppermute | solution.py:202
  113.9 5.3 %copy-start.10 = (f32[256,512]{1,0:T(8,128)S(1)}, f32[256,512]{1,0:T(8,128)}, u32[]{:S(2)}) copy-start(f32[256,512]{1,0:T(8,128)} %copy-done.9) | copy-start | bytes 1572868
  115.4 6.8 %copy-start.16 = (bf16[1,256,1,256]{3,2,1,0:T(2,128)(2,1)S(1)}, bf16[1,256,1,256]{3,2,1,0:T(2,128)(2,1)}, u32[]{:S(2)}) copy-start(bf16[1,256,1,256]{3,2,1,0:T(2,128)(2,1)} %get-tuple-element.29) | copy-start | bytes 393220
  116.5 8.0 %collective-permute-start.21 = (bf16[256,256]{1,0:T(8,128)(2,1)S(1)}, bf16[256,256]{1,0:T(8,128)(2,1)S(1)}, u32[]{:S(2)}, u32[]{:S(2)}) collective-permute-start(bf16[256,256]{1,0:T(8,128)(2,1)S(1)} %bitcast.64), channel_id=1, source_target_pairs={{0,2},{2,4},{4,6},{6,0},{1,3},{3,5},{5,7},{7,1},{8,10},{10,12},{12... | collective-permute-start | bytes 393224 | tf_op jit(solution)/shard_map/ppermute | solution.py:203
  121.1 18.5 %copy-start.18 = (f32[256,1]{1,0:T(8,128)S(1)}, f32[256,1]{1,0:T(8,128)}, u32[]{:S(2)}) copy-start(f32[256,1]{1,0:T(8,128)} %copy.26) | copy-start | bytes 3076
  121.2 7.7 %collective-permute-start.22 = (bf16[256,256]{1,0:T(8,128)(2,1)S(1)}, bf16[256,256]{1,0:T(8,128)(2,1)S(1)}, u32[]{:S(2)}, u32[]{:S(2)}) collective-permute-start(bf16[256,256]{1,0:T(8,128)(2,1)S(1)} %bitcast.66), channel_id=1, source_target_pairs={{0,4},{2,6},{4,0},{6,2},{1,5},{3,7},{5,1},{7,3},{8,12},{10,14},{12... | collective-permute-start | bytes 393224 | tf_op jit(solution)/shard_map/ppermute | solution.py:203
  121.9 8.3 %collective-permute-start.23 = (bf16[256,256]{1,0:T(8,128)(2,1)S(1)}, bf16[256,256]{1,0:T(8,128)(2,1)S(1)}, u32[]{:S(2)}, u32[]{:S(2)}) collective-permute-start(bf16[256,256]{1,0:T(8,128)(2,1)S(1)} %bitcast.65), channel_id=1, source_target_pairs={{0,6},{2,0},{4,2},{6,4},{1,7},{3,1},{5,3},{7,5},{8,14},{10,8},{12,... | collective-permute-start | bytes 393224 | tf_op jit(solution)/shard_map/ppermute | solution.py:203
  131.0 20.0 %all-to-all-start = ((bf16[8,32,512]{2,1,0:T(8,128)(2,1)}), bf16[8,32,512]{2,1,0:T(8,128)(2,1)S(1)}, u32[]{:S(2)}, u32[]{:S(2)}) async-start(bf16[8,32,512]{2,1,0:T(8,128)(2,1)} %pad_maximum_fusion.3), calls=%async_computation | async-start | bytes 524288 | tf_op jit(solution)/shard_map/all_to_all | solution.py:205
  151.7 2.2 %copy-start.1 = (bf16[256,8192]{1,0:T(8,128)(2,1)S(1)}, bf16[256,8192]{1,0:T(8,128)(2,1)}, u32[]{:S(2)}) copy-start(bf16[256,8192]{1,0:T(8,128)(2,1)} %tok_own.3) | copy-start | bytes 12582916

commit v2 on v0

v2 whole, which is shorter than its diff:
```python
import jax
import jax.numpy as jnp
import numpy as np
from jax import lax
from jax.experimental import pallas as pl
from jax.experimental.pallas import tpu as pltpu
from jax.sharding import Mesh, PartitionSpec as P

BF, F32 = jnp.bfloat16, jnp.float32
NZ, NYL, NYH, NX, NC = 8, 2, 2, 4, 2
AXES = ("z", "yl", "yh", "x", "c")
SIZES = (NZ, NYL, NYH, NX, NC)
BLK, HALF = 512, 256
COLS = (((1,), (1,)), ((), ()))


def permute(array, target):
    pairs = []
    for flat_id in range(256):
        z, yl, yh, x, c = np.unravel_index(flat_id, SIZES)
        to = target(z, yh * 2 + yl, x, c)
        if to is not None:
            z, y, x, c = to[0] % NZ, to[1] % 4, to[2] % NX, to[3] % NC
            pairs.append((flat_id, int(np.ravel_multi_index((z, y % 2, y // 2, x, c), SIZES))))
    return lax.ppermute(array, AXES, pairs)


def swap_core(array):
    return permute(array, lambda z, y, x, c: (z, y, x, c + 1))


def first_axis(array, step):
    return permute(
        array, lambda z, y, x, c: (z, y, x + step, c) if c == 0 else (z, y + step, x, c)
    )


def second_axis(array, step):
    return permute(
        array, lambda z, y, x, c: (z, y + step, x, c) if c == 0 else (z, y, x + step, c)
    )


def gather_first(array, step):
    def target(z, y, x, c):
        if c == 0:
            return z, y, x + step, c
        return (z, y + 2, x, c) if step == 1 else None

    return permute(array, target)


def gather_second(array, step):
    def target(z, y, x, c):
        if c == 1:
            return z, y, x + step, c
        return (z, y + 2, x, c) if step < 3 else None

    return permute(array, target)


def along_z(array, step):
    return permute(array, lambda z, y, x, c: (z + step, y, x, c))


def vmem():
    return pl.BlockSpec(memory_space=pltpu.VMEM)


def smem():
    return pl.BlockSpec(memory_space=pltpu.SMEM)


def anywhere():
    return pl.BlockSpec(memory_space=pl.ANY)


def call(kernel, name, outs, grid_args, limit, flops, size, **kw):
    return pl.pallas_call(
        kernel,
        name=name,
        out_shape=outs,
        compiler_params=pltpu.CompilerParams(vmem_limit_bytes=limit * 2**20),
        cost_estimate=pl.CostEstimate(flops=flops, bytes_accessed=size, transcendentals=0),
        **grid_args,
        **kw,
    )


def arr(shape, dtype=BF):
    return jax.ShapeDtypeStruct(shape, dtype)


def flat(inputs, outputs, unused=0):
    return dict(
        in_specs=[smem()] + [vmem()] * inputs + [anywhere()] * unused,
        out_specs=[vmem()] * outputs,
    )


def rows_spec(cols):
    return pl.BlockSpec((32, cols), lambda r: (r, 0))


def weight_kernel(where, codes, scales, gain, out):
    half = where[4] % 2
    column = jnp.broadcast_to(gain[pl.ds(where[5], 1), :], (8, BLK)).T[:, :1]
    for group in range(2):
        rows = pl.ds(pl.multiple_of(half * HALF + group * 128, 128), 128)
        values = codes[rows, :].astype(F32) * scales[pl.ds(half * 2 + group, 1), :]
        part = jnp.where(
            half == 0, column[group * 128 : group * 128 + 128], column[HALF + group * 128 :][:128]
        )
        out[group * 128 : group * 128 + 128, :] = (values * part).astype(BF)


def prep_kernel(where, tokens, key_grad, after, send, scaled, inverse):
    c = where[3]
    squares = jnp.zeros((32, 128), F32)
    for block in range(16):
        values = tokens[:, block * BLK : (block + 1) * BLK].astype(F32)
        values = values * values
        for lane in range(4):
            squares += values[:, lane * 128 : (lane + 1) * 128]
    for block in range(8):
        col = pl.multiple_of((block * NC + 1 - c) * BLK, BLK)
        send[:, block * BLK : (block + 1) * BLK] = tokens[:, pl.ds(col, BLK)]
    inv = lax.rsqrt(jnp.sum(squares, axis=-1, keepdims=True) / 8192.0 + 1e-05)
    inverse[...] = jnp.broadcast_to(inv, (32, 128))
    kg = (key_grad[...].astype(F32) * inv).astype(BF)
    scaled[...] = kg
    send[:, 4096:] = kg


def partial_kernel(where, tok_own, tok_far, kg_own, *refs):
    outs, kgt = refs[:4], refs[4]
    x, c = where[0], where[3]
    y = where[2] * 2 + where[1]
    for side, kg in enumerate((kg_own[...], tok_far[:, 4096:])):
        turned = kg.T
        for row in range(16):
            to = (row % 2) * 256 + (row // 2) * 32
            kgt[to : to + 32, side * 256 : side * 256 + 256] = turned[row * 32 : row * 32 + 32, :]
    for step in range(4):
        to_x, to_y = (x + step) % NX, (y + step) % 4
        for rh in range(2):
            for ch in range(2):
                row = jnp.where(c == 0, rh, to_y % 2)
                block = jnp.where(c == 0, ch * NX + to_x, (to_y // 2) * NX + rh * 2 + ch)
                left = kgt[pl.ds(pl.multiple_of(row * 256, 256), 256), :]
                own_col = pl.multiple_of((block * NC + c) * BLK, BLK)
                far_col = pl.multiple_of(block * BLK, BLK)
                value = jnp.dot(
                    left[:, :256], tok_own[:, pl.ds(own_col, BLK)], preferred_element_type=F32
                ) + jnp.dot(
                    left[:, 256:], tok_far[:, pl.ds(far_col, BLK)], preferred_element_type=F32
                )
                outs[step][rh * 256 : rh * 256 + 256, ch * BLK : ch * BLK + BLK] = value.astype(BF)


def add(parts, rows, cols):
    out = parts[0][rows, cols].astype(F32)
    for part in parts[1:]:
        out = out + part[rows, cols].astype(F32)
    return out.astype(BF)


def cut_kernel(where, *refs):
    parts, outs = refs[:4], refs[4:]
    c = where[3]
    for step in range(4):
        to_x, to_y = (where[0] + step) % NX, (where[2] * 2 + where[1] + step) % 4
        row = jnp.where(c == 0, to_y % 2, to_x // 2)
        col = jnp.where(c == 0, to_y // 2, to_x % 2)
        outs[step][...] = add(
            parts, pl.ds(pl.multiple_of(row * 256, 256), 256), pl.ds(pl.multiple_of(col * BLK, BLK), BLK)
        )


def sum_kernel(where, *refs):
    refs[4][...] = add(refs[:4], slice(None), slice(None))


def end_kernel(where, gain, parts, out):
    total = jnp.sum(parts[...].astype(F32), axis=0)
    out[...] = (total * gain[pl.ds(where[5], 1), :]).T


def pick_kernel(where, pair, rest, first, out):
    @pl.when(where[3] == 0)
    def _():
        out[...] = rest[...]

    @pl.when(where[3] != 0)
    def _():
        out[...] = pair[...]


def order_kernel(where, pair, rest, got_1, got_2, got_3, up, down):
    up[:BLK, :] = pair[...]

    @pl.when(where[3] == 0)
    def _():
        up[BLK:, :] = rest[...]
        down[:BLK, :] = got_1[...]
        down[BLK:, :] = got_2[...]

    @pl.when(where[3] != 0)
    def _():
        up[BLK:, :] = got_1[...]
        down[:BLK, :] = got_2[...]
        down[BLK:, :] = got_3[...]


def project_kernel(where, tok_own, tok_far, kg_own, *refs):
    pieces, (key_own, key_far, grad_own, grad_far) = refs[:4], refs[-4:]
    x, yh, c, z = where[0], where[2], where[3], where[4]
    key_own[...] = jnp.zeros_like(key_own)
    key_far[...] = jnp.zeros_like(key_far)
    for index in range(16):
        entry = index % 8
        hop = jnp.where(c == 0, entry % 4, entry // 2)
        flip = jnp.where(c == 0, entry // 4, entry % 2)
        block = (yh + flip) % NYH * NX + (x + NX - hop) % NX
        offset = (z + index // 8) % 2 * HALF
        own_col = pl.multiple_of((block * NC + c) * BLK + offset, HALF)
        far_col = pl.multiple_of(block * BLK + offset, HALF)
        weight = pieces[index // 4][(entry % 4) * HALF : (entry % 4 + 1) * HALF, :]
        key_own[...] += jnp.dot(
            tok_own[:, pl.ds(own_col, HALF)], weight, preferred_element_type=F32
        )
        key_far[...] += jnp.dot(
            tok_far[:, pl.ds(far_col, HALF)], weight, preferred_element_type=F32
        )
        for kg, grad in ((kg_own[...], grad_own), (tok_far[:, 4096:], grad_far)):
            grad[:, pl.ds(far_col, HALF)] = lax.dot_general(
                kg, weight, COLS, preferred_element_type=F32
            ).astype(BF)


def finish_kernel(
    where, tokens, grad_a, grad_b, key_a, key_b, kg, inverse, after, key_out, token_grad
):
    c = where[3]
    inv = inverse[:, :1]
    key_sum = key_a[...] + key_b[...]
    key_out[...] = (key_sum * inv).astype(BF)
    dotted = jnp.sum(kg[...].astype(F32) * key_sum, axis=-1, keepdims=True) / 8192.0
    slope = inv * inv * inv * dotted
    for block in range(NYH * NX):
        for refs, parity in ((grad_a, c), (grad_b, 1 - c)):
            col = pl.multiple_of((block * NC + parity) * BLK, BLK)
            part = refs[:, block * BLK : (block + 1) * BLK].astype(F32)
            values = tokens[:, pl.ds(col, BLK)].astype(F32)
            token_grad[:, pl.ds(col, BLK)] = (part - values * slope).astype(BF)


def on_device(tokens, norm_gain, weight_codes, weight_scales, key_grad):
    x, yl, yh, c, z = [lax.axis_index(name) for name in ("x", "yl", "yh", "c", "z")]
    shard = (yh * NX + x) * NC + c
    where = jnp.stack([x, yl, yh, c, z, shard]).astype(jnp.int32)
    gains = norm_gain.reshape(16, BLK)

    weight = call(weight_kernel, "weight", arr((HALF, 512)), dict(in_specs=[smem()] + [vmem()] * 3, out_specs=vmem()), 8, 2**19, 2**20)(
        where, weight_codes, weight_scales, gains
    )
    near = [gather_first(weight, s) for s in (2, 1, 3)]
    pair = jnp.concatenate([weight, near[1]], axis=0)
    rest = jnp.concatenate([near[0], near[2]], axis=0)

    send, kg, inverse = call(
        prep_kernel,
        "prep",
        [arr((256, 4608)), arr((256, 512)), arr((256, 128), F32)],
        dict(
            grid=(8,),
            in_specs=[smem(), rows_spec(8192), rows_spec(512), anywhere()],
            out_specs=[rows_spec(4608), rows_spec(512), rows_spec(128)],
        ),
        8,
        2**22,
        7 * 2**20,
    )(where, tokens, key_grad, weight)
    tok_far = swap_core(send)

    second = call(pick_kernel, "pick", arr((512, 512)), dict(in_specs=[smem()] + [vmem()] * 2 + [anywhere()], out_specs=vmem()), 8, 2**18, 3 * 2**19)(
        where, pair, rest, weight
    )
    got = [gather_second(pair, 1), gather_second(second, 2), gather_second(pair, 3)]
    up, down = call(order_kernel, "order", [arr((1024, 512))] * 2, flat(5, 2), 12, 2**19, 9 * 2**19)(
        where, pair, rest, *got
    )
    pieces = [up, down, along_z(up, 1), along_z(down, -1)]

    outs = call(
        partial_kernel,
        "partial",
        [arr((512, 1024))] * 4,
        flat(3, 4),
        20,
        2**31,
        11 * 2**20,
        scratch_shapes=[pltpu.VMEM((512, 512), BF)],
    )(where, tokens, tok_far, kg)
    cuts = call(cut_kernel, "cut", [arr((256, 512))] * 4, flat(4, 4), 8, 2**20, 5 * 2**20)(
        where, outs[0], *[first_axis(outs[s], s) for s in (1, 2, 3)]
    )
    plane = call(sum_kernel, "sum", arr((256, 512)), dict(in_specs=[smem()] + [vmem()] * 4, out_specs=vmem()), 8, 2**19, 5 * 2**18)(
        where, cuts[0], *[second_axis(cuts[s], s) for s in (1, 2, 3)]
    )
    over_z = lax.all_to_all(
        plane.reshape(NZ, 32, BLK), "z", split_axis=0, concat_axis=0, tiled=True
    )
    weight_grad = call(
        end_kernel, "end", arr((BLK, 32), F32), dict(in_specs=[smem()] + [vmem()] * 2, out_specs=vmem()), 8, 2**17, 2**19
    )(where, gains, over_z)

    key_own, key_far, grad_own, grad_far = call(
        project_kernel,
        "project",
        [arr((256, 512), F32)] * 2 + [arr((256, 4096))] * 2,
        flat(7, 4, 1),
        24,
        2**32,
        16 * 2**20,
    )(where, tokens, tok_far, kg, *pieces, cuts[0])
    key_out, token_grad = call(
        finish_kernel,
        "finish",
        [arr((256, 512)), arr((256, 8192))],
        dict(
            grid=(8,),
            in_specs=[smem()]
            + [rows_spec(n) for n in (8192, 4096, 4096, 512, 512, 512, 128)]
            + [anywhere()],
            out_specs=[rows_spec(512), rows_spec(8192)],
        ),
        8,
        2**23,
        13 * 2**20,
    )(where, tokens, grad_own, swap_core(grad_far), key_own, swap_core(key_far), key_grad, inverse, plane)
    return key_out, token_grad, weight_grad


def solution(mesh):
    fine = Mesh(np.asarray(mesh.devices).reshape(SIZES), AXES)
    outer, inner = ("z", "yl"), ("yh", "x", "c")
    in_specs = (P(outer + inner, None), P(), P(inner, None), P(inner, None), P(outer + inner, None))
    out_specs = (P(outer + inner, None), P(outer + inner, None), P(inner, outer))
    return jax.shard_map(
        on_device, mesh=fine, in_specs=in_specs, out_specs=out_specs, check_vma=False
    )
```

time: 302 us -> 128 us (0.42); the launches traced: 297 us -> 126 us
  waiting for transfers between devices: 166 us -> 51.2 us
  other arithmetic: 35.4 us -> 0.03 us
  matrix products: 24.1 us -> 0 us
  Pallas kernels: 0 us -> 23.5 us
  between operations: 14.1 us -> 0.82 us
  local copies, waits for them, and re-layouts: 15.4 us -> 9.6 us
    all_to_all x4 -> x0, waiting for transfers between devices: 109 us -> none  [the longest x1 95.5 us: on_device(): lax.all_to_all(code_vals, 'inner', split_axis=0, concat_axis=0, tiled=True)]
    all_gather x1 -> x0, waiting for transfers between devices: 56 us -> none  [on_device(): lax.all_gather(coded, 'inner', axis=0, tiled=True)]
    ppermute x0 -> x17, waiting for transfers between devices: none -> 51.2 us  [permute(): return lax.ppermute(array, AXES, pairs)]
    convert_element_type x7 -> x0, other arithmetic: 28.6 us -> none  [the longest x2 10 us: quantize(): code_vals = (groups / group_scale[:, None, :]).astype(jnp.bfloat16)]
    ppermute x0 -> x17, starting transfers between devices: none -> 24.3 us  [permute(): return lax.ppermute(array, AXES, pairs)]
    dot_general x3 -> x0, matrix products: 24.1 us -> none  [the longest x1 9.95 us: on_device(): key_sum = jnp.dot(normed, weight, preferred_element_type=jnp.float32)]
    all_to_all x4 -> x0, starting transfers between devices: 23.9 us -> none  [the longest x1 7.37 us: on_device(): lax.all_to_all(second_scale.astype(jnp.bfloat16), 'outer', split_axis=2,...]
    pallas_call x0 -> x10, Pallas kernels: none -> 23.5 us  [the longest x1 7.25 us: on_device(): call(finish_kernel, 'finish', [arr((256, 512)), arr((256, 8192))], dict(g...]
  transfers between devices with their start and end apart: 5 -> 17, of which waited for: 4 -> 9; matrix products, arithmetic and copies ran while one was open for 14% -> 1% of each run, Pallas kernels for 0% -> 5%
where the time goes in v2:
time: 128 us; the launch traced here: 126 us
  waiting for transfers between devices  51.2 us (40%)
  starting transfers between devices  24.3 us (19%)
  Pallas kernels  23.5 us (18%)
  blocking collectives  17 us (13%)
  local copies, waits for them, and re-layouts  9.6 us (8%)
    ppermute x17, waiting for transfers between devices, permute(): return lax.ppermute(array, AXES, pairs)  51.2 us
    ppermute x17, starting transfers between devices, permute(): return lax.ppermute(array, AXES, pairs)  24.3 us
    all_to_all x1, blocking collectives, on_device(): lax.all_to_all(plane.reshape(NZ, 32, BLK), 'z', split_axis=0, concat_axis...  17 us
    unnamed x20, local copies, waits for them, and re-layouts  8.73 us
    pallas_call x1, Pallas kernels, on_device(): call(finish_kernel, 'finish', [arr((256, 512)), arr((256, 8192))], dict(g...  7.25 us
    pallas_call x1, Pallas kernels, on_device(): call(project_kernel, 'project', [arr((256, 512), F32)] * 2 + [arr((256, 4...  6.4 us
    pallas_call x1, Pallas kernels, on_device(): call(partial_kernel, 'partial', [arr((512, 1024))] * 4, flat(3, 4), 20, 2...  3 us
  transfers between devices with their start and end apart: 17, of which 9 were waited for; matrix products, arithmetic and copies ran while one was open for 1% of the time, Pallas kernels for 5%

profile of v2, /device:TPU:6, one launch (start us, length us, event | category | flops | bytes accessed | tf_op | source)
XLA Modules:
  0.0 126.4 jit_solution(3087936730019573360)
XLA Ops:
  0.6 0.8 reshape.12.gain
  1.4 0.1 stack.27.where
  1.5 1.0 copy-done.5
  2.5 0.7 copy-done.8
  3.2 0.8 weight.1.after.first
  4.0 0.0 copy-start
  4.0 2.2 %copy-done = bf16[256,8192]{1,0:T(8,128)(2,1)S(1)} copy-done((bf16[256,8192]{1,0:T(8,128)(2,1)S(1)}, bf16[256,8192]{1,0:T(8,128)(2,1)}, u32[]{:S(2)}) %copy-start) | copy-done | bytes 4194328
  6.2 0.9 copy-done.3
  7.1 2.4 %prep.1 = (bf16[256,4608]{1,0:T(8,128)(2,1)S(1)}, bf16[256,512]{1,0:T(8,128)(2,1)S(1)}, f32[256,128]{1,0:T(8,128)S(1)}) custom-call(s32[6]{0:T(128)S(1)} %stack.27.where, bf16[256,8192]{1,0:T(8,128)(2,1)S(1)} %copy-done, bf16[256,512]{1,0:T(8,128)(2,1)S(1)} %copy-done.3, bf16[256,512]{1,0:T(8,128)(2,1)S(1)} %weight.1.after.first), custom_call_target="tpu_custom_call" | custom-call | flops 4194304 | bytes 7340032 | tf_op jit(solution)/shard_map/prep/pallas_call | solution.py:271
  9.5 0.0 copy-start.6
  9.5 0.1 collective-permute-start
  9.6 3.3 %collective-permute-start.2 = (bf16[256,512]{1,0:T(8,128)(2,1)S(1)}, bf16[256,512]{1,0:T(8,128)(2,1)S(1)}, u32[]{:S(2)}, u32[]{:S(2)}) collective-permute-start(bf16[256,512]{1,0:T(8,128)(2,1)S(1)} %weight.1.after.first), channel_id=1, source_target_pairs={{0,4},{2,6},{4,0},{6,2},{8,12},{10,14},{12,8},{14,10},{16,20},{18,... | collective-permute-start | bytes 786440 | tf_op jit(solution)/shard_map/ppermute | solution.py:25
  12.9 2.2 %collective-permute-start.1 = (bf16[256,512]{1,0:T(8,128)(2,1)S(1)}, bf16[256,512]{1,0:T(8,128)(2,1)S(1)}, u32[]{:S(2)}, u32[]{:S(2)}) collective-permute-start(bf16[256,512]{1,0:T(8,128)(2,1)S(1)} %weight.1.after.first), channel_id=1, source_target_pairs={{0,2},{1,9},{2,4},{3,11},{4,6},{5,13},{6,0},{7,15},{8,10},{9,1},{1... | collective-permute-start | bytes 786440 | tf_op jit(solution)/shard_map/ppermute | solution.py:25
  15.1 1.9 %collective-permute-start.3 = (bf16[256,512]{1,0:T(8,128)(2,1)S(1)}, bf16[256,512]{1,0:T(8,128)(2,1)S(1)}, u32[]{:S(2)}, u32[]{:S(2)}) collective-permute-start(bf16[256,512]{1,0:T(8,128)(2,1)S(1)} %weight.1.after.first), channel_id=1, source_target_pairs={{0,6},{2,0},{4,2},{6,4},{8,14},{10,8},{12,10},{14,12},{16,22},{18,... | collective-permute-start | bytes 786440 | tf_op jit(solution)/shard_map/ppermute | solution.py:25
  17.0 2.4 %collective-permute-done.2 = bf16[256,512]{1,0:T(8,128)(2,1)S(1)} collective-permute-done((bf16[256,512]{1,0:T(8,128)(2,1)S(1)}, bf16[256,512]{1,0:T(8,128)(2,1)S(1)}, u32[]{:S(2)}, u32[]{:S(2)}) %collective-permute-start.2) | collective-permute-done | bytes 262176 | tf_op jit(solution)/shard_map/ppermute | solution.py:25
  19.4 2.4 %collective-permute-done.1 = bf16[256,512]{1,0:T(8,128)(2,1)S(1)} collective-permute-done((bf16[256,512]{1,0:T(8,128)(2,1)S(1)}, bf16[256,512]{1,0:T(8,128)(2,1)S(1)}, u32[]{:S(2)}, u32[]{:S(2)}) %collective-permute-start.1) | collective-permute-done | bytes 262176 | tf_op jit(solution)/shard_map/ppermute | solution.py:25
  21.8 9.4 %collective-permute-done.3 = bf16[256,512]{1,0:T(8,128)(2,1)S(1)} collective-permute-done((bf16[256,512]{1,0:T(8,128)(2,1)S(1)}, bf16[256,512]{1,0:T(8,128)(2,1)S(1)}, u32[]{:S(2)}, u32[]{:S(2)}) %collective-permute-start.3) | collective-permute-done | bytes 262176 | tf_op jit(solution)/shard_map/ppermute | solution.py:25
  31.2 0.6 pick.1
  31.8 3.3 %collective-permute-start.5 = (bf16[512,512]{1,0:T(8,128)(2,1)S(1)}, bf16[512,512]{1,0:T(8,128)(2,1)S(1)}, u32[]{:S(2)}, u32[]{:S(2)}) collective-permute-start(bf16[512,512]{1,0:T(8,128)(2,1)S(1)} %pick.1), channel_id=1, source_target_pairs={{0,8},{1,5},{2,10},{3,7},{4,12},{5,1},{6,14},{7,3},{8,0},{9,13},{1... | collective-permute-start | bytes 1572872 | tf_op jit(solution)/shard_map/ppermute | solution.py:25
  35.1 0.3 collective-permute-start.4
  35.5 0.7 collective-permute-start.6
  36.1 0.0 collective-permute-done.tok_far
  36.2 3.0 %partial.1 = (bf16[512,1024]{1,0:T(8,128)(2,1)S(1)}, bf16[512,1024]{1,0:T(8,128)(2,1)S(1)}, bf16[512,1024]{1,0:T(8,128)(2,1)S(1)}, bf16[512,1024]{1,0:T(8,128)(2,1)S(1)}) custom-call(s32[6]{0:T(128)S(1)} %stack.27.where, bf16[256,8192]{1,0:T(8,128)(2,1)S(1)} %copy-done.1, bf16[256,4608]{1,0:T(8,128)(2,1)S(1)} %collective-permute-done.tok_far, ...), custom_call_target="tpu_custom_call" | custom-call | flops 2147483648 | bytes 11534336 | tf_op jit(solution)/shard_map/partial/pallas_call | solution.py:295
  39.2 0.1 collective-permute-start.10
  39.3 0.4 collective-permute-start.11
  39.7 8.6 %collective-permute-done.5.got_2 = bf16[512,512]{1,0:T(8,128)(2,1)S(1)} collective-permute-done((bf16[512,512]{1,0:T(8,128)(2,1)S(1)}, bf16[512,512]{1,0:T(8,128)(2,1)S(1)}, u32[]{:S(2)}, u32[]{:S(2)}) %collective-permute-start.5) | collective-permute-done | bytes 524320 | tf_op jit(solution)/shard_map/ppermute | solution.py:25
  48.3 0.0 collective-permute-start.9
  48.3 11.2 %collective-permute-done.4.got_1 = bf16[512,512]{1,0:T(8,128)(2,1)S(1)} collective-permute-done((bf16[512,512]{1,0:T(8,128)(2,1)S(1)}, bf16[512,512]{1,0:T(8,128)(2,1)S(1)}, u32[]{:S(2)}, u32[]{:S(2)}) %collective-permute-start.4) | collective-permute-done | bytes 524320 | tf_op jit(solution)/shard_map/ppermute | solution.py:25
  59.5 0.7 order.1
  60.2 2.0 %collective-permute-start.7 = (bf16[1024,512]{1,0:T(8,128)(2,1)S(1)}, bf16[1024,512]{1,0:T(8,128)(2,1)S(1)}, u32[]{:S(2)}, u32[]{:S(2)}) collective-permute-start(bf16[1024,512]{1,0:T(8,128)(2,1)S(1)} %get-tuple-element.24.refs_0_), channel_id=1, source_target_pairs={{0,32},{1,33},{2,34},{3,35},{4,36},{5,37},{6,38},{7,39},{8,40},{9,... | collective-permute-start | bytes 3145736 | tf_op jit(solution)/shard_map/ppermute | solution.py:25
  62.2 4.2 %collective-permute-start.8 = (bf16[1024,512]{1,0:T(8,128)(2,1)S(1)}, bf16[1024,512]{1,0:T(8,128)(2,1)S(1)}, u32[]{:S(2)}, u32[]{:S(2)}) collective-permute-start(bf16[1024,512]{1,0:T(8,128)(2,1)S(1)} %get-tuple-element.25.refs_1_), channel_id=1, source_target_pairs={{0,224},{1,225},{2,226},{3,227},{4,228},{5,229},{6,230},{7,231},{8... | collective-permute-start | bytes 3145736 | tf_op jit(solution)/shard_map/ppermute | solution.py:25
  66.4 0.2 collective-permute-done.11.refs_3_
  66.6 1.1 cut.1
  67.7 11.2 %collective-permute-done.7.refs_2_ = bf16[1024,512]{1,0:T(8,128)(2,1)S(1)} collective-permute-done((bf16[1024,512]{1,0:T(8,128)(2,1)S(1)}, bf16[1024,512]{1,0:T(8,128)(2,1)S(1)}, u32[]{:S(2)}, u32[]{:S(2)}) %collective-permute-start.7) | collective-permute-done | bytes 1048608 | tf_op jit(solution)/shard_map/ppermute | solution.py:25
  78.9 6.4 %project.1 = (f32[256,512]{1,0:T(8,128)S(1)}, f32[256,512]{1,0:T(8,128)}, bf16[256,4096]{1,0:T(8,128)(2,1)S(1)}, bf16[256,4096]{1,0:T(8,128)(2,1)}) custom-call(s32[6]{0:T(128)S(1)} %stack.27.where, bf16[256,8192]{1,0:T(8,128)(2,1)S(1)} %copy-done.1, bf16[256,4608]{1,0:T(8,128)(2,1)S(1)} %collective-permute-done.tok_far, ...), custom_call_target="tpu_custom_call" | custom-call | flops 4294967296 | bytes 16777216 | tf_op jit(solution)/shard_map/project/pallas_call | solution.py:318
  85.3 1.6 %collective-permute-start.14 = (bf16[256,512]{1,0:T(8,128)(2,1)S(1)}, bf16[256,512]{1,0:T(8,128)(2,1)S(1)}, u32[]{:S(2)}, u32[]{:S(2)}) collective-permute-start(bf16[256,512]{1,0:T(8,128)(2,1)S(1)} %get-tuple-element.36), channel_id=1, source_target_pairs={{0,16},{1,3},{2,18},{3,5},{4,20},{5,7},{6,22},{7,1},{8,24},{9,11},... | collective-permute-start | bytes 786440 | tf_op jit(solution)/shard_map/ppermute | solution.py:25
  86.9 2.9 %collective-permute-start.15 = (bf16[256,512]{1,0:T(8,128)(2,1)S(1)}, bf16[256,512]{1,0:T(8,128)(2,1)S(1)}, u32[]{:S(2)}, u32[]{:S(2)}) collective-permute-start(bf16[256,512]{1,0:T(8,128)(2,1)S(1)} %get-tuple-element.37), channel_id=1, source_target_pairs={{0,8},{1,5},{2,10},{3,7},{4,12},{5,1},{6,14},{7,3},{8,0},{9,13},{1... | collective-permute-start | bytes 786440 | tf_op jit(solution)/shard_map/ppermute | solution.py:25
  89.8 1.4 %collective-permute-start.16 = (bf16[256,512]{1,0:T(8,128)(2,1)S(1)}, bf16[256,512]{1,0:T(8,128)(2,1)S(1)}, u32[]{:S(2)}, u32[]{:S(2)}) collective-permute-start(bf16[256,512]{1,0:T(8,128)(2,1)S(1)} %get-tuple-element.38), channel_id=1, source_target_pairs={{0,24},{1,7},{2,26},{3,1},{4,28},{5,3},{6,30},{7,5},{8,16},{9,15},... | collective-permute-start | bytes 786440 | tf_op jit(solution)/shard_map/ppermute | solution.py:25
  91.2 1.8 %collective-permute-done.14.refs_1_ = bf16[256,512]{1,0:T(8,128)(2,1)S(1)} collective-permute-done((bf16[256,512]{1,0:T(8,128)(2,1)S(1)}, bf16[256,512]{1,0:T(8,128)(2,1)S(1)}, u32[]{:S(2)}, u32[]{:S(2)}) %collective-permute-start.14) | collective-permute-done | bytes 262176 | tf_op jit(solution)/shard_map/ppermute | solution.py:25
  92.9 4.0 %collective-permute-done.15.refs_2_ = bf16[256,512]{1,0:T(8,128)(2,1)S(1)} collective-permute-done((bf16[256,512]{1,0:T(8,128)(2,1)S(1)}, bf16[256,512]{1,0:T(8,128)(2,1)S(1)}, u32[]{:S(2)}, u32[]{:S(2)}) %collective-permute-start.15) | collective-permute-done | bytes 262176 | tf_op jit(solution)/shard_map/ppermute | solution.py:25
  97.0 0.7 sum.1.after
  97.6 17.0 %all_to_all.5.parts = bf16[8,32,512]{2,1,0:T(8,128)(2,1)S(1)} all-to-all(bf16[8,32,512]{2,1,0:T(8,128)(2,1)S(1)} %bitcast.7), channel_id=1, replica_groups=mesh['z'=8,'yl'=2,'yh'=2,'x'=4,'c'=2] {'z'}, dimensions={0} | all-to-all | bytes 524288 | tf_op jit(solution)/shard_map/all_to_all | solution.py:311
  114.6 0.7 end.1
  115.3 0.7 copy.8
  116.1 0.0 copy-start.2
  116.1 2.2 %copy-done.2 = bf16[256,8192]{1,0:T(8,128)(2,1)S(1)} copy-done((bf16[256,8192]{1,0:T(8,128)(2,1)S(1)}, bf16[256,8192]{1,0:T(8,128)(2,1)}, u32[]{:S(2)}) %copy-start.2) | copy-done | bytes 4194328
  118.2 0.9 copy-done.7
  119.1 7.2 %finish.1 = (bf16[256,512]{1,0:T(8,128)(2,1)}, bf16[256,8192]{1,0:T(8,128)(2,1)}) custom-call(s32[6]{0:T(128)S(1)} %stack.27.where, bf16[256,8192]{1,0:T(8,128)(2,1)S(1)} %copy-done.2, bf16[256,4096]{1,0:T(8,128)(2,1)S(1)} %get-tuple-element.31.grad_a, bf16[256,4096]{1,0:T(8,128)(2,1)} %collective-permute-done.12.grad_b, ...), custom_call_target="tpu_custom_call" | custom-call | flops 8388608 | bytes 13631488 | tf_op jit(solution)/shard_map/finish/pallas_call | solution.py:327
  (21 shorter events, 0.1 us)
Async XLA Ops:
  1.5 1.0 copy-start.5
  2.5 0.7 copy-start.8
  4.0 2.2 %copy-start = (bf16[256,8192]{1,0:T(8,128)(2,1)S(1)}, bf16[256,8192]{1,0:T(8,128)(2,1)}, u32[]{:S(2)}) copy-start(bf16[256,8192]{1,0:T(8,128)(2,1)} %tokens.3) | copy-start | bytes 12582916
  6.2 0.9 copy-start.3
  7.1 29.0 %copy-start.1 = (bf16[256,8192]{1,0:T(8,128)(2,1)S(1)}, bf16[256,8192]{1,0:T(8,128)(2,1)}, u32[]{:S(2)}) copy-start(bf16[256,8192]{1,0:T(8,128)(2,1)} %tokens.3) | copy-start | bytes 12582916
  9.5 26.6 %copy-start.6 = (f32[256,128]{1,0:T(8,128)}, f32[256,128]{1,0:T(8,128)S(1)}, u32[]{:S(2)}) copy-start(f32[256,128]{1,0:T(8,128)S(1)} %get-tuple-element.35.inverse) | copy-start | bytes 393220
  9.5 26.6 %collective-permute-start = (bf16[256,4608]{1,0:T(8,128)(2,1)S(1)}, bf16[256,4608]{1,0:T(8,128)(2,1)S(1)}, u32[]{:S(2)}, u32[]{:S(2)}) collective-permute-start(bf16[256,4608]{1,0:T(8,128)(2,1)S(1)} %get-tuple-element.22), channel_id=1, source_target_pairs={{0,1},{1,0},{2,3},{3,2},{4,5},{5,4},{6,7},{7,6},{8,9},{9,8},{10,11... | collective-permute-start | bytes 7077896 | tf_op jit(solution)/shard_map/ppermute | solution.py:25
  9.6 9.8 %collective-permute-start.2 = (bf16[256,512]{1,0:T(8,128)(2,1)S(1)}, bf16[256,512]{1,0:T(8,128)(2,1)S(1)}, u32[]{:S(2)}, u32[]{:S(2)}) collective-permute-start(bf16[256,512]{1,0:T(8,128)(2,1)S(1)} %weight.1.after.first), channel_id=1, source_target_pairs={{0,4},{2,6},{4,0},{6,2},{8,12},{10,14},{12,8},{14,10},{16,20},{18,... | collective-permute-start | bytes 786440 | tf_op jit(solution)/shard_map/ppermute | solution.py:25
  12.9 8.8 %collective-permute-start.1 = (bf16[256,512]{1,0:T(8,128)(2,1)S(1)}, bf16[256,512]{1,0:T(8,128)(2,1)S(1)}, u32[]{:S(2)}, u32[]{:S(2)}) collective-permute-start(bf16[256,512]{1,0:T(8,128)(2,1)S(1)} %weight.1.after.first), channel_id=1, source_target_pairs={{0,2},{1,9},{2,4},{3,11},{4,6},{5,13},{6,0},{7,15},{8,10},{9,1},{1... | collective-permute-start | bytes 786440 | tf_op jit(solution)/shard_map/ppermute | solution.py:25
  15.1 16.1 %collective-permute-start.3 = (bf16[256,512]{1,0:T(8,128)(2,1)S(1)}, bf16[256,512]{1,0:T(8,128)(2,1)S(1)}, u32[]{:S(2)}, u32[]{:S(2)}) collective-permute-start(bf16[256,512]{1,0:T(8,128)(2,1)S(1)} %weight.1.after.first), channel_id=1, source_target_pairs={{0,6},{2,0},{4,2},{6,4},{8,14},{10,8},{12,10},{14,12},{16,22},{18,... | collective-permute-start | bytes 786440 | tf_op jit(solution)/shard_map/ppermute | solution.py:25
  31.8 16.5 %collective-permute-start.5 = (bf16[512,512]{1,0:T(8,128)(2,1)S(1)}, bf16[512,512]{1,0:T(8,128)(2,1)S(1)}, u32[]{:S(2)}, u32[]{:S(2)}) collective-permute-start(bf16[512,512]{1,0:T(8,128)(2,1)S(1)} %pick.1), channel_id=1, source_target_pairs={{0,8},{1,5},{2,10},{3,7},{4,12},{5,1},{6,14},{7,3},{8,0},{9,13},{1... | collective-permute-start | bytes 1572872 | tf_op jit(solution)/shard_map/ppermute | solution.py:25
  35.1 24.4 %collective-permute-start.4 = (bf16[512,512]{1,0:T(8,128)(2,1)S(1)}, bf16[512,512]{1,0:T(8,128)(2,1)S(1)}, u32[]{:S(2)}, u32[]{:S(2)}) collective-permute-start(bf16[512,512]{1,0:T(8,128)(2,1)S(1)} %pad_maximum_fusion.pair), channel_id=1, source_target_pairs={{0,8},{1,3},{2,10},{3,5},{4,12},{5,7},{6,14},{7,1},{8,0},{9,11},{1... | collective-permute-start | bytes 1572872 | tf_op jit(solution)/shard_map/ppermute | solution.py:25
  35.5 24.1 %collective-permute-start.6 = (bf16[512,512]{1,0:T(8,128)(2,1)S(1)}, bf16[512,512]{1,0:T(8,128)(2,1)S(1)}, u32[]{:S(2)}, u32[]{:S(2)}) collective-permute-start(bf16[512,512]{1,0:T(8,128)(2,1)S(1)} %pad_maximum_fusion.pair), channel_id=1, source_target_pairs={{1,7},{3,1},{5,3},{7,5},{9,15},{11,9},{13,11},{15,13},{17,23},{19,... | collective-permute-start | bytes 1572872 | tf_op jit(solution)/shard_map/ppermute | solution.py:25
  39.2 27.2 %collective-permute-start.10 = (bf16[512,1024]{1,0:T(8,128)(2,1)S(1)}, bf16[512,1024]{1,0:T(8,128)(2,1)S(1)}, u32[]{:S(2)}, u32[]{:S(2)}) collective-permute-start(bf16[512,1024]{1,0:T(8,128)(2,1)S(1)} %get-tuple-element.28), channel_id=1, source_target_pairs={{0,4},{1,9},{2,6},{3,11},{4,0},{5,13},{6,2},{7,15},{8,12},{9,1},{1... | collective-permute-start | bytes 3145736 | tf_op jit(solution)/shard_map/ppermute | solution.py:25
  39.3 27.3 %collective-permute-start.11 = (bf16[512,1024]{1,0:T(8,128)(2,1)S(1)}, bf16[512,1024]{1,0:T(8,128)(2,1)S(1)}, u32[]{:S(2)}, u32[]{:S(2)}) collective-permute-start(bf16[512,1024]{1,0:T(8,128)(2,1)S(1)} %get-tuple-element.29), channel_id=1, source_target_pairs={{0,6},{1,25},{2,0},{3,27},{4,2},{5,29},{6,4},{7,31},{8,14},{9,17},... | collective-permute-start | bytes 3145736 | tf_op jit(solution)/shard_map/ppermute | solution.py:25
  48.3 18.3 %collective-permute-start.9 = (bf16[512,1024]{1,0:T(8,128)(2,1)S(1)}, bf16[512,1024]{1,0:T(8,128)(2,1)S(1)}, u32[]{:S(2)}, u32[]{:S(2)}) collective-permute-start(bf16[512,1024]{1,0:T(8,128)(2,1)S(1)} %get-tuple-element.27), channel_id=1, source_target_pairs={{0,2},{1,17},{2,4},{3,19},{4,6},{5,21},{6,0},{7,23},{8,10},{9,25},... | collective-permute-start | bytes 3145736 | tf_op jit(solution)/shard_map/ppermute | solution.py:25
  60.2 18.7 %collective-permute-start.7 = (bf16[1024,512]{1,0:T(8,128)(2,1)S(1)}, bf16[1024,512]{1,0:T(8,128)(2,1)S(1)}, u32[]{:S(2)}, u32[]{:S(2)}) collective-permute-start(bf16[1024,512]{1,0:T(8,128)(2,1)S(1)} %get-tuple-element.24.refs_0_), channel_id=1, source_target_pairs={{0,32},{1,33},{2,34},{3,35},{4,36},{5,37},{6,38},{7,39},{8,40},{9,... | collective-permute-start | bytes 3145736 | tf_op jit(solution)/shard_map/ppermute | solution.py:25
  62.2 16.7 %collective-permute-start.8 = (bf16[1024,512]{1,0:T(8,128)(2,1)S(1)}, bf16[1024,512]{1,0:T(8,128)(2,1)S(1)}, u32[]{:S(2)}, u32[]{:S(2)}) collective-permute-start(bf16[1024,512]{1,0:T(8,128)(2,1)S(1)} %get-tuple-element.25.refs_1_), channel_id=1, source_target_pairs={{0,224},{1,225},{2,226},{3,227},{4,228},{5,229},{6,230},{7,231},{8... | collective-permute-start | bytes 3145736 | tf_op jit(solution)/shard_map/ppermute | solution.py:25
  85.3 30.7 %copy-start.4 = (bf16[256,512]{1,0:T(8,128)(2,1)S(1)}, bf16[256,512]{1,0:T(8,128)(2,1)}, u32[]{:S(2)}) copy-start(bf16[256,512]{1,0:T(8,128)(2,1)} %kg.1) | copy-start | bytes 786436
  85.3 30.7 %collective-permute-start.12 = (bf16[256,4096]{1,0:T(8,128)(2,1)}, bf16[256,4096]{1,0:T(8,128)(2,1)}, u32[]{:S(2)}, u32[]{:S(2)}) collective-permute-start(bf16[256,4096]{1,0:T(8,128)(2,1)} %get-tuple-element.32), channel_id=1, source_target_pairs={{0,1},{1,0},{2,3},{3,2},{4,5},{5,4},{6,7},{7,6},{8,9},{9,8},{10,11... | collective-permute-start | bytes 6291464 | tf_op jit(solution)/shard_map/ppermute | solution.py:25
  85.3 7.6 %collective-permute-start.14 = (bf16[256,512]{1,0:T(8,128)(2,1)S(1)}, bf16[256,512]{1,0:T(8,128)(2,1)S(1)}, u32[]{:S(2)}, u32[]{:S(2)}) collective-permute-start(bf16[256,512]{1,0:T(8,128)(2,1)S(1)} %get-tuple-element.36), channel_id=1, source_target_pairs={{0,16},{1,3},{2,18},{3,5},{4,20},{5,7},{6,22},{7,1},{8,24},{9,11},... | collective-permute-start | bytes 786440 | tf_op jit(solution)/shard_map/ppermute | solution.py:25
  86.9 10.1 %collective-permute-start.15 = (bf16[256,512]{1,0:T(8,128)(2,1)S(1)}, bf16[256,512]{1,0:T(8,128)(2,1)S(1)}, u32[]{:S(2)}, u32[]{:S(2)}) collective-permute-start(bf16[256,512]{1,0:T(8,128)(2,1)S(1)} %get-tuple-element.37), channel_id=1, source_target_pairs={{0,8},{1,5},{2,10},{3,7},{4,12},{5,1},{6,14},{7,3},{8,0},{9,13},{1... | collective-permute-start | bytes 786440 | tf_op jit(solution)/shard_map/ppermute | solution.py:25
  89.8 7.2 %collective-permute-start.16 = (bf16[256,512]{1,0:T(8,128)(2,1)S(1)}, bf16[256,512]{1,0:T(8,128)(2,1)S(1)}, u32[]{:S(2)}, u32[]{:S(2)}) collective-permute-start(bf16[256,512]{1,0:T(8,128)(2,1)S(1)} %get-tuple-element.38), channel_id=1, source_target_pairs={{0,24},{1,7},{2,26},{3,1},{4,28},{5,3},{6,30},{7,5},{8,16},{9,15},... | collective-permute-start | bytes 786440 | tf_op jit(solution)/shard_map/ppermute | solution.py:25
  91.2 24.9 %collective-permute-start.13 = (f32[256,512]{1,0:T(8,128)}, f32[256,512]{1,0:T(8,128)}, u32[]{:S(2)}, u32[]{:S(2)}) collective-permute-start(f32[256,512]{1,0:T(8,128)} %get-tuple-element.34), channel_id=1, source_target_pairs={{0,1},{1,0},{2,3},{3,2},{4,5},{5,4},{6,7},{7,6},{8,9},{9,8},{10,11... | collective-permute-start | bytes 1572872 | tf_op jit(solution)/shard_map/ppermute | solution.py:25
  116.1 2.2 %copy-start.2 = (bf16[256,8192]{1,0:T(8,128)(2,1)S(1)}, bf16[256,8192]{1,0:T(8,128)(2,1)}, u32[]{:S(2)}) copy-start(bf16[256,8192]{1,0:T(8,128)(2,1)} %tokens.3) | copy-start | bytes 12582916
  118.2 0.9 copy-start.7

commit v3 on v2

v3 whole, which is shorter than its diff:
```python
import functools

import jax
import jax.numpy as jnp
import numpy as np
from jax import lax
from jax.experimental import pallas as pl
from jax.experimental.pallas import tpu as pltpu
from jax.sharding import Mesh, PartitionSpec as P

BF, F32 = jnp.bfloat16, jnp.float32
NZ, NYL, NYH, NX, NC = 8, 2, 2, 4, 2
AXES = ("z", "yl", "yh", "x", "c")
SIZES = (NZ, NYL, NYH, NX, NC)
BLK, HALF = 512, 256
COLS = (((1,), (1,)), ((), ()))


def permute(array, target):
    pairs = []
    for flat_id in range(256):
        z, yl, yh, x, c = np.unravel_index(flat_id, SIZES)
        to = target(z, yh * 2 + yl, x, c)
        if to is not None:
            z, y, x, c = to[0] % NZ, to[1] % 4, to[2] % NX, to[3] % NC
            pairs.append((flat_id, int(np.ravel_multi_index((z, y % 2, y // 2, x, c), SIZES))))
    return lax.ppermute(array, AXES, pairs)


def swap_core(array):
    return permute(array, lambda z, y, x, c: (z, y, x, c + 1))


def first_axis(array, step):
    return permute(
        array, lambda z, y, x, c: (z, y, x + step, c) if c == 0 else (z, y + step, x, c)
    )


def second_axis(array, step):
    return permute(
        array, lambda z, y, x, c: (z, y + step, x, c) if c == 0 else (z, y, x + step, c)
    )


def gather_first(array, step):
    def target(z, y, x, c):
        if c == 0:
            return z, y, x + step, c
        return z, y + (2 if step != 2 else 0), x + (2 if step != 1 else 0), c

    return permute(array, target)


def gather_second(array, step):
    def target(z, y, x, c):
        return (z, y + 2, x, c) if c == 0 else (z, y, x + step, c)

    return permute(array, target)


def along_z(array, step):
    return permute(array, lambda z, y, x, c: (z + step, y, x, c))


MARK = jax.ShapeDtypeStruct((8, 128), F32)


def vmem():
    return pl.BlockSpec(memory_space=pltpu.VMEM)


def smem():
    return pl.BlockSpec(memory_space=pltpu.SMEM)


def anywhere():
    return pl.BlockSpec(memory_space=pl.ANY)


def call(kernel, name, outs, grid_args, limit, flops, size, **kw):
    return pl.pallas_call(
        kernel,
        name=name,
        out_shape=outs,
        compiler_params=pltpu.CompilerParams(vmem_limit_bytes=limit * 2**20),
        cost_estimate=pl.CostEstimate(flops=flops, bytes_accessed=size, transcendentals=0),
        **grid_args,
        **kw,
    )


def arr(shape, dtype=BF):
    return jax.ShapeDtypeStruct(shape, dtype)


def flat(inputs, outputs, unused=0):
    return dict(
        in_specs=[smem()] + [vmem()] * inputs + [anywhere()] * unused,
        out_specs=[vmem()] * outputs,
    )


def rows_spec(cols):
    return pl.BlockSpec((64, cols), lambda r: (r, 0))


def weight_kernel(where, codes, scales, gain, out):
    half = where[4] % 2
    column = jnp.broadcast_to(gain[...], (8, HALF)).T[:, :1]
    for group in range(2):
        rows = slice(group * 128, group * 128 + 128)
        values = codes[rows, :].astype(F32) * scales[pl.ds(half * 2 + group, 1), :]
        out[rows, :] = (values * column[rows]).astype(BF)


def prep_kernel(where, tokens, key_grad, after, send, keep, scaled, inverse):
    c = where[3]
    squares = jnp.zeros((64, 128), F32)
    for block in range(16):
        values = tokens[:, block * BLK : (block + 1) * BLK].astype(F32)
        values = values * values
        for lane in range(4):
            squares += values[:, lane * 128 : (lane + 1) * 128]
    for block in range(8):
        col = pl.multiple_of((block * NC + 1 - c) * BLK, BLK)
        send[:, block * BLK : (block + 1) * BLK] = tokens[:, pl.ds(col, BLK)]
        col = pl.multiple_of((block * NC + c) * BLK, BLK)
        keep[:, block * BLK : (block + 1) * BLK] = tokens[:, pl.ds(col, BLK)]
    inv = lax.rsqrt(jnp.sum(squares, axis=-1, keepdims=True) / 8192.0 + 1e-05)
    inverse[...] = jnp.broadcast_to(inv, (64, 128))
    kg = (key_grad[...].astype(F32) * inv).astype(BF)
    scaled[...] = kg
    send[:, 4096:] = kg


def partial_kernel(where, tok_own, tok_far, kg_own, *refs):
    outs, mark, kgt = refs[:4], refs[4], refs[5]
    mark[...] = jnp.zeros_like(mark)
    x, c = where[0], where[3]
    y = where[2] * 2 + where[1]
    for side, kg in enumerate((kg_own[...], tok_far[:, 4096:])):
        turned = kg.T
        for row in range(16):
            to = (row % 2) * 256 + (row // 2) * 32
            kgt[to : to + 32, side * 256 : side * 256 + 256] = turned[row * 32 : row * 32 + 32, :]
    for step in range(4):
        to_x, to_y = (x + step) % NX, (y + step) % 4
        for rh in range(2):
            for ch in range(2):
                row = jnp.where(c == 0, rh, to_y % 2)
                block = jnp.where(c == 0, ch * NX + to_x, (to_y // 2) * NX + rh * 2 + ch)
                left = kgt[pl.ds(pl.multiple_of(row * 256, 256), 256), :]
                cols = pl.ds(pl.multiple_of(block * BLK, BLK), BLK)
                value = jnp.dot(
                    left[:, :256], tok_own[:, cols], preferred_element_type=F32
                ) + jnp.dot(left[:, 256:], tok_far[:, cols], preferred_element_type=F32)
                outs[step][rh * 256 : rh * 256 + 256, ch * BLK : ch * BLK + BLK] = value.astype(BF)


def add(parts, rows, cols):
    out = parts[0][rows, cols].astype(F32)
    for part in parts[1:]:
        out = out + part[rows, cols].astype(F32)
    return out.astype(BF)


def cut_kernel(where, *refs):
    parts, outs = refs[:4], refs[4:]
    c = where[3]
    for step in range(4):
        to_x, to_y = (where[0] + step) % NX, (where[2] * 2 + where[1] + step) % 4
        row = jnp.where(c == 0, to_y % 2, to_x // 2)
        col = jnp.where(c == 0, to_y // 2, to_x % 2)
        outs[step][...] = add(
            parts, pl.ds(pl.multiple_of(row * 256, 256), 256), pl.ds(pl.multiple_of(col * BLK, BLK), BLK)
        )


def sum_kernel(where, *refs):
    refs[4][...] = add(refs[:4], slice(None), slice(None))


def end_kernel(where, gain, parts, after, out):
    out[...] = jnp.sum(parts[...].astype(F32), axis=0) * gain[...]


def pick_kernel(where, weight, near_1, near_2, near_3, after, pair, rest, second):
    pair[:HALF, :] = weight[...]
    pair[HALF:, :] = near_1[...]
    rest[:HALF, :] = near_2[...]
    rest[HALF:, :] = near_3[...]

    @pl.when(where[3] == 0)
    def _():
        second[...] = rest[...]

    @pl.when(where[3] != 0)
    def _():
        second[...] = pair[...]


def order_kernel(where, pair, rest, got_1, got_2, up, down):
    up[:BLK, :] = pair[...]
    down[BLK:, :] = got_2[...]

    @pl.when(where[3] == 0)
    def _():
        up[BLK:, :] = rest[...]
        down[:BLK, :] = got_1[...]

    @pl.when(where[3] != 0)
    def _():
        up[BLK:, :] = got_1[...]
        down[:BLK, :] = rest[...]


def project_kernel(other, where, tok_own, tok_far, kg_own, up, down, *refs):
    key_own, key_far, grad_own, grad_far = refs[-4:]
    x, yh, c, z = where[0], where[2], where[3], where[4]
    if other:
        key_own[...] = refs[0][...]
        key_far[...] = refs[1][...]
    else:
        key_own[...] = jnp.zeros_like(key_own)
        key_far[...] = jnp.zeros_like(key_far)
    for entry in range(8):
        hop = jnp.where(c == 0, entry % 4, entry // 2)
        flip = jnp.where(c == 0, entry // 4, entry % 2)
        block = (yh + flip) % NYH * NX + (x + NX - hop) % NX
        cols = pl.ds(pl.multiple_of(block * BLK + (z + other) % 2 * HALF, HALF), HALF)
        to = pl.ds(pl.multiple_of(block * HALF, HALF), HALF)
        weight = (up, down)[entry // 4][(entry % 4) * HALF : (entry % 4 + 1) * HALF, :]
        key_own[...] += jnp.dot(tok_own[:, cols], weight, preferred_element_type=F32)
        key_far[...] += jnp.dot(tok_far[:, cols], weight, preferred_element_type=F32)
        for kg, grad in ((kg_own[...], grad_own), (tok_far[:, 4096:], grad_far)):
            grad[:, to] = lax.dot_general(kg, weight, COLS, preferred_element_type=F32).astype(BF)


def finish_kernel(where, tokens, *refs):
    grads, (key_a, key_b, kg, inverse, key_out, token_grad, mark) = refs[:4], refs[4:]
    mark[...] = jnp.zeros_like(mark)
    c, z = where[3], where[4]
    inv = inverse[:, :1]
    key_sum = key_a[...] + key_b[...]
    key_out[...] = (key_sum * inv).astype(BF)
    dotted = jnp.sum(kg[...].astype(F32) * key_sum, axis=-1, keepdims=True) / 8192.0
    slope = inv * inv * inv * dotted
    for block in range(NYH * NX):
        for index, grad in enumerate(grads):
            parity, half = (c + index // 2) % 2, (z + index) % 2
            cols = pl.ds(pl.multiple_of((block * NC + parity) * BLK + half * HALF, HALF), HALF)
            part = grad[:, block * HALF : (block + 1) * HALF].astype(F32)
            token_grad[:, cols] = (part - tokens[:, cols].astype(F32) * slope).astype(BF)


def on_device(tokens, norm_gain, weight_codes, weight_scales, key_grad):
    x, yl, yh, c, z = [lax.axis_index(name) for name in ("x", "yl", "yh", "c", "z")]
    shard = (yh * NX + x) * NC + c
    where = jnp.stack([x, yl, yh, c, z, shard]).astype(jnp.int32)
    tokens, key_grad, weight_codes, weight_scales, gains = [
        pltpu.with_memory_space_constraint(array, pltpu.HBM)
        for array in (tokens, key_grad, weight_codes, weight_scales, norm_gain.reshape(1, 8192))
    ]

    weight = call(
        weight_kernel,
        "weight",
        arr((HALF, 512)),
        dict(
            grid_spec=pltpu.PrefetchScalarGridSpec(
                num_scalar_prefetch=1,
                grid=(1,),
                in_specs=[
                    pl.BlockSpec((HALF, 512), lambda i, w: (w[4] % 2, 0)),
                    pl.BlockSpec((4, 512), lambda i, w: (0, 0)),
                    pl.BlockSpec((1, HALF), lambda i, w: (0, w[5] * 2 + w[4] % 2)),
                ],
                out_specs=pl.BlockSpec((HALF, 512), lambda i, w: (0, 0)),
            )
        ),
        8,
        2**19,
        2**20,
    )(where, weight_codes, weight_scales, gains)
    near = [gather_first(weight, s) for s in (1, 2, 3)]

    send, keep, kg, inverse = call(
        prep_kernel,
        "prep",
        [arr((256, 4608)), arr((256, 4096)), arr((256, 512)), arr((256, 128), F32)],
        dict(
            grid=(4,),
            in_specs=[smem(), rows_spec(8192), rows_spec(512), anywhere()],
            out_specs=[rows_spec(4608), rows_spec(4096), rows_spec(512), rows_spec(128)],
        ),
        14,
        2**22,
        9 * 2**20,
    )(where, tokens, key_grad, weight)
    tok_far = swap_core(send)

    *outs, partial_mark = call(
        partial_kernel,
        "partial",
        [arr((512, 1024))] * 4 + [MARK],
        flat(3, 5),
        16,
        2**31,
        9 * 2**20,
        scratch_shapes=[pltpu.VMEM((512, 512), BF)],
    )(where, keep, tok_far, kg)
    outs_here = [first_axis(outs[s], s) for s in (1, 2, 3)]

    pair, rest, second = call(
        pick_kernel, "pick", [arr((512, 512))] * 3, flat(4, 3, 1), 8, 2**18, 3 * 2**20
    )(where, weight, *near, partial_mark)
    got = [gather_second(pair, 1), gather_second(second, 3)]
    up, down = call(
        order_kernel, "order", [arr((1024, 512))] * 2, flat(4, 2), 12, 2**19, 9 * 2**19
    )(where, pair, rest, *got)

    cuts = call(cut_kernel, "cut", [arr((256, 512))] * 4, flat(4, 4), 10, 2**20, 5 * 2**20)(
        where, outs[0], *outs_here
    )
    crossed = [second_axis(cuts[s], s) for s in (1, 2, 3)]

    def project(other, *operands, unused=0):
        return call(
            functools.partial(project_kernel, other),
            "project",
            [arr((256, 512), F32)] * 2 + [arr((256, 2048))] * 2,
            flat(len(operands) - unused, 4, unused),
            16,
            2**31,
            10 * 2**20,
        )(where, *operands)

    key_1, key_far_1, grad_1, grad_far_1 = project(0, keep, tok_far, kg, up, down)
    key_2, key_far_2, grad_2, grad_far_2 = project(
        1, keep, tok_far, kg, along_z(up, 1), along_z(down, -1), key_1, key_far_1, *crossed, unused=3
    )
    plane = call(
        sum_kernel,
        "sum",
        arr((256, 512)),
        dict(in_specs=[smem()] + [vmem()] * 4, out_specs=vmem()),
        8,
        2**19,
        5 * 2**18,
    )(where, cuts[0], *crossed)
    over_z = lax.all_to_all(
        plane.reshape(NZ, 32, BLK), "z", split_axis=0, concat_axis=0, tiled=True
    )
    key_out, token_grad, finish_mark = call(
        finish_kernel,
        "finish",
        [arr((256, 512)), arr((256, 8192)), MARK],
        dict(
            grid=(4,),
            in_specs=[smem(), rows_spec(8192)]
            + [rows_spec(2048)] * 4
            + [rows_spec(n) for n in (512, 512, 512, 128)],
            out_specs=[rows_spec(512), rows_spec(8192), pl.BlockSpec((8, 128), lambda r: (0, 0))],
        ),
        14,
        2**23,
        13 * 2**20,
    )(
        where,
        tokens,
        grad_1,
        grad_2,
        swap_core(grad_far_1),
        swap_core(grad_far_2),
        key_2,
        swap_core(key_far_2),
        key_grad,
        inverse,
    )
    weight_grad = call(
        end_kernel,
        "end",
        arr((32, BLK), F32),
        dict(
            grid_spec=pltpu.PrefetchScalarGridSpec(
                num_scalar_prefetch=1,
                grid=(1,),
                in_specs=[
                    pl.BlockSpec((1, BLK), lambda i, w: (0, w[5])),
                    pl.BlockSpec((NZ, 32, BLK), lambda i, w: (0, 0, 0)),
                    anywhere(),
                ],
                out_specs=pl.BlockSpec((32, BLK), lambda i, w: (0, 0)),
            )
        ),
        8,
        2**17,
        2**19,
    )(where, gains, over_z, finish_mark).T
    return key_out, token_grad, weight_grad


def solution(mesh):
    fine = Mesh(np.asarray(mesh.devices).reshape(SIZES), AXES)
    outer, inner = ("z", "yl"), ("yh", "x", "c")
    in_specs = (P(outer + inner, None), P(), P(inner, None), P(inner, None), P(outer + inner, None))
    out_specs = (P(outer + inner, None), P(outer + inner, None), P(inner, outer))
    return jax.shard_map(
        on_device, mesh=fine, in_specs=in_specs, out_specs=out_specs, check_vma=False
    )
```

time: 128 us -> 103 us (0.80)
  blocking collectives: 17 us -> 0 us
  waiting for transfers between devices: 51.2 us -> 40.4 us
  local copies, waits for them, and re-layouts: 9.6 us -> 1.12 us
  starting transfers between devices: 24.3 us -> 31.6 us
  Pallas kernels: 23.5 us -> 27.8 us
    all_to_all x1 -> x0, blocking collectives: 17 us -> none  [on_device(): lax.all_to_all(plane.reshape(NZ, 32, BLK), 'z', split_axis=0, concat_axis...]
    ppermute x17, waiting for transfers between devices: 51.2 us -> 34.9 us  [permute(): return lax.ppermute(array, AXES, pairs)]
    unnamed x20 -> x4, local copies, waits for them, and re-layouts: 8.73 us -> 1.04 us
    all_to_all x0 -> x1, starting transfers between devices: none -> 6.41 us  [on_device(): lax.all_to_all(plane.reshape(NZ, 32, BLK), 'z', split_axis=0, concat_axis...]
    all_to_all x0 -> x1, waiting for transfers between devices: none -> 5.48 us  [on_device(): lax.all_to_all(plane.reshape(NZ, 32, BLK), 'z', split_axis=0, concat_axis...]
    pallas_call x9 -> x10, Pallas kernels: 22.8 us -> 26.4 us  [the longest x2 7.82 us: project(): call(functools.partial(project_kernel, other), 'project', [arr((256, 512)...]
  transfers between devices with their start and end apart: 17 -> 18, of which waited for: 9 -> 9; matrix products, arithmetic and copies ran while one was open for 1% -> 0% of each run, Pallas kernels for 5% -> 20%
where the time goes in v3:
time: 103 us; the launch traced here: 102 us
  waiting for transfers between devices  40.4 us (39%)
  starting transfers between devices  31.6 us (31%)
  Pallas kernels  27.8 us (27%)
  local copies, waits for them, and re-layouts  1.12 us (1%)
    ppermute x17, waiting for transfers between devices, permute(): return lax.ppermute(array, AXES, pairs)  34.9 us
    ppermute x17, starting transfers between devices, permute(): return lax.ppermute(array, AXES, pairs)  25.2 us
    pallas_call x2, Pallas kernels, project(): call(functools.partial(project_kernel, other), 'project', [arr((256, 512)...  7.82 us
    all_to_all x1, starting transfers between devices, on_device(): lax.all_to_all(plane.reshape(NZ, 32, BLK), 'z', split_axis=0, concat_axis...  6.41 us
    pallas_call x1, Pallas kernels, on_device(): call(finish_kernel, 'finish', [arr((256, 512)), arr((256, 8192)), MARK],...  6 us
    all_to_all x1, waiting for transfers between devices, on_device(): lax.all_to_all(plane.reshape(NZ, 32, BLK), 'z', split_axis=0, concat_axis...  5.48 us
    pallas_call x1, Pallas kernels, on_device(): call(prep_kernel, 'prep', [arr((256, 4608)), arr((256, 4096)), arr((256,...  3.55 us
    pallas_call x1, Pallas kernels, on_device(): call(partial_kernel, 'partial', [arr((512, 1024))] * 4 + [MARK], flat(3,...  3 us
  transfers between devices with their start and end apart: 18, of which 9 were waited for; matrix products, arithmetic and copies ran while one was open for 0% of the time, Pallas kernels for 20%

profile of v3, /device:TPU:6, one launch (start us, length us, event | category | flops | bytes accessed | tf_op | source)
XLA Modules:
  0.0 101.6 jit_solution(8028793323975850947)
XLA Ops:
  0.6 0.1 stack.27.where
  0.7 1.8 %weight.1.after = bf16[256,512]{1,0:T(8,128)(2,1)S(1)} custom-call(s32[6]{0:T(128)S(1)} %stack.27.where, bf16[512,512]{1,0:T(8,128)(2,1)} %codes.1, f32[4,512]{1,0:T(4,128)} %scales.1, f32[1,8192]{1,0:T(1,128)} %bitcast.9), custom_call_target="tpu_custom_call" | custom-call | flops 524288 | bytes 1048576 | tf_op jit(solution)/shard_map/weight/pallas_call | solution.py:266
  2.5 3.6 %prep.1 = (bf16[256,4608]{1,0:T(8,128)(2,1)S(1)}, bf16[256,4096]{1,0:T(8,128)(2,1)S(1)}, bf16[256,512]{1,0:T(8,128)(2,1)S(1)}, f32[256,128]{1,0:T(8,128)S(1)}) custom-call(s32[6]{0:T(128)S(1)} %stack.27.where, bf16[256,8192]{1,0:T(8,128)(2,1)} %tokens.3, bf16[256,512]{1,0:T(8,128)(2,1)} %refs_6_.1, bf16[256,512]{1,0:T(8,128)(2,1)S(1)} %weight.1.after), custom_call_target="tpu_custom_call" | custom-call | flops 4194304 | bytes 9437184 | tf_op jit(solution)/shard_map/prep/pallas_call | solution.py:288
  6.1 0.1 collective-permute-start
  6.2 2.3 %collective-permute-start.1 = (bf16[256,512]{1,0:T(8,128)(2,1)S(1)}, bf16[256,512]{1,0:T(8,128)(2,1)S(1)}, u32[]{:S(2)}, u32[]{:S(2)}) collective-permute-start(bf16[256,512]{1,0:T(8,128)(2,1)S(1)} %weight.1.after), channel_id=1, source_target_pairs={{0,2},{1,9},{2,4},{3,11},{4,6},{5,13},{6,0},{7,15},{8,10},{9,1},{1... | collective-permute-start | bytes 786440 | tf_op jit(solution)/shard_map/ppermute | solution.py:27
  8.4 0.7 collective-permute-start.2
  9.1 0.3 collective-permute-start.3
  9.4 1.3 %collective-permute-done.tok_far = bf16[256,4608]{1,0:T(8,128)(2,1)S(1)} collective-permute-done((bf16[256,4608]{1,0:T(8,128)(2,1)S(1)}, bf16[256,4608]{1,0:T(8,128)(2,1)S(1)}, u32[]{:S(2)}, u32[]{:S(2)}) %collective-permute-start) | collective-permute-done | bytes 2359328 | tf_op jit(solution)/shard_map/ppermute | solution.py:27
  10.7 3.0 %partial.1 = (bf16[512,1024]{1,0:T(8,128)(2,1)S(1)}, bf16[512,1024]{1,0:T(8,128)(2,1)S(1)}, bf16[512,1024]{1,0:T(8,128)(2,1)S(1)}, bf16[512,1024]{1,0:T(8,128)(2,1)S(1)}, f32[8,128]{1,0:T(8,128)S(1)}) custom-call(s32[6]{0:T(128)S(1)} %stack.27.where, bf16[256,4096]{1,0:T(8,128)(2,1)S(1)} %get-tuple-element.32.tok_own, ...), custom_call_target="tpu_custom_call" | custom-call | flops 2147483648 | bytes 9437184 | tf_op jit(solution)/shard_map/partial/pallas_call | solution.py:303
  13.7 7.1 %collective-permute-done.1.near_1 = bf16[256,512]{1,0:T(8,128)(2,1)S(1)} collective-permute-done((bf16[256,512]{1,0:T(8,128)(2,1)S(1)}, bf16[256,512]{1,0:T(8,128)(2,1)S(1)}, u32[]{:S(2)}, u32[]{:S(2)}) %collective-permute-start.1) | collective-permute-done | bytes 262176 | tf_op jit(solution)/shard_map/ppermute | solution.py:27
  20.8 0.0 collective-permute-done.2.near_2
  20.8 3.8 %collective-permute-done.3.near_3 = bf16[256,512]{1,0:T(8,128)(2,1)S(1)} collective-permute-done((bf16[256,512]{1,0:T(8,128)(2,1)S(1)}, bf16[256,512]{1,0:T(8,128)(2,1)S(1)}, u32[]{:S(2)}, u32[]{:S(2)}) %collective-permute-start.3) | collective-permute-done | bytes 262176 | tf_op jit(solution)/shard_map/ppermute | solution.py:27
  24.5 0.6 pick.1
  25.2 0.8 collective-permute-start.4
  26.0 2.8 %collective-permute-start.5 = (bf16[512,512]{1,0:T(8,128)(2,1)S(1)}, bf16[512,512]{1,0:T(8,128)(2,1)S(1)}, u32[]{:S(2)}, u32[]{:S(2)}) collective-permute-start(bf16[512,512]{1,0:T(8,128)(2,1)S(1)} %get-tuple-element.38), channel_id=1, source_target_pairs={{0,8},{1,7},{2,10},{3,1},{4,12},{5,3},{6,14},{7,5},{8,0},{9,15},{1... | collective-permute-start | bytes 1572872 | tf_op jit(solution)/shard_map/ppermute | solution.py:27
  28.8 0.0 collective-permute-start.10
  28.8 3.2 %collective-permute-start.8 = (bf16[512,1024]{1,0:T(8,128)(2,1)S(1)}, bf16[512,1024]{1,0:T(8,128)(2,1)S(1)}, u32[]{:S(2)}, u32[]{:S(2)}) collective-permute-start(bf16[512,1024]{1,0:T(8,128)(2,1)S(1)} %get-tuple-element.45), channel_id=1, source_target_pairs={{0,2},{1,17},{2,4},{3,19},{4,6},{5,21},{6,0},{7,23},{8,10},{9,25},... | collective-permute-start | bytes 3145736 | tf_op jit(solution)/shard_map/ppermute | solution.py:27
  32.1 0.0 collective-permute-start.9
  32.1 7.7 %collective-permute-done.4.got_1 = bf16[512,512]{1,0:T(8,128)(2,1)S(1)} collective-permute-done((bf16[512,512]{1,0:T(8,128)(2,1)S(1)}, bf16[512,512]{1,0:T(8,128)(2,1)S(1)}, u32[]{:S(2)}, u32[]{:S(2)}) %collective-permute-start.4) | collective-permute-done | bytes 524320 | tf_op jit(solution)/shard_map/ppermute | solution.py:27
  39.8 11.2 %collective-permute-done.5.got_2 = bf16[512,512]{1,0:T(8,128)(2,1)S(1)} collective-permute-done((bf16[512,512]{1,0:T(8,128)(2,1)S(1)}, bf16[512,512]{1,0:T(8,128)(2,1)S(1)}, u32[]{:S(2)}, u32[]{:S(2)}) %collective-permute-start.5) | collective-permute-done | bytes 524320 | tf_op jit(solution)/shard_map/ppermute | solution.py:27
  51.0 0.7 order.1
  51.7 0.1 collective-permute-start.6
  51.8 3.2 %collective-permute-start.7 = (bf16[1024,512]{1,0:T(8,128)(2,1)S(1)}, bf16[1024,512]{1,0:T(8,128)(2,1)S(1)}, u32[]{:S(2)}, u32[]{:S(2)}) collective-permute-start(bf16[1024,512]{1,0:T(8,128)(2,1)S(1)} %get-tuple-element.40.down), channel_id=1, source_target_pairs={{0,224},{1,225},{2,226},{3,227},{4,228},{5,229},{6,230},{7,231},{8... | collective-permute-start | bytes 3145736 | tf_op jit(solution)/shard_map/ppermute | solution.py:27
  55.0 3.5 %collective-permute-done.10.refs_3_ = bf16[512,1024]{1,0:T(8,128)(2,1)S(1)} collective-permute-done((bf16[512,1024]{1,0:T(8,128)(2,1)S(1)}, bf16[512,1024]{1,0:T(8,128)(2,1)S(1)}, u32[]{:S(2)}, u32[]{:S(2)}) %collective-permute-start.10) | collective-permute-done | bytes 1048608 | tf_op jit(solution)/shard_map/ppermute | solution.py:27
  58.5 0.0 collective-permute-done.8.refs_1_
  58.5 0.0 collective-permute-done.9.refs_2_
  58.5 1.1 %cut.1 = (bf16[256,512]{1,0:T(8,128)(2,1)S(1)}, bf16[256,512]{1,0:T(8,128)(2,1)S(1)}, bf16[256,512]{1,0:T(8,128)(2,1)S(1)}, bf16[256,512]{1,0:T(8,128)(2,1)S(1)}) custom-call(s32[6]{0:T(128)S(1)} %stack.27.where, bf16[512,1024]{1,0:T(8,128)(2,1)S(1)} %get-tuple-element.44.refs_0_, bf16[512,1024]{1,0:T(8,128)(2,1)S(1)} %collective-permute-done.8.refs_1_, ...), custom_call_target="tpu_custom_call" | custom-call | flops 1048576 | bytes 5242880 | tf_op jit(solution)/shard_map/cut/pallas_call | solution.py:323
  59.6 0.3 collective-permute-start.11
  59.9 3.7 %collective-permute-start.12 = (bf16[256,512]{1,0:T(8,128)(2,1)S(1)}, bf16[256,512]{1,0:T(8,128)(2,1)S(1)}, u32[]{:S(2)}, u32[]{:S(2)}) collective-permute-start(bf16[256,512]{1,0:T(8,128)(2,1)S(1)} %get-tuple-element.49), channel_id=1, source_target_pairs={{0,8},{1,5},{2,10},{3,7},{4,12},{5,1},{6,14},{7,3},{8,0},{9,13},{1... | collective-permute-start | bytes 786440 | tf_op jit(solution)/shard_map/ppermute | solution.py:27
  63.6 0.5 collective-permute-start.13
  64.1 3.9 %project.2 = (f32[256,512]{1,0:T(8,128)S(1)}, f32[256,512]{1,0:T(8,128)S(1)}, bf16[256,2048]{1,0:T(8,128)(2,1)S(1)}, bf16[256,2048]{1,0:T(8,128)(2,1)}) custom-call(s32[6]{0:T(128)S(1)} %stack.27.where, bf16[256,4096]{1,0:T(8,128)(2,1)S(1)} %get-tuple-element.32.tok_own, bf16[256,4608]{1,0:T(8,128)(2,1)S(1)} %collective-permute-done.tok_far, ...), custom_call_target="tpu_custom_call" | custom-call | flops 2147483648 | bytes 10485760 | tf_op jit(solution)/shard_map/project/pallas_call | solution.py:329
  67.9 0.0 collective-permute-done.11.refs_2_.refs_1_
  67.9 2.7 %collective-permute-start.14 = (bf16[256,2048]{1,0:T(8,128)(2,1)}, bf16[256,2048]{1,0:T(8,128)(2,1)S(1)}, u32[]{:S(2)}, u32[]{:S(2)}) collective-permute-start(bf16[256,2048]{1,0:T(8,128)(2,1)} %get-tuple-element.52), channel_id=1, source_target_pairs={{0,1},{1,0},{2,3},{3,2},{4,5},{5,4},{6,7},{7,6},{8,9},{9,8},{10,11... | collective-permute-start | bytes 3145736 | tf_op jit(solution)/shard_map/ppermute | solution.py:27
  70.6 0.1 collective-permute-done.12.refs_3_.refs_2_
  70.7 0.2 collective-permute-done.13.refs_4_.refs_3_
  71.0 0.0 collective-permute-done.6.up
  71.0 0.0 collective-permute-done.7.down
  71.0 4.0 %project.3 = (f32[256,512]{1,0:T(8,128)S(1)}, f32[256,512]{1,0:T(8,128)}, bf16[256,2048]{1,0:T(8,128)(2,1)S(1)}, bf16[256,2048]{1,0:T(8,128)(2,1)}) custom-call(s32[6]{0:T(128)S(1)} %stack.27.where, bf16[256,4096]{1,0:T(8,128)(2,1)S(1)} %get-tuple-element.32.tok_own, bf16[256,4608]{1,0:T(8,128)(2,1)S(1)} %collective-permute-done.tok_far, ...), custom_call_target="tpu_custom_call" | custom-call | flops 2147483648 | bytes 10485760 | tf_op jit(solution)/shard_map/project/pallas_call | solution.py:329
  74.9 4.5 %collective-permute-start.15 = (bf16[256,2048]{1,0:T(8,128)(2,1)}, bf16[256,2048]{1,0:T(8,128)(2,1)}, u32[]{:S(2)}, u32[]{:S(2)}) collective-permute-start(bf16[256,2048]{1,0:T(8,128)(2,1)} %get-tuple-element.53), channel_id=1, source_target_pairs={{0,1},{1,0},{2,3},{3,2},{4,5},{5,4},{6,7},{7,6},{8,9},{9,8},{10,11... | collective-permute-start | bytes 3145736 | tf_op jit(solution)/shard_map/ppermute | solution.py:27
  79.4 0.0 collective-permute-start.16
  79.4 1.4 %sum.1 = bf16[256,512]{1,0:T(8,128)(2,1)} custom-call(s32[6]{0:T(128)S(1)} %stack.27.where, bf16[256,512]{1,0:T(8,128)(2,1)S(1)} %get-tuple-element.59.refs_0_, bf16[256,512]{1,0:T(8,128)(2,1)S(1)} %collective-permute-done.11.refs_2_.refs_1_, bf16[256,512]{1,0:T(8,128)(2,1)S(1)} %collective-permute-done.12.refs_3_.refs_2_, ...), custom_call_target="tpu_custom_call" | custom-call | flops 524288 | bytes 1310720 | tf_op jit(solution)/shard_map/sum/pallas_call | solution.py:343
  80.8 6.4 %all-to-all-start = ((bf16[8,32,512]{2,1,0:T(8,128)(2,1)}), bf16[8,32,512]{2,1,0:T(8,128)(2,1)S(1)}, u32[]{:S(2)}, u32[]{:S(2)}) async-start(bf16[8,32,512]{2,1,0:T(8,128)(2,1)} %bitcast.7), calls=%async_computation | async-start | bytes 524288 | tf_op jit(solution)/shard_map/all_to_all | solution.py:352
  87.2 0.0 collective-permute-done.14.refs_2_
  87.2 0.0 collective-permute-done.15.refs_3_
  87.2 1.0 %copy-done.1 = f32[256,512]{1,0:T(8,128)S(1)} copy-done((f32[256,512]{1,0:T(8,128)S(1)}, f32[256,512]{1,0:T(8,128)}, u32[]{:S(2)}) %copy-start.1) | copy-done | bytes 524312
  88.3 6.0 %finish.1 = (bf16[256,512]{1,0:T(8,128)(2,1)}, bf16[256,8192]{1,0:T(8,128)(2,1)}, f32[8,128]{1,0:T(8,128)S(1)}) custom-call(s32[6]{0:T(128)S(1)} %stack.27.where, bf16[256,8192]{1,0:T(8,128)(2,1)} %tokens.3, bf16[256,2048]{1,0:T(8,128)(2,1)S(1)} %get-tuple-element.41.refs_0_, bf16[256,2048]{1,0:T(8,128)(2,1)S(1)} %get-tuple-element.51.refs_1_, ...), custom_call_target="tpu_custom_call" | custom-call | flops 8388608 | bytes 13631488 | tf_op jit(solution)/shard_map/finish/pallas_call | solution.py:355
  94.3 5.5 %all-to-all-done.parts = bf16[8,32,512]{2,1,0:T(8,128)(2,1)S(1)} async-done(((bf16[8,32,512]{2,1,0:T(8,128)(2,1)}), bf16[8,32,512]{2,1,0:T(8,128)(2,1)S(1)}, u32[]{:S(2)}, u32[]{:S(2)}) %all-to-all-start) | async-done | bytes 262176 | tf_op jit(solution)/shard_map/all_to_all | solution.py:352
  99.7 1.9 %end.1 = f32[32,512]{1,0:T(8,128)} custom-call(s32[6]{0:T(128)S(1)} %stack.27.where, f32[1,8192]{1,0:T(1,128)} %bitcast.10, bf16[8,32,512]{2,1,0:T(8,128)(2,1)S(1)} %all-to-all-done.parts, f32[8,128]{1,0:T(8,128)S(1)} %get-tuple-element.60.after), custom_call_target="tpu_custom_call" | custom-call | flops 131072 | bytes 524288 | tf_op jit(solution)/shard_map/end/pallas_call | solution.py:381
  (4 shorter events, 0.0 us)
Async XLA Ops:
  6.1 4.6 %collective-permute-start = (bf16[256,4608]{1,0:T(8,128)(2,1)S(1)}, bf16[256,4608]{1,0:T(8,128)(2,1)S(1)}, u32[]{:S(2)}, u32[]{:S(2)}) collective-permute-start(bf16[256,4608]{1,0:T(8,128)(2,1)S(1)} %get-tuple-element.33), channel_id=1, source_target_pairs={{0,1},{1,0},{2,3},{3,2},{4,5},{5,4},{6,7},{7,6},{8,9},{9,8},{10,11... | collective-permute-start | bytes 7077896 | tf_op jit(solution)/shard_map/ppermute | solution.py:27
  6.2 14.6 %collective-permute-start.1 = (bf16[256,512]{1,0:T(8,128)(2,1)S(1)}, bf16[256,512]{1,0:T(8,128)(2,1)S(1)}, u32[]{:S(2)}, u32[]{:S(2)}) collective-permute-start(bf16[256,512]{1,0:T(8,128)(2,1)S(1)} %weight.1.after), channel_id=1, source_target_pairs={{0,2},{1,9},{2,4},{3,11},{4,6},{5,13},{6,0},{7,15},{8,10},{9,1},{1... | collective-permute-start | bytes 786440 | tf_op jit(solution)/shard_map/ppermute | solution.py:27
  8.4 12.4 %collective-permute-start.2 = (bf16[256,512]{1,0:T(8,128)(2,1)S(1)}, bf16[256,512]{1,0:T(8,128)(2,1)S(1)}, u32[]{:S(2)}, u32[]{:S(2)}) collective-permute-start(bf16[256,512]{1,0:T(8,128)(2,1)S(1)} %weight.1.after), channel_id=1, source_target_pairs={{0,4},{1,5},{2,6},{3,7},{4,0},{5,1},{6,2},{7,3},{8,12},{9,13},{10,... | collective-permute-start | bytes 786440 | tf_op jit(solution)/shard_map/ppermute | solution.py:27
  9.1 15.4 %collective-permute-start.3 = (bf16[256,512]{1,0:T(8,128)(2,1)S(1)}, bf16[256,512]{1,0:T(8,128)(2,1)S(1)}, u32[]{:S(2)}, u32[]{:S(2)}) collective-permute-start(bf16[256,512]{1,0:T(8,128)(2,1)S(1)} %weight.1.after), channel_id=1, source_target_pairs={{0,6},{1,13},{2,0},{3,15},{4,2},{5,9},{6,4},{7,11},{8,14},{9,5},{1... | collective-permute-start | bytes 786440 | tf_op jit(solution)/shard_map/ppermute | solution.py:27
  25.2 14.6 %collective-permute-start.4 = (bf16[512,512]{1,0:T(8,128)(2,1)S(1)}, bf16[512,512]{1,0:T(8,128)(2,1)S(1)}, u32[]{:S(2)}, u32[]{:S(2)}) collective-permute-start(bf16[512,512]{1,0:T(8,128)(2,1)S(1)} %get-tuple-element.36.pair), channel_id=1, source_target_pairs={{0,8},{1,3},{2,10},{3,5},{4,12},{5,7},{6,14},{7,1},{8,0},{9,11},{1... | collective-permute-start | bytes 1572872 | tf_op jit(solution)/shard_map/ppermute | solution.py:27
  26.0 25.1 %collective-permute-start.5 = (bf16[512,512]{1,0:T(8,128)(2,1)S(1)}, bf16[512,512]{1,0:T(8,128)(2,1)S(1)}, u32[]{:S(2)}, u32[]{:S(2)}) collective-permute-start(bf16[512,512]{1,0:T(8,128)(2,1)S(1)} %get-tuple-element.38), channel_id=1, source_target_pairs={{0,8},{1,7},{2,10},{3,1},{4,12},{5,3},{6,14},{7,5},{8,0},{9,15},{1... | collective-permute-start | bytes 1572872 | tf_op jit(solution)/shard_map/ppermute | solution.py:27
  28.8 29.7 %collective-permute-start.10 = (bf16[512,1024]{1,0:T(8,128)(2,1)S(1)}, bf16[512,1024]{1,0:T(8,128)(2,1)S(1)}, u32[]{:S(2)}, u32[]{:S(2)}) collective-permute-start(bf16[512,1024]{1,0:T(8,128)(2,1)S(1)} %get-tuple-element.47), channel_id=1, source_target_pairs={{0,6},{1,25},{2,0},{3,27},{4,2},{5,29},{6,4},{7,31},{8,14},{9,17},... | collective-permute-start | bytes 3145736 | tf_op jit(solution)/shard_map/ppermute | solution.py:27
  28.8 29.7 %collective-permute-start.8 = (bf16[512,1024]{1,0:T(8,128)(2,1)S(1)}, bf16[512,1024]{1,0:T(8,128)(2,1)S(1)}, u32[]{:S(2)}, u32[]{:S(2)}) collective-permute-start(bf16[512,1024]{1,0:T(8,128)(2,1)S(1)} %get-tuple-element.45), channel_id=1, source_target_pairs={{0,2},{1,17},{2,4},{3,19},{4,6},{5,21},{6,0},{7,23},{8,10},{9,25},... | collective-permute-start | bytes 3145736 | tf_op jit(solution)/shard_map/ppermute | solution.py:27
  32.1 26.5 %collective-permute-start.9 = (bf16[512,1024]{1,0:T(8,128)(2,1)S(1)}, bf16[512,1024]{1,0:T(8,128)(2,1)S(1)}, u32[]{:S(2)}, u32[]{:S(2)}) collective-permute-start(bf16[512,1024]{1,0:T(8,128)(2,1)S(1)} %get-tuple-element.46), channel_id=1, source_target_pairs={{0,4},{1,9},{2,6},{3,11},{4,0},{5,13},{6,2},{7,15},{8,12},{9,1},{1... | collective-permute-start | bytes 3145736 | tf_op jit(solution)/shard_map/ppermute | solution.py:27
  51.7 19.2 %collective-permute-start.6 = (bf16[1024,512]{1,0:T(8,128)(2,1)S(1)}, bf16[1024,512]{1,0:T(8,128)(2,1)S(1)}, u32[]{:S(2)}, u32[]{:S(2)}) collective-permute-start(bf16[1024,512]{1,0:T(8,128)(2,1)S(1)} %get-tuple-element.39.up), channel_id=1, source_target_pairs={{0,32},{1,33},{2,34},{3,35},{4,36},{5,37},{6,38},{7,39},{8,40},{9,... | collective-permute-start | bytes 3145736 | tf_op jit(solution)/shard_map/ppermute | solution.py:27
  51.8 19.2 %collective-permute-start.7 = (bf16[1024,512]{1,0:T(8,128)(2,1)S(1)}, bf16[1024,512]{1,0:T(8,128)(2,1)S(1)}, u32[]{:S(2)}, u32[]{:S(2)}) collective-permute-start(bf16[1024,512]{1,0:T(8,128)(2,1)S(1)} %get-tuple-element.40.down), channel_id=1, source_target_pairs={{0,224},{1,225},{2,226},{3,227},{4,228},{5,229},{6,230},{7,231},{8... | collective-permute-start | bytes 3145736 | tf_op jit(solution)/shard_map/ppermute | solution.py:27
  59.6 8.4 %collective-permute-start.11 = (bf16[256,512]{1,0:T(8,128)(2,1)S(1)}, bf16[256,512]{1,0:T(8,128)(2,1)S(1)}, u32[]{:S(2)}, u32[]{:S(2)}) collective-permute-start(bf16[256,512]{1,0:T(8,128)(2,1)S(1)} %get-tuple-element.48), channel_id=1, source_target_pairs={{0,16},{1,3},{2,18},{3,5},{4,20},{5,7},{6,22},{7,1},{8,24},{9,11},... | collective-permute-start | bytes 786440 | tf_op jit(solution)/shard_map/ppermute | solution.py:27
  59.9 10.8 %collective-permute-start.12 = (bf16[256,512]{1,0:T(8,128)(2,1)S(1)}, bf16[256,512]{1,0:T(8,128)(2,1)S(1)}, u32[]{:S(2)}, u32[]{:S(2)}) collective-permute-start(bf16[256,512]{1,0:T(8,128)(2,1)S(1)} %get-tuple-element.49), channel_id=1, source_target_pairs={{0,8},{1,5},{2,10},{3,7},{4,12},{5,1},{6,14},{7,3},{8,0},{9,13},{1... | collective-permute-start | bytes 786440 | tf_op jit(solution)/shard_map/ppermute | solution.py:27
  63.6 7.4 %collective-permute-start.13 = (bf16[256,512]{1,0:T(8,128)(2,1)S(1)}, bf16[256,512]{1,0:T(8,128)(2,1)S(1)}, u32[]{:S(2)}, u32[]{:S(2)}) collective-permute-start(bf16[256,512]{1,0:T(8,128)(2,1)S(1)} %get-tuple-element.50), channel_id=1, source_target_pairs={{0,24},{1,7},{2,26},{3,1},{4,28},{5,3},{6,30},{7,5},{8,16},{9,15},... | collective-permute-start | bytes 786440 | tf_op jit(solution)/shard_map/ppermute | solution.py:27
  67.9 19.2 %collective-permute-start.14 = (bf16[256,2048]{1,0:T(8,128)(2,1)}, bf16[256,2048]{1,0:T(8,128)(2,1)S(1)}, u32[]{:S(2)}, u32[]{:S(2)}) collective-permute-start(bf16[256,2048]{1,0:T(8,128)(2,1)} %get-tuple-element.52), channel_id=1, source_target_pairs={{0,1},{1,0},{2,3},{3,2},{4,5},{5,4},{6,7},{7,6},{8,9},{9,8},{10,11... | collective-permute-start | bytes 3145736 | tf_op jit(solution)/shard_map/ppermute | solution.py:27
  74.9 5.9 %copy-start = (f32[256,512]{1,0:T(8,128)}, f32[256,512]{1,0:T(8,128)S(1)}, u32[]{:S(2)}) copy-start(f32[256,512]{1,0:T(8,128)S(1)} %get-tuple-element.54.refs_4_) | copy-start | bytes 1572868
  74.9 12.3 %collective-permute-start.15 = (bf16[256,2048]{1,0:T(8,128)(2,1)}, bf16[256,2048]{1,0:T(8,128)(2,1)}, u32[]{:S(2)}, u32[]{:S(2)}) collective-permute-start(bf16[256,2048]{1,0:T(8,128)(2,1)} %get-tuple-element.53), channel_id=1, source_target_pairs={{0,1},{1,0},{2,3},{3,2},{4,5},{5,4},{6,7},{7,6},{8,9},{9,8},{10,11... | collective-permute-start | bytes 3145736 | tf_op jit(solution)/shard_map/ppermute | solution.py:27
  79.4 7.8 %collective-permute-start.16 = (f32[256,512]{1,0:T(8,128)}, f32[256,512]{1,0:T(8,128)}, u32[]{:S(2)}, u32[]{:S(2)}) collective-permute-start(f32[256,512]{1,0:T(8,128)} %get-tuple-element.55), channel_id=1, source_target_pairs={{0,1},{1,0},{2,3},{3,2},{4,5},{5,4},{6,7},{7,6},{8,9},{9,8},{10,11... | collective-permute-start | bytes 1572872 | tf_op jit(solution)/shard_map/ppermute | solution.py:27
  80.8 19.0 %all-to-all-start = ((bf16[8,32,512]{2,1,0:T(8,128)(2,1)}), bf16[8,32,512]{2,1,0:T(8,128)(2,1)S(1)}, u32[]{:S(2)}, u32[]{:S(2)}) async-start(bf16[8,32,512]{2,1,0:T(8,128)(2,1)} %bitcast.7), calls=%async_computation | async-start | bytes 524288 | tf_op jit(solution)/shard_map/all_to_all | solution.py:352
  87.2 1.0 %copy-start.1 = (f32[256,512]{1,0:T(8,128)S(1)}, f32[256,512]{1,0:T(8,128)}, u32[]{:S(2)}) copy-start(f32[256,512]{1,0:T(8,128)} %copy-done) | copy-start | bytes 1572868

commit v4 on v3

v4 whole, which is shorter than its diff:
```python
import functools

import jax
import jax.numpy as jnp
import numpy as np
from jax import lax
from jax.experimental import pallas as pl
from jax.experimental.pallas import tpu as pltpu
from jax.sharding import Mesh, PartitionSpec as P

BF, F32 = jnp.bfloat16, jnp.float32
NZ, NYL, NYH, NX, NC = 8, 2, 2, 4, 2
AXES = ("z", "yl", "yh", "x", "c")
SIZES = (NZ, NYL, NYH, NX, NC)
BLK, HALF = 512, 256
COLS = (((1,), (1,)), ((), ()))


def permute(array, target):
    pairs = []
    for flat_id in range(256):
        z, yl, yh, x, c = np.unravel_index(flat_id, SIZES)
        to = target(z, yh * 2 + yl, x, c)
        if to is not None:
            z, y, x, c = to[0] % NZ, to[1] % 4, to[2] % NX, to[3] % NC
            pairs.append((flat_id, int(np.ravel_multi_index((z, y % 2, y // 2, x, c), SIZES))))
    return lax.ppermute(array, AXES, pairs)


def swap_core(array):
    return permute(array, lambda z, y, x, c: (z, y, x, c + 1))


def first_axis(array, step):
    return permute(
        array, lambda z, y, x, c: (z, y, x + step, c) if c == 0 else (z, y + step, x, c)
    )


def second_axis(array, step):
    return permute(
        array, lambda z, y, x, c: (z, y + step, x, c) if c == 0 else (z, y, x + step, c)
    )


ORIGIN = (
    ((0, 0), (1, 0), (2, 0), (3, 0), (0, 1), (1, 1), (2, 1), (3, 1)),
    ((0, 0), (0, 1), (1, 0), (3, 1), (1, 1), (2, 0), (3, 0), (2, 1)),
)


def block_of(where, core, entry):
    hops = [ORIGIN[core_id][entry] for core_id in range(2)]
    hop = jnp.where(core == 0, hops[0][0], hops[1][0])
    flip = jnp.where(core == 0, hops[0][1], hops[1][1])
    return (where[2] + flip) % NYH * NX + (where[0] + NX - hop) % NX


def gather_first(array, step):
    def target(z, y, x, c):
        if c == 0:
            return z, y, x + step, c
        return ((z, y + 2, x, c), (z, y, x + 1, c), (z, y + 2, x - 1, c))[step - 1]

    return permute(array, target)


def gather_second(array, step):
    def target(z, y, x, c):
        return (z, y + 2, x, c) if c == 0 else (z, y, x + step, c)

    return permute(array, target)


def along_z(array, step):
    return permute(array, lambda z, y, x, c: (z + step, y, x, c))


COSTLY = ("sum", "finish")
MARK = jax.ShapeDtypeStruct((8, 128), F32)


def vmem():
    return pl.BlockSpec(memory_space=pltpu.VMEM)


def smem():
    return pl.BlockSpec(memory_space=pltpu.SMEM)


def anywhere():
    return pl.BlockSpec(memory_space=pl.ANY)


def call(kernel, name, outs, grid_args, limit, flops, size, **kw):
    return pl.pallas_call(
        kernel,
        name=name,
        out_shape=outs,
        compiler_params=pltpu.CompilerParams(vmem_limit_bytes=limit * 2**20),
        cost_estimate=pl.CostEstimate(
            flops=flops if name in COSTLY else 1, bytes_accessed=size if name in COSTLY else 1, transcendentals=0
        ),
        **grid_args,
        **kw,
    )


def arr(shape, dtype=BF):
    return jax.ShapeDtypeStruct(shape, dtype)


def flat(inputs, outputs, unused=0):
    return dict(
        in_specs=[smem()] + [vmem()] * inputs + [anywhere()] * unused,
        out_specs=[vmem()] * outputs,
    )


def rows_spec(cols):
    return pl.BlockSpec((64, cols), lambda r: (r, 0))


def prep_kernel(
    where, tokens, key_grad, codes, scales, gain, send, keep, scaled, inverse, weight, other, row
):
    @pl.when(pl.program_id(0) == 0)
    def _():
        row[...] = jnp.broadcast_to(gain[...], (8, BLK))
        column = jnp.broadcast_to(gain[...], (8, BLK)).T[:, :1]
        for group in range(4):
            rows = slice(group * 128, group * 128 + 128)
            to = slice((group % 2) * 128, (group % 2) * 128 + 128)
            part = codes[rows, :].astype(F32) * scales[group : group + 1, :]
            part = (part * column[rows]).astype(BF)

            @pl.when(where[4] % 2 == group // 2)
            def _():
                weight[to, :] = part

            @pl.when(where[4] % 2 != group // 2)
            def _():
                other[to, :] = part

    c = where[3]
    squares = jnp.zeros((64, 128), F32)
    for block in range(16):
        values = tokens[:, block * BLK : (block + 1) * BLK].astype(F32)
        values = values * values
        for lane in range(4):
            squares += values[:, lane * 128 : (lane + 1) * 128]
    for block in range(8):
        col = pl.multiple_of((block * NC + 1 - c) * BLK, BLK)
        send[:, block * BLK : (block + 1) * BLK] = tokens[:, pl.ds(col, BLK)]
        col = pl.multiple_of((block * NC + c) * BLK, BLK)
        keep[:, block * BLK : (block + 1) * BLK] = tokens[:, pl.ds(col, BLK)]
    inv = lax.rsqrt(jnp.sum(squares, axis=-1, keepdims=True) / 8192.0 + 1e-05)
    inverse[...] = jnp.broadcast_to(inv, (64, 128))
    kg = (key_grad[...].astype(F32) * inv).astype(BF)
    scaled[...] = kg
    send[:, 4096:] = kg


def partial_kernel(steps, where, tok_own, tok_far, kg_own, *refs):
    *outs, mark, kgt = refs
    mark[...] = jnp.zeros_like(mark)
    x, c = where[0], where[3]
    y = where[2] * 2 + where[1]
    for side, kg in enumerate((kg_own[...], tok_far[:, 4096:])):
        turned = kg.T
        for row in range(16):
            to = (row % 2) * 256 + (row // 2) * 32
            kgt[to : to + 32, side * 256 : side * 256 + 256] = turned[row * 32 : row * 32 + 32, :]
    for step, out in zip(steps, outs):
        to_x, to_y = (x + step) % NX, (y + step) % 4
        for rh in range(2):
            for ch in range(2):
                row = jnp.where(c == 0, rh, to_y % 2)
                block = jnp.where(c == 0, ch * NX + to_x, (to_y // 2) * NX + rh * 2 + ch)
                left = kgt[pl.ds(pl.multiple_of(row * 256, 256), 256), :]
                cols = pl.ds(pl.multiple_of(block * BLK, BLK), BLK)
                value = jnp.dot(
                    left[:, :256], tok_own[:, cols], preferred_element_type=F32
                ) + jnp.dot(left[:, 256:], tok_far[:, cols], preferred_element_type=F32)
                out[rh * 256 : rh * 256 + 256, ch * BLK : ch * BLK + BLK] = value.astype(BF)


def add(parts, rows, cols):
    out = parts[0][rows, cols].astype(F32)
    for part in parts[1:]:
        out = out + part[rows, cols].astype(F32)
    return out.astype(BF)


def cut_kernel(where, *refs):
    parts, outs, mark = refs[:4], refs[-5:-1], refs[-1]
    mark[...] = jnp.zeros_like(mark)
    c = where[3]
    for step in range(4):
        to_x, to_y = (where[0] + step) % NX, (where[2] * 2 + where[1] + step) % 4
        row = jnp.where(c == 0, to_y % 2, to_x // 2)
        col = jnp.where(c == 0, to_y // 2, to_x % 2)
        outs[step][...] = add(
            parts, pl.ds(pl.multiple_of(row * 256, 256), 256), pl.ds(pl.multiple_of(col * BLK, BLK), BLK)
        )


def sum_kernel(where, *refs):
    refs[5][...] = add(refs[:4], slice(None), slice(None))


def end_kernel(where, gain, parts, after, out):
    out[...] = jnp.sum(parts[...].astype(F32), axis=0) * gain[:1, :]


def pick_kernel(where, weight, near_1, near_2, near_3, after, rows, send_1, send_2):
    rows[:HALF, :] = near_1[...]
    rows[HALF:BLK, :] = near_2[...]
    rows[BLK:, :] = near_3[...]
    send_2[HALF:, :] = near_3[...]

    @pl.when(where[3] == 0)
    def _():
        send_1[:HALF, :] = weight[...]
        send_1[HALF:, :] = near_1[...]
        send_2[:HALF, :] = near_2[...]

    @pl.when(where[3] != 0)
    def _():
        send_1[:HALF, :] = near_1[...]
        send_1[HALF:, :] = near_2[...]
        send_2[:HALF, :] = weight[...]


def relay_kernel(where, source, after, out):
    out[...] = source[...]


def project_kernel(first, where, tok_own, tok_far, kg_own, *refs):
    key_own, key_far, grad_own, grad_far, mark = refs[-5:]
    mark[...] = jnp.zeros_like(mark)
    if first == 0:
        key_own[...] = jnp.zeros_like(key_own)
        key_far[...] = jnp.zeros_like(key_far)
    else:
        key_own[...] = refs[4][...]
        key_far[...] = refs[5][...]
    pieces = [ref.at[row : row + HALF, :] for ref in refs[:4] for row in range(0, ref.shape[0], HALF)]
    if first == 0:
        pieces = [pieces[index] for index in (0, 2, 3, 4, 1, 5, 6, 7)]
    for index, piece in enumerate(pieces):
        half = (where[4] + index // 4) % 2
        block = block_of(where, where[3], first + index % 4)
        cols = pl.ds(pl.multiple_of(block * BLK + half * HALF, HALF), HALF)
        to = slice(index * HALF, (index + 1) * HALF)
        weight = piece[...]
        key_own[...] += jnp.dot(tok_own[:, cols], weight, preferred_element_type=F32)
        key_far[...] += jnp.dot(tok_far[:, cols], weight, preferred_element_type=F32)
        for kg, grad in ((kg_own[...], grad_own), (tok_far[:, 4096:], grad_far)):
            grad[:, to] = lax.dot_general(kg, weight, COLS, preferred_element_type=F32).astype(BF)


def finish_kernel(where, tokens, *refs):
    grads, (key_a, key_b, kg, inverse, key_out, token_grad, mark) = refs[:4], refs[4:]
    mark[...] = jnp.zeros_like(mark)
    c, z = where[3], where[4]
    inv = inverse[:, :1]
    key_sum = key_a[...] + key_b[...]
    key_out[...] = (key_sum * inv).astype(BF)
    dotted = jnp.sum(kg[...].astype(F32) * key_sum, axis=-1, keepdims=True) / 8192.0
    slope = inv * inv * inv * dotted
    for source, grad in enumerate(grads):
        core = (c + source // 2) % 2
        for index in range(8):
            half = (z + index // 4) % 2
            block = block_of(where, core, (source % 2) * 4 + index % 4)
            cols = pl.ds(pl.multiple_of((block * NC + core) * BLK + half * HALF, HALF), HALF)
            part = grad[:, index * HALF : (index + 1) * HALF].astype(F32)
            token_grad[:, cols] = (part - tokens[:, cols].astype(F32) * slope).astype(BF)


def on_device(tokens, norm_gain, weight_codes, weight_scales, key_grad):
    x, yl, yh, c, z = [lax.axis_index(name) for name in ("x", "yl", "yh", "c", "z")]
    shard = (yh * NX + x) * NC + c
    where = jnp.stack([x, yl, yh, c, z, shard]).astype(jnp.int32)
    tokens, key_grad, weight_codes, weight_scales, gains = [
        pltpu.with_memory_space_constraint(array, pltpu.HBM)
        for array in (tokens, key_grad, weight_codes, weight_scales, norm_gain.reshape(1, 8192))
    ]

    def fixed(rows, cols):
        return pl.BlockSpec((rows, cols), lambda r, w: (0, 0))

    def moving(cols):
        return pl.BlockSpec((64, cols), lambda r, w: (r, 0))

    send, keep, kg, inverse, weight, weight_other, gain_row = call(
        prep_kernel,
        "prep",
        [arr((256, 4608)), arr((256, 4096)), arr((256, 512)), arr((256, 128), F32)]
        + [arr((HALF, 512))] * 2
        + [arr((8, BLK), F32)],
        dict(
            grid_spec=pltpu.PrefetchScalarGridSpec(
                num_scalar_prefetch=1,
                grid=(4,),
                in_specs=[
                    moving(8192),
                    moving(512),
                    fixed(BLK, 512),
                    fixed(4, 512),
                    pl.BlockSpec((1, BLK), lambda r, w: (0, w[5])),
                ],
                out_specs=[moving(4608), moving(4096), moving(512), moving(128)]
                + [fixed(HALF, 512)] * 2
                + [fixed(8, BLK)],
            )
        ),
        14,
        2**22,
        9 * 2**20,
    )(where, tokens, key_grad, weight_codes, weight_scales, gains)
    near = [gather_first(weight, s) for s in (1, 2, 3)]
    tok_far = swap_core(send)

    *parts, partial_mark = call(
        functools.partial(partial_kernel, range(4)),
        "partial",
        [arr((512, 1024))] * 4 + [MARK],
        flat(3, 5),
        16,
        2**31,
        9 * 2**20,
        scratch_shapes=[pltpu.VMEM((512, 512), BF)],
    )(where, keep, tok_far, kg)

    near_rows, send_1, send_2 = call(
        pick_kernel,
        "pick",
        [arr((768, 512)), arr((512, 512)), arr((512, 512))],
        flat(4, 3, 1),
        8,
        2**18,
        3 * 2**20,
    )(where, weight, *near, partial_mark)
    got_1, got_2 = gather_second(send_1, 1), gather_second(send_2, 3)


    def project(first, *operands, unused=0):
        return call(
            functools.partial(project_kernel, first),
            "project",
            [arr((256, 512), F32)] * 2 + [arr((256, 2048))] * 2 + [MARK],
            flat(len(operands) - unused, 5, unused),
            16,
            2**31,
            10 * 2**20,
        )(where, *operands)

    key_1, key_far_1, grad_1, grad_far_1, early_mark = project(
        0, keep, tok_far, kg, weight, weight_other, near_rows, along_z(near_rows, 1)
    )
    relayed = call(
        relay_kernel,
        "relay",
        arr((512, 512)),
        dict(in_specs=[smem(), vmem(), anywhere()], out_specs=vmem()),
        8,
        2**18,
        2**20,
    )(where, got_2, early_mark)
    *cuts, cut_mark = call(cut_kernel, "cut", [arr((256, 512))] * 4 + [MARK], flat(4, 5, 1), 10, 2**20, 5 * 2**20)(
        where,
        parts[0],
        first_axis(parts[1], 1),
        first_axis(parts[2], 2),
        first_axis(parts[3], 3),
        early_mark,
    )
    crossed = [second_axis(cuts[s], s) for s in (1, 2, 3)]
    key_2, key_far_2, grad_2, grad_far_2, project_mark = project(
        4,
        keep,
        tok_far,
        kg,
        got_1,
        got_2,
        along_z(got_1, 1),
        along_z(relayed, -1),
        key_1,
        key_far_1,
        cut_mark,
        unused=1,
    )

    plane = call(
        sum_kernel,
        "sum",
        arr((256, 512)),
        dict(in_specs=[smem()] + [vmem()] * 4 + [anywhere()], out_specs=vmem()),
        8,
        14 * 10**9,
        5 * 2**18,
    )(where, cuts[0], *crossed, project_mark)
    over_z = lax.all_to_all(
        plane.reshape(NZ, 32, BLK), "z", split_axis=0, concat_axis=0, tiled=True
    )
    key_out, token_grad, finish_mark = call(
        finish_kernel,
        "finish",
        [arr((256, 512)), arr((256, 8192)), MARK],
        dict(
            grid=(4,),
            in_specs=[smem(), rows_spec(8192)]
            + [rows_spec(2048)] * 4
            + [rows_spec(n) for n in (512, 512, 512, 128)],
            out_specs=[rows_spec(512), rows_spec(8192), pl.BlockSpec((8, 128), lambda r: (0, 0))],
        ),
        14,
        2**23,
        13 * 2**20,
    )(
        where,
        tokens,
        grad_1,
        grad_2,
        swap_core(grad_far_1),
        swap_core(grad_far_2),
        key_2,
        swap_core(key_far_2),
        key_grad,
        inverse,
    )
    weight_grad = call(
        end_kernel,
        "end",
        arr((32, BLK), F32),
        dict(in_specs=[smem(), vmem(), vmem(), anywhere()], out_specs=vmem()),
        8,
        2**17,
        2**19,
    )(where, gain_row, over_z, finish_mark).T
    return key_out, token_grad, weight_grad


def solution(mesh):
    fine = Mesh(np.asarray(mesh.devices).reshape(SIZES), AXES)
    outer, inner = ("z", "yl"), ("yh", "x", "c")
    in_specs = (P(outer + inner, None), P(), P(inner, None), P(inner, None), P(outer + inner, None))
    out_specs = (P(outer + inner, None), P(outer + inner, None), P(inner, outer))
    return jax.shard_map(
        on_device, mesh=fine, in_specs=in_specs, out_specs=out_specs, check_vma=False
    )
```

time: 103 us -> 96.8 us (0.940)
  waiting for transfers between devices: 40.4 us -> 31.3 us
  starting transfers between devices: 31.6 us -> 35.4 us
  Pallas kernels: 27.8 us -> 25.7 us
  local copies, waits for them, and re-layouts: 1.12 us -> 3.12 us
    ppermute x17 -> x18, waiting for transfers between devices: 34.9 us -> 26.3 us  [permute(): return lax.ppermute(array, AXES, pairs)]
    ppermute x17 -> x18, starting transfers between devices: 25.2 us -> 28.7 us  [permute(): return lax.ppermute(array, AXES, pairs)]
    pallas_call x8 -> x7, Pallas kernels: 16.9 us -> 14.2 us  [the longest x2 7.74 us: project(): call(functools.partial(project_kernel, first), 'project', [arr((256, 512)...]
    unnamed x4 -> x10, local copies, waits for them, and re-layouts: 1.04 us -> 3.04 us
    pallas_call x1, Pallas kernels: 3.55 us -> 4.78 us  [on_device(): call(prep_kernel, 'prep', [arr((256, 4608)), arr((256, 4096)), arr((256,...]
  transfers between devices with their start and end apart: 18 -> 19, of which waited for: 9 -> 9; matrix products, arithmetic and copies ran while one was open for 0% -> 0% of each run, Pallas kernels for 20% -> 20%
where the time goes in v4:
time: 96.8 us; the launch traced here: 96.3 us
  starting transfers between devices  35.4 us (37%)
  waiting for transfers between devices  31.3 us (32%)
  Pallas kernels  25.7 us (27%)
  local copies, waits for them, and re-layouts  3.12 us (3%)
    ppermute x18, starting transfers between devices, permute(): return lax.ppermute(array, AXES, pairs)  28.7 us
    ppermute x18, waiting for transfers between devices, permute(): return lax.ppermute(array, AXES, pairs)  26.3 us
    pallas_call x2, Pallas kernels, project(): call(functools.partial(project_kernel, first), 'project', [arr((256, 512)...  7.74 us
    all_to_all x1, starting transfers between devices, on_device(): lax.all_to_all(plane.reshape(NZ, 32, BLK), 'z', split_axis=0, concat_axis...  6.71 us
    pallas_call x1, Pallas kernels, on_device(): call(finish_kernel, 'finish', [arr((256, 512)), arr((256, 8192)), MARK],...  6.01 us
    all_to_all x1, waiting for transfers between devices, on_device(): lax.all_to_all(plane.reshape(NZ, 32, BLK), 'z', split_axis=0, concat_axis...  5.06 us
    pallas_call x1, Pallas kernels, on_device(): call(prep_kernel, 'prep', [arr((256, 4608)), arr((256, 4096)), arr((256,...  4.78 us
    unnamed x10, local copies, waits for them, and re-layouts  3.04 us
  transfers between devices with their start and end apart: 19, of which 9 were waited for; matrix products, arithmetic and copies ran while one was open for 0% of the time, Pallas kernels for 20%

profile of v4, /device:TPU:6, one launch (start us, length us, event | category | flops | bytes accessed | tf_op | source)
XLA Modules:
  0.0 96.3 jit_solution(8315733532296411740)
XLA Ops:
  0.6 0.1 stack.27.where
  0.7 4.8 %prep.1 = (bf16[256,4608]{1,0:T(8,128)(2,1)S(1)}, bf16[256,4096]{1,0:T(8,128)(2,1)S(1)}, bf16[256,512]{1,0:T(8,128)(2,1)S(1)}, f32[256,128]{1,0:T(8,128)S(1)}, b...) custom-call(s32[6]{0:T(128)S(1)} %stack.27.where, bf16[256,8192]{1,0:T(8,128)(2,1)} %tokens.3, ...), custom_call_target="tpu_custom_call" | custom-call | flops 1 | bytes 1 | tf_op jit(solution)/shard_map/prep/pallas_call | solution.py:297
  5.5 0.0 copy-start.3
  5.5 0.6 copy-done.3
  6.1 2.2 %collective-permute-start.1 = (bf16[256,512]{1,0:T(8,128)(2,1)S(1)}, bf16[256,512]{1,0:T(8,128)(2,1)S(1)}, u32[]{:S(2)}, u32[]{:S(2)}) collective-permute-start(bf16[256,512]{1,0:T(8,128)(2,1)S(1)} %get-tuple-element.39.weight.refs_0_), channel_id=1, source_target_pairs={{0,2},{1,9},{2,4},{3,11},{4,6},{5,13},{6,0},{7,15},{8,10},{9,1},{1... | collective-permute-start | bytes 786440 | tf_op jit(solution)/shard_map/ppermute | solution.py:27
  8.3 0.7 collective-permute-start.2
  9.0 0.2 collective-permute-start.3
  9.2 1.5 %collective-permute-done.tok_far = bf16[256,4608]{1,0:T(8,128)(2,1)S(1)} collective-permute-done((bf16[256,4608]{1,0:T(8,128)(2,1)S(1)}, bf16[256,4608]{1,0:T(8,128)(2,1)S(1)}, u32[]{:S(2)}, u32[]{:S(2)}) %collective-permute-start) | collective-permute-done | bytes 2359328 | tf_op jit(solution)/shard_map/ppermute | solution.py:27
  10.7 3.0 %partial.1 = (bf16[512,1024]{1,0:T(8,128)(2,1)S(1)}, bf16[512,1024]{1,0:T(8,128)(2,1)S(1)}, bf16[512,1024]{1,0:T(8,128)(2,1)S(1)}, bf16[512,1024]{1,0:T(8,128)(2,1)S(1)}, f32[8,128]{1,0:T(8,128)S(1)}) custom-call(s32[6]{0:T(128)S(1)} %stack.27.where, bf16[256,4096]{1,0:T(8,128)(2,1)S(1)} %get-tuple-element.36.tok_own, ...), custom_call_target="tpu_custom_call" | custom-call | flops 1 | bytes 1 | tf_op jit(solution)/shard_map/partial/pallas_call | solution.py:326
  13.6 2.8 %collective-permute-done.1.near_1 = bf16[256,512]{1,0:T(8,128)(2,1)S(1)} collective-permute-done((bf16[256,512]{1,0:T(8,128)(2,1)S(1)}, bf16[256,512]{1,0:T(8,128)(2,1)S(1)}, u32[]{:S(2)}, u32[]{:S(2)}) %collective-permute-start.1) | collective-permute-done | bytes 262176 | tf_op jit(solution)/shard_map/ppermute | solution.py:27
  16.5 2.4 %collective-permute-done.2.near_2 = bf16[256,512]{1,0:T(8,128)(2,1)S(1)} collective-permute-done((bf16[256,512]{1,0:T(8,128)(2,1)S(1)}, bf16[256,512]{1,0:T(8,128)(2,1)S(1)}, u32[]{:S(2)}, u32[]{:S(2)}) %collective-permute-start.2) | collective-permute-done | bytes 262176 | tf_op jit(solution)/shard_map/ppermute | solution.py:27
  18.9 2.4 %collective-permute-done.3.near_3 = bf16[256,512]{1,0:T(8,128)(2,1)S(1)} collective-permute-done((bf16[256,512]{1,0:T(8,128)(2,1)S(1)}, bf16[256,512]{1,0:T(8,128)(2,1)S(1)}, u32[]{:S(2)}, u32[]{:S(2)}) %collective-permute-start.3) | collective-permute-done | bytes 262176 | tf_op jit(solution)/shard_map/ppermute | solution.py:27
  21.3 0.7 pick.1
  22.0 2.2 %collective-permute-start.5 = (bf16[512,512]{1,0:T(8,128)(2,1)S(1)}, bf16[512,512]{1,0:T(8,128)(2,1)S(1)}, u32[]{:S(2)}, u32[]{:S(2)}) collective-permute-start(bf16[512,512]{1,0:T(8,128)(2,1)S(1)} %get-tuple-element.44), channel_id=1, source_target_pairs={{0,8},{1,3},{2,10},{3,5},{4,12},{5,7},{6,14},{7,1},{8,0},{9,11},{1... | collective-permute-start | bytes 1572872 | tf_op jit(solution)/shard_map/ppermute | solution.py:27
  24.2 1.9 %collective-permute-start.4 = (bf16[768,512]{1,0:T(8,128)(2,1)S(1)}, bf16[768,512]{1,0:T(8,128)(2,1)S(1)}, u32[]{:S(2)}, u32[]{:S(2)}) collective-permute-start(bf16[768,512]{1,0:T(8,128)(2,1)S(1)} %get-tuple-element.42.refs_2_), channel_id=1, source_target_pairs={{0,32},{1,33},{2,34},{3,35},{4,36},{5,37},{6,38},{7,39},{8,40},{9,... | collective-permute-start | bytes 2359304 | tf_op jit(solution)/shard_map/ppermute | solution.py:27
  26.1 1.4 %collective-permute-start.10 = (bf16[512,1024]{1,0:T(8,128)(2,1)S(1)}, bf16[512,1024]{1,0:T(8,128)(2,1)S(1)}, u32[]{:S(2)}, u32[]{:S(2)}) collective-permute-start(bf16[512,1024]{1,0:T(8,128)(2,1)S(1)} %get-tuple-element.51), channel_id=1, source_target_pairs={{0,4},{1,9},{2,6},{3,11},{4,0},{5,13},{6,2},{7,15},{8,12},{9,1},{1... | collective-permute-start | bytes 3145736 | tf_op jit(solution)/shard_map/ppermute | solution.py:27
  27.5 3.2 %collective-permute-start.9 = (bf16[512,1024]{1,0:T(8,128)(2,1)S(1)}, bf16[512,1024]{1,0:T(8,128)(2,1)S(1)}, u32[]{:S(2)}, u32[]{:S(2)}) collective-permute-start(bf16[512,1024]{1,0:T(8,128)(2,1)S(1)} %get-tuple-element.50), channel_id=1, source_target_pairs={{0,2},{1,17},{2,4},{3,19},{4,6},{5,21},{6,0},{7,23},{8,10},{9,25},... | collective-permute-start | bytes 3145736 | tf_op jit(solution)/shard_map/ppermute | solution.py:27
  30.8 5.7 %collective-permute-done.5.refs_0_ = bf16[512,512]{1,0:T(8,128)(2,1)S(1)} collective-permute-done((bf16[512,512]{1,0:T(8,128)(2,1)S(1)}, bf16[512,512]{1,0:T(8,128)(2,1)S(1)}, u32[]{:S(2)}, u32[]{:S(2)}) %collective-permute-start.5) | collective-permute-done | bytes 524320 | tf_op jit(solution)/shard_map/ppermute | solution.py:27
  36.5 3.6 %collective-permute-start.6 = (bf16[512,512]{1,0:T(8,128)(2,1)S(1)}, bf16[512,512]{1,0:T(8,128)(2,1)S(1)}, u32[]{:S(2)}, u32[]{:S(2)}) collective-permute-start(bf16[512,512]{1,0:T(8,128)(2,1)S(1)} %get-tuple-element.45), channel_id=1, source_target_pairs={{0,8},{1,7},{2,10},{3,1},{4,12},{5,3},{6,14},{7,5},{8,0},{9,15},{1... | collective-permute-start | bytes 1572872 | tf_op jit(solution)/shard_map/ppermute | solution.py:27
  40.1 6.7 %collective-permute-done.4.refs_3_ = bf16[768,512]{1,0:T(8,128)(2,1)S(1)} collective-permute-done((bf16[768,512]{1,0:T(8,128)(2,1)S(1)}, bf16[768,512]{1,0:T(8,128)(2,1)S(1)}, u32[]{:S(2)}, u32[]{:S(2)}) %collective-permute-start.4) | collective-permute-done | bytes 786464 | tf_op jit(solution)/shard_map/ppermute | solution.py:27
  46.8 0.0 collective-permute-start.7
  46.8 3.8 %project.2 = (f32[256,512]{1,0:T(8,128)S(1)}, f32[256,512]{1,0:T(8,128)S(1)}, bf16[256,2048]{1,0:T(8,128)(2,1)S(1)}, bf16[256,2048]{1,0:T(8,128)(2,1)}, f32[8,128]{1,0:T(8,128)S(1)}) custom-call(s32[6]{0:T(128)S(1)} %stack.27.where, bf16[256,4096]{1,0:T(8,128)(2,1)S(1)} %get-tuple-element.36.tok_own, bf16[256,4608]{1,0:T(8,128)(2,1)S(1)} %collective-permute-done.tok_far, ...), custom_call_target="tpu_custom_call" | custom-call | flops 1 | bytes 1 | tf_op jit(solution)/shard_map/project/pallas_call | solution.py:350
  50.7 2.2 %collective-permute-done.6.source.refs_1_ = bf16[512,512]{1,0:T(8,128)(2,1)S(1)} collective-permute-done((bf16[512,512]{1,0:T(8,128)(2,1)S(1)}, bf16[512,512]{1,0:T(8,128)(2,1)S(1)}, u32[]{:S(2)}, u32[]{:S(2)}) %collective-permute-start.6) | collective-permute-done | bytes 524320 | tf_op jit(solution)/shard_map/ppermute | solution.py:27
  52.9 0.6 relay.1
  53.5 6.5 %collective-permute-start.8 = (bf16[512,512]{1,0:T(8,128)(2,1)S(1)}, bf16[512,512]{1,0:T(8,128)(2,1)S(1)}, u32[]{:S(2)}, u32[]{:S(2)}) collective-permute-start(bf16[512,512]{1,0:T(8,128)(2,1)S(1)} %relay.1), channel_id=1, source_target_pairs={{0,224},{1,225},{2,226},{3,227},{4,228},{5,229},{6,230},{7,231},{8... | collective-permute-start | bytes 1572872 | tf_op jit(solution)/shard_map/ppermute | solution.py:27
  60.0 0.0 collective-permute-done.10.refs_2_
  60.0 0.0 collective-permute-done.11.refs_3_
  60.0 0.0 collective-permute-done.9.refs_1_
  60.0 1.1 %cut.1 = (bf16[256,512]{1,0:T(8,128)(2,1)S(1)}, bf16[256,512]{1,0:T(8,128)(2,1)S(1)}, bf16[256,512]{1,0:T(8,128)(2,1)S(1)}, bf16[256,512]{1,0:T(8,128)(2,1)S(1)}, f32[8,128]{1,0:T(8,128)S(1)}) custom-call(s32[6]{0:T(128)S(1)} %stack.27.where, bf16[512,1024]{1,0:T(8,128)(2,1)S(1)} %get-tuple-element.49.refs_0_, ...), custom_call_target="tpu_custom_call" | custom-call | flops 1 | bytes 1 | tf_op jit(solution)/shard_map/cut/pallas_call | solution.py:372
  61.1 1.5 %collective-permute-start.15 = (bf16[256,512]{1,0:T(8,128)(2,1)S(1)}, bf16[256,512]{1,0:T(8,128)(2,1)S(1)}, u32[]{:S(2)}, u32[]{:S(2)}) collective-permute-start(bf16[256,512]{1,0:T(8,128)(2,1)S(1)} %get-tuple-element.64), channel_id=1, source_target_pairs={{0,16},{1,3},{2,18},{3,5},{4,20},{5,7},{6,22},{7,1},{8,24},{9,11},... | collective-permute-start | bytes 786440 | tf_op jit(solution)/shard_map/ppermute | solution.py:27
  62.5 3.3 %collective-permute-start.16 = (bf16[256,512]{1,0:T(8,128)(2,1)S(1)}, bf16[256,512]{1,0:T(8,128)(2,1)S(1)}, u32[]{:S(2)}, u32[]{:S(2)}) collective-permute-start(bf16[256,512]{1,0:T(8,128)(2,1)S(1)} %get-tuple-element.65), channel_id=1, source_target_pairs={{0,8},{1,5},{2,10},{3,7},{4,12},{5,1},{6,14},{7,3},{8,0},{9,13},{1... | collective-permute-start | bytes 786440 | tf_op jit(solution)/shard_map/ppermute | solution.py:27
  65.8 1.5 %collective-permute-start.17 = (bf16[256,512]{1,0:T(8,128)(2,1)S(1)}, bf16[256,512]{1,0:T(8,128)(2,1)S(1)}, u32[]{:S(2)}, u32[]{:S(2)}) collective-permute-start(bf16[256,512]{1,0:T(8,128)(2,1)S(1)} %get-tuple-element.66), channel_id=1, source_target_pairs={{0,24},{1,7},{2,26},{3,1},{4,28},{5,3},{6,30},{7,5},{8,16},{9,15},... | collective-permute-start | bytes 786440 | tf_op jit(solution)/shard_map/ppermute | solution.py:27
  67.3 0.0 collective-permute-done.7.refs_2_
  67.3 2.5 %collective-permute-done.8.refs_3_ = bf16[512,512]{1,0:T(8,128)(2,1)S(1)} collective-permute-done((bf16[512,512]{1,0:T(8,128)(2,1)S(1)}, bf16[512,512]{1,0:T(8,128)(2,1)S(1)}, u32[]{:S(2)}, u32[]{:S(2)}) %collective-permute-start.8) | collective-permute-done | bytes 524320 | tf_op jit(solution)/shard_map/ppermute | solution.py:27
  69.8 3.9 %project.3 = (f32[256,512]{1,0:T(8,128)S(1)}, f32[256,512]{1,0:T(8,128)}, bf16[256,2048]{1,0:T(8,128)(2,1)S(1)}, bf16[256,2048]{1,0:T(8,128)(2,1)}, f32[8,128]{1,0:T(8,128)S(1)}) custom-call(s32[6]{0:T(128)S(1)} %stack.27.where, bf16[256,4096]{1,0:T(8,128)(2,1)S(1)} %get-tuple-element.36.tok_own, bf16[256,4608]{1,0:T(8,128)(2,1)S(1)} %collective-permute-done.tok_far, ...), custom_call_target="tpu_custom_call" | custom-call | flops 1 | bytes 1 | tf_op jit(solution)/shard_map/project/pallas_call | solution.py:350
  73.7 0.0 collective-permute-start.13
  73.7 0.0 collective-permute-done.15.refs_1_
  73.7 0.5 collective-permute-start.14
  74.2 0.0 collective-permute-done.16.refs_2_
  74.2 0.0 collective-permute-done.17.refs_3_
  74.2 0.7 sum.1
  74.9 0.7 copy-done.2
  75.6 6.7 %all-to-all-start = ((bf16[8,32,512]{2,1,0:T(8,128)(2,1)}), bf16[8,32,512]{2,1,0:T(8,128)(2,1)S(1)}, u32[]{:S(2)}, u32[]{:S(2)}) async-start(bf16[8,32,512]{2,1,0:T(8,128)(2,1)} %bitcast.9), calls=%async_computation | async-start | bytes 524288 | tf_op jit(solution)/shard_map/all_to_all | solution.py:405
  82.3 1.0 %copy-done.1 = f32[256,512]{1,0:T(8,128)S(1)} copy-done((f32[256,512]{1,0:T(8,128)S(1)}, f32[256,512]{1,0:T(8,128)}, u32[]{:S(2)}) %copy-start.1) | copy-done | bytes 524312
  83.3 6.0 %finish.1 = (bf16[256,512]{1,0:T(8,128)(2,1)}, bf16[256,8192]{1,0:T(8,128)(2,1)}, f32[8,128]{1,0:T(8,128)S(1)}) custom-call(s32[6]{0:T(128)S(1)} %stack.27.where, bf16[256,8192]{1,0:T(8,128)(2,1)} %tokens.3, bf16[256,2048]{1,0:T(8,128)(2,1)S(1)} %get-tuple-element.43.refs_0_, bf16[256,2048]{1,0:T(8,128)(2,1)S(1)} %get-tuple-element.54.refs_1_, ...), custom_call_target="tpu_custom_call" | custom-call | flops 8388608 | bytes 13631488 | tf_op jit(solution)/shard_map/finish/pallas_call | solution.py:408
  89.3 5.1 %all-to-all-done.parts = bf16[8,32,512]{2,1,0:T(8,128)(2,1)S(1)} async-done(((bf16[8,32,512]{2,1,0:T(8,128)(2,1)}), bf16[8,32,512]{2,1,0:T(8,128)(2,1)S(1)}, u32[]{:S(2)}, u32[]{:S(2)}) %all-to-all-start) | async-done | bytes 262176 | tf_op jit(solution)/shard_map/all_to_all | solution.py:405
  94.4 0.7 copy-done.4
  95.1 1.2 %end.1 = f32[32,512]{1,0:T(8,128)} custom-call(s32[6]{0:T(128)S(1)} %stack.27.where, f32[8,512]{1,0:T(8,128)S(1)} %copy-done.4, bf16[8,32,512]{2,1,0:T(8,128)(2,1)S(1)} %all-to-all-done.parts, f32[8,128]{1,0:T(8,128)S(1)} %get-tuple-element.68.after), custom_call_target="tpu_custom_call" | custom-call | flops 1 | bytes 1 | tf_op jit(solution)/shard_map/end/pallas_call | solution.py:434
  (11 shorter events, 0.0 us)
Async XLA Ops:
  5.5 0.6 copy-start.3
  6.1 4.5 %collective-permute-start = (bf16[256,4608]{1,0:T(8,128)(2,1)S(1)}, bf16[256,4608]{1,0:T(8,128)(2,1)S(1)}, u32[]{:S(2)}, u32[]{:S(2)}) collective-permute-start(bf16[256,4608]{1,0:T(8,128)(2,1)S(1)} %get-tuple-element.37), channel_id=1, source_target_pairs={{0,1},{1,0},{2,3},{3,2},{4,5},{5,4},{6,7},{7,6},{8,9},{9,8},{10,11... | collective-permute-start | bytes 7077896 | tf_op jit(solution)/shard_map/ppermute | solution.py:27
  6.1 10.3 %collective-permute-start.1 = (bf16[256,512]{1,0:T(8,128)(2,1)S(1)}, bf16[256,512]{1,0:T(8,128)(2,1)S(1)}, u32[]{:S(2)}, u32[]{:S(2)}) collective-permute-start(bf16[256,512]{1,0:T(8,128)(2,1)S(1)} %get-tuple-element.39.weight.refs_0_), channel_id=1, source_target_pairs={{0,2},{1,9},{2,4},{3,11},{4,6},{5,13},{6,0},{7,15},{8,10},{9,1},{1... | collective-permute-start | bytes 786440 | tf_op jit(solution)/shard_map/ppermute | solution.py:27
  8.3 10.5 %collective-permute-start.2 = (bf16[256,512]{1,0:T(8,128)(2,1)S(1)}, bf16[256,512]{1,0:T(8,128)(2,1)S(1)}, u32[]{:S(2)}, u32[]{:S(2)}) collective-permute-start(bf16[256,512]{1,0:T(8,128)(2,1)S(1)} %get-tuple-element.39.weight.refs_0_), channel_id=1, source_target_pairs={{0,4},{1,3},{2,6},{3,5},{4,0},{5,7},{6,2},{7,1},{8,12},{9,11},{10,... | collective-permute-start | bytes 786440 | tf_op jit(solution)/shard_map/ppermute | solution.py:27
  9.0 12.3 %collective-permute-start.3 = (bf16[256,512]{1,0:T(8,128)(2,1)S(1)}, bf16[256,512]{1,0:T(8,128)(2,1)S(1)}, u32[]{:S(2)}, u32[]{:S(2)}) collective-permute-start(bf16[256,512]{1,0:T(8,128)(2,1)S(1)} %get-tuple-element.39.weight.refs_0_), channel_id=1, source_target_pairs={{0,6},{1,15},{2,0},{3,9},{4,2},{5,11},{6,4},{7,13},{8,14},{9,7},{1... | collective-permute-start | bytes 786440 | tf_op jit(solution)/shard_map/ppermute | solution.py:27
  22.0 14.5 %collective-permute-start.5 = (bf16[512,512]{1,0:T(8,128)(2,1)S(1)}, bf16[512,512]{1,0:T(8,128)(2,1)S(1)}, u32[]{:S(2)}, u32[]{:S(2)}) collective-permute-start(bf16[512,512]{1,0:T(8,128)(2,1)S(1)} %get-tuple-element.44), channel_id=1, source_target_pairs={{0,8},{1,3},{2,10},{3,5},{4,12},{5,7},{6,14},{7,1},{8,0},{9,11},{1... | collective-permute-start | bytes 1572872 | tf_op jit(solution)/shard_map/ppermute | solution.py:27
  24.2 22.7 %collective-permute-start.4 = (bf16[768,512]{1,0:T(8,128)(2,1)S(1)}, bf16[768,512]{1,0:T(8,128)(2,1)S(1)}, u32[]{:S(2)}, u32[]{:S(2)}) collective-permute-start(bf16[768,512]{1,0:T(8,128)(2,1)S(1)} %get-tuple-element.42.refs_2_), channel_id=1, source_target_pairs={{0,32},{1,33},{2,34},{3,35},{4,36},{5,37},{6,38},{7,39},{8,40},{9,... | collective-permute-start | bytes 2359304 | tf_op jit(solution)/shard_map/ppermute | solution.py:27
  26.1 33.9 %collective-permute-start.10 = (bf16[512,1024]{1,0:T(8,128)(2,1)S(1)}, bf16[512,1024]{1,0:T(8,128)(2,1)S(1)}, u32[]{:S(2)}, u32[]{:S(2)}) collective-permute-start(bf16[512,1024]{1,0:T(8,128)(2,1)S(1)} %get-tuple-element.51), channel_id=1, source_target_pairs={{0,4},{1,9},{2,6},{3,11},{4,0},{5,13},{6,2},{7,15},{8,12},{9,1},{1... | collective-permute-start | bytes 3145736 | tf_op jit(solution)/shard_map/ppermute | solution.py:27
  27.5 32.5 %collective-permute-start.11 = (bf16[512,1024]{1,0:T(8,128)(2,1)S(1)}, bf16[512,1024]{1,0:T(8,128)(2,1)S(1)}, u32[]{:S(2)}, u32[]{:S(2)}) collective-permute-start(bf16[512,1024]{1,0:T(8,128)(2,1)S(1)} %get-tuple-element.52), channel_id=1, source_target_pairs={{0,6},{1,25},{2,0},{3,27},{4,2},{5,29},{6,4},{7,31},{8,14},{9,17},... | collective-permute-start | bytes 3145736 | tf_op jit(solution)/shard_map/ppermute | solution.py:27
  27.5 32.5 %collective-permute-start.9 = (bf16[512,1024]{1,0:T(8,128)(2,1)S(1)}, bf16[512,1024]{1,0:T(8,128)(2,1)S(1)}, u32[]{:S(2)}, u32[]{:S(2)}) collective-permute-start(bf16[512,1024]{1,0:T(8,128)(2,1)S(1)} %get-tuple-element.50), channel_id=1, source_target_pairs={{0,2},{1,17},{2,4},{3,19},{4,6},{5,21},{6,0},{7,23},{8,10},{9,25},... | collective-permute-start | bytes 3145736 | tf_op jit(solution)/shard_map/ppermute | solution.py:27
  36.5 16.4 %collective-permute-start.6 = (bf16[512,512]{1,0:T(8,128)(2,1)S(1)}, bf16[512,512]{1,0:T(8,128)(2,1)S(1)}, u32[]{:S(2)}, u32[]{:S(2)}) collective-permute-start(bf16[512,512]{1,0:T(8,128)(2,1)S(1)} %get-tuple-element.45), channel_id=1, source_target_pairs={{0,8},{1,7},{2,10},{3,1},{4,12},{5,3},{6,14},{7,5},{8,0},{9,15},{1... | collective-permute-start | bytes 1572872 | tf_op jit(solution)/shard_map/ppermute | solution.py:27
  46.8 20.5 %collective-permute-start.7 = (bf16[512,512]{1,0:T(8,128)(2,1)S(1)}, bf16[512,512]{1,0:T(8,128)(2,1)S(1)}, u32[]{:S(2)}, u32[]{:S(2)}) collective-permute-start(bf16[512,512]{1,0:T(8,128)(2,1)S(1)} %collective-permute-done.5.refs_0_), channel_id=1, source_target_pairs={{0,32},{1,33},{2,34},{3,35},{4,36},{5,37},{6,38},{7,39},{8,40},{9,... | collective-permute-start | bytes 1572872 | tf_op jit(solution)/shard_map/ppermute | solution.py:27
  53.5 16.3 %collective-permute-start.8 = (bf16[512,512]{1,0:T(8,128)(2,1)S(1)}, bf16[512,512]{1,0:T(8,128)(2,1)S(1)}, u32[]{:S(2)}, u32[]{:S(2)}) collective-permute-start(bf16[512,512]{1,0:T(8,128)(2,1)S(1)} %relay.1), channel_id=1, source_target_pairs={{0,224},{1,225},{2,226},{3,227},{4,228},{5,229},{6,230},{7,231},{8... | collective-permute-start | bytes 1572872 | tf_op jit(solution)/shard_map/ppermute | solution.py:27
  61.1 12.6 %collective-permute-start.15 = (bf16[256,512]{1,0:T(8,128)(2,1)S(1)}, bf16[256,512]{1,0:T(8,128)(2,1)S(1)}, u32[]{:S(2)}, u32[]{:S(2)}) collective-permute-start(bf16[256,512]{1,0:T(8,128)(2,1)S(1)} %get-tuple-element.64), channel_id=1, source_target_pairs={{0,16},{1,3},{2,18},{3,5},{4,20},{5,7},{6,22},{7,1},{8,24},{9,11},... | collective-permute-start | bytes 786440 | tf_op jit(solution)/shard_map/ppermute | solution.py:27
  62.5 11.6 %collective-permute-start.16 = (bf16[256,512]{1,0:T(8,128)(2,1)S(1)}, bf16[256,512]{1,0:T(8,128)(2,1)S(1)}, u32[]{:S(2)}, u32[]{:S(2)}) collective-permute-start(bf16[256,512]{1,0:T(8,128)(2,1)S(1)} %get-tuple-element.65), channel_id=1, source_target_pairs={{0,8},{1,5},{2,10},{3,7},{4,12},{5,1},{6,14},{7,3},{8,0},{9,13},{1... | collective-permute-start | bytes 786440 | tf_op jit(solution)/shard_map/ppermute | solution.py:27
  65.8 8.4 %collective-permute-start.17 = (bf16[256,512]{1,0:T(8,128)(2,1)S(1)}, bf16[256,512]{1,0:T(8,128)(2,1)S(1)}, u32[]{:S(2)}, u32[]{:S(2)}) collective-permute-start(bf16[256,512]{1,0:T(8,128)(2,1)S(1)} %get-tuple-element.66), channel_id=1, source_target_pairs={{0,24},{1,7},{2,26},{3,1},{4,28},{5,3},{6,30},{7,5},{8,16},{9,15},... | collective-permute-start | bytes 786440 | tf_op jit(solution)/shard_map/ppermute | solution.py:27
  67.3 15.0 %collective-permute-start.12 = (bf16[256,2048]{1,0:T(8,128)(2,1)}, bf16[256,2048]{1,0:T(8,128)(2,1)S(1)}, u32[]{:S(2)}, u32[]{:S(2)}) collective-permute-start(bf16[256,2048]{1,0:T(8,128)(2,1)} %get-tuple-element.55), channel_id=1, source_target_pairs={{0,1},{1,0},{2,3},{3,2},{4,5},{5,4},{6,7},{7,6},{8,9},{9,8},{10,11... | collective-permute-start | bytes 3145736 | tf_op jit(solution)/shard_map/ppermute | solution.py:27
  73.7 1.2 %copy-start = (f32[256,512]{1,0:T(8,128)}, f32[256,512]{1,0:T(8,128)S(1)}, u32[]{:S(2)}) copy-start(f32[256,512]{1,0:T(8,128)S(1)} %get-tuple-element.57.refs_4_) | copy-start | bytes 1572868
  73.7 8.6 %collective-permute-start.13 = (bf16[256,2048]{1,0:T(8,128)(2,1)}, bf16[256,2048]{1,0:T(8,128)(2,1)}, u32[]{:S(2)}, u32[]{:S(2)}) collective-permute-start(bf16[256,2048]{1,0:T(8,128)(2,1)} %get-tuple-element.56), channel_id=1, source_target_pairs={{0,1},{1,0},{2,3},{3,2},{4,5},{5,4},{6,7},{7,6},{8,9},{9,8},{10,11... | collective-permute-start | bytes 3145736 | tf_op jit(solution)/shard_map/ppermute | solution.py:27
  73.7 8.6 %collective-permute-start.14 = (f32[256,512]{1,0:T(8,128)}, f32[256,512]{1,0:T(8,128)}, u32[]{:S(2)}, u32[]{:S(2)}) collective-permute-start(f32[256,512]{1,0:T(8,128)} %get-tuple-element.58), channel_id=1, source_target_pairs={{0,1},{1,0},{2,3},{3,2},{4,5},{5,4},{6,7},{7,6},{8,9},{9,8},{10,11... | collective-permute-start | bytes 1572872 | tf_op jit(solution)/shard_map/ppermute | solution.py:27
  74.9 0.7 copy-start.2
  75.6 18.8 %all-to-all-start = ((bf16[8,32,512]{2,1,0:T(8,128)(2,1)}), bf16[8,32,512]{2,1,0:T(8,128)(2,1)S(1)}, u32[]{:S(2)}, u32[]{:S(2)}) async-start(bf16[8,32,512]{2,1,0:T(8,128)(2,1)} %bitcast.9), calls=%async_computation | async-start | bytes 524288 | tf_op jit(solution)/shard_map/all_to_all | solution.py:405
  82.3 1.0 %copy-start.1 = (f32[256,512]{1,0:T(8,128)S(1)}, f32[256,512]{1,0:T(8,128)}, u32[]{:S(2)}) copy-start(f32[256,512]{1,0:T(8,128)} %copy-done) | copy-start | bytes 1572868
  94.4 0.7 copy-start.4

commit v5 on v4

--- a/solution.py
+++ b/solution.py
@@ -205,12 +205,15 @@
         )
 
 
-def sum_kernel(where, *refs):
-    refs[5][...] = add(refs[:4], slice(None), slice(None))
-
-
-def end_kernel(where, gain, parts, after, out):
-    out[...] = jnp.sum(parts[...].astype(F32), axis=0) * gain[:1, :]
+def sum_kernel(where, gain, *refs):
+    total = refs[0][...].astype(F32)
+    for part in refs[1:4]:
+        total = total + part[...].astype(F32)
+    refs[5][...] = (total * gain[:1, :]).astype(BF)
+
+
+def end_kernel(where, parts, after, out):
+    out[...] = jnp.sum(parts[...].astype(F32), axis=0)
 
 
 def pick_kernel(where, weight, near_1, near_2, near_3, after, rows, send_1, send_2):
@@ -397,11 +400,11 @@
         sum_kernel,
         "sum",
         arr((256, 512)),
-        dict(in_specs=[smem()] + [vmem()] * 4 + [anywhere()], out_specs=vmem()),
+        dict(in_specs=[smem()] + [vmem()] * 5 + [anywhere()], out_specs=vmem()),
         8,
         14 * 10**9,
         5 * 2**18,
-    )(where, cuts[0], *crossed, project_mark)
+    )(where, gain_row, cuts[0], *crossed, project_mark)
     over_z = lax.all_to_all(
         plane.reshape(NZ, 32, BLK), "z", split_axis=0, concat_axis=0, tiled=True
     )
@@ -435,11 +438,11 @@
         end_kernel,
         "end",
         arr((32, BLK), F32),
-        dict(in_specs=[smem(), vmem(), vmem(), anywhere()], out_specs=vmem()),
+        dict(in_specs=[smem(), vmem(), anywhere()], out_specs=vmem()),
         8,
         2**17,
         2**19,
-    )(where, gain_row, over_z, finish_mark).T
+    )(where, over_z, finish_mark).T
     return key_out, token_grad, weight_grad
 
 

time: 96.8 us -> 95.6 us (0.988)
  local copies, waits for them, and re-layouts: 3.12 us -> 1.8 us
    unnamed x10 -> x6, local copies, waits for them, and re-layouts: 3.04 us -> 1.71 us
where the time goes in v5:
time: 95.6 us; the launch traced here: 95.3 us
  starting transfers between devices  35.2 us (37%)
  waiting for transfers between devices  31.8 us (33%)
  Pallas kernels  25.8 us (27%)
  local copies, waits for them, and re-layouts  1.8 us (2%)
    ppermute x18, starting transfers between devices, permute(): return lax.ppermute(array, AXES, pairs)  28.4 us
    ppermute x18, waiting for transfers between devices, permute(): return lax.ppermute(array, AXES, pairs)  26.7 us
    pallas_call x2, Pallas kernels, project(): call(functools.partial(project_kernel, first), 'project', [arr((256, 512)...  7.77 us
    all_to_all x1, starting transfers between devices, on_device(): lax.all_to_all(plane.reshape(NZ, 32, BLK), 'z', split_axis=0, concat_axis...  6.75 us
    pallas_call x1, Pallas kernels, on_device(): call(finish_kernel, 'finish', [arr((256, 512)), arr((256, 8192)), MARK],...  6.01 us
    all_to_all x1, waiting for transfers between devices, on_device(): lax.all_to_all(plane.reshape(NZ, 32, BLK), 'z', split_axis=0, concat_axis...  5.06 us
    pallas_call x1, Pallas kernels, on_device(): call(prep_kernel, 'prep', [arr((256, 4608)), arr((256, 4096)), arr((256,...  4.78 us
    pallas_call x1, Pallas kernels, on_device(): call(functools.partial(partial_kernel, range(4)), 'partial', [arr((512, 1...  2.98 us
  transfers between devices with their start and end apart: 19, of which 9 were waited for; matrix products, arithmetic and copies ran while one was open for 0% of the time, Pallas kernels for 20%

profile of v5, /device:TPU:6, one launch (start us, length us, event | category | flops | bytes accessed | tf_op | source)
XLA Modules:
  0.0 95.3 jit_solution(15630551599874393203)
XLA Ops:
  0.6 0.1 stack.27.where
  0.7 4.8 %prep.1 = (bf16[256,4608]{1,0:T(8,128)(2,1)S(1)}, bf16[256,4096]{1,0:T(8,128)(2,1)S(1)}, bf16[256,512]{1,0:T(8,128)(2,1)S(1)}, f32[256,128]{1,0:T(8,128)S(1)}, b...) custom-call(s32[6]{0:T(128)S(1)} %stack.27.where, bf16[256,8192]{1,0:T(8,128)(2,1)} %tokens.3, ...), custom_call_target="tpu_custom_call" | custom-call | flops 1 | bytes 1 | tf_op jit(solution)/shard_map/prep/pallas_call | solution.py:300
  5.5 0.1 collective-permute-start
  5.6 2.3 %collective-permute-start.1 = (bf16[256,512]{1,0:T(8,128)(2,1)S(1)}, bf16[256,512]{1,0:T(8,128)(2,1)S(1)}, u32[]{:S(2)}, u32[]{:S(2)}) collective-permute-start(bf16[256,512]{1,0:T(8,128)(2,1)S(1)} %get-tuple-element.39.weight.refs_0_), channel_id=1, source_target_pairs={{0,2},{1,9},{2,4},{3,11},{4,6},{5,13},{6,0},{7,15},{8,10},{9,1},{1... | collective-permute-start | bytes 786440 | tf_op jit(solution)/shard_map/ppermute | solution.py:27
  7.9 0.7 collective-permute-start.2
  8.6 0.3 collective-permute-start.3
  8.9 1.3 %collective-permute-done.tok_far = bf16[256,4608]{1,0:T(8,128)(2,1)S(1)} collective-permute-done((bf16[256,4608]{1,0:T(8,128)(2,1)S(1)}, bf16[256,4608]{1,0:T(8,128)(2,1)S(1)}, u32[]{:S(2)}, u32[]{:S(2)}) %collective-permute-start) | collective-permute-done | bytes 2359328 | tf_op jit(solution)/shard_map/ppermute | solution.py:27
  10.1 3.0 %partial.1 = (bf16[512,1024]{1,0:T(8,128)(2,1)S(1)}, bf16[512,1024]{1,0:T(8,128)(2,1)S(1)}, bf16[512,1024]{1,0:T(8,128)(2,1)S(1)}, bf16[512,1024]{1,0:T(8,128)(2,1)S(1)}, f32[8,128]{1,0:T(8,128)S(1)}) custom-call(s32[6]{0:T(128)S(1)} %stack.27.where, bf16[256,4096]{1,0:T(8,128)(2,1)S(1)} %get-tuple-element.36.tok_own, ...), custom_call_target="tpu_custom_call" | custom-call | flops 1 | bytes 1 | tf_op jit(solution)/shard_map/partial/pallas_call | solution.py:329
  13.1 3.0 %collective-permute-done.1.near_1 = bf16[256,512]{1,0:T(8,128)(2,1)S(1)} collective-permute-done((bf16[256,512]{1,0:T(8,128)(2,1)S(1)}, bf16[256,512]{1,0:T(8,128)(2,1)S(1)}, u32[]{:S(2)}, u32[]{:S(2)}) %collective-permute-start.1) | collective-permute-done | bytes 262176 | tf_op jit(solution)/shard_map/ppermute | solution.py:27
  16.1 2.4 %collective-permute-done.2.near_2 = bf16[256,512]{1,0:T(8,128)(2,1)S(1)} collective-permute-done((bf16[256,512]{1,0:T(8,128)(2,1)S(1)}, bf16[256,512]{1,0:T(8,128)(2,1)S(1)}, u32[]{:S(2)}, u32[]{:S(2)}) %collective-permute-start.2) | collective-permute-done | bytes 262176 | tf_op jit(solution)/shard_map/ppermute | solution.py:27
  18.5 2.4 %collective-permute-done.3.near_3 = bf16[256,512]{1,0:T(8,128)(2,1)S(1)} collective-permute-done((bf16[256,512]{1,0:T(8,128)(2,1)S(1)}, bf16[256,512]{1,0:T(8,128)(2,1)S(1)}, u32[]{:S(2)}, u32[]{:S(2)}) %collective-permute-start.3) | collective-permute-done | bytes 262176 | tf_op jit(solution)/shard_map/ppermute | solution.py:27
  20.9 0.7 pick.1
  21.6 2.1 %collective-permute-start.5 = (bf16[512,512]{1,0:T(8,128)(2,1)S(1)}, bf16[512,512]{1,0:T(8,128)(2,1)S(1)}, u32[]{:S(2)}, u32[]{:S(2)}) collective-permute-start(bf16[512,512]{1,0:T(8,128)(2,1)S(1)} %get-tuple-element.44), channel_id=1, source_target_pairs={{0,8},{1,3},{2,10},{3,5},{4,12},{5,7},{6,14},{7,1},{8,0},{9,11},{1... | collective-permute-start | bytes 1572872 | tf_op jit(solution)/shard_map/ppermute | solution.py:27
  23.7 1.9 %collective-permute-start.4 = (bf16[768,512]{1,0:T(8,128)(2,1)S(1)}, bf16[768,512]{1,0:T(8,128)(2,1)S(1)}, u32[]{:S(2)}, u32[]{:S(2)}) collective-permute-start(bf16[768,512]{1,0:T(8,128)(2,1)S(1)} %get-tuple-element.42.refs_2_), channel_id=1, source_target_pairs={{0,32},{1,33},{2,34},{3,35},{4,36},{5,37},{6,38},{7,39},{8,40},{9,... | collective-permute-start | bytes 2359304 | tf_op jit(solution)/shard_map/ppermute | solution.py:27
  25.6 1.5 %collective-permute-start.10 = (bf16[512,1024]{1,0:T(8,128)(2,1)S(1)}, bf16[512,1024]{1,0:T(8,128)(2,1)S(1)}, u32[]{:S(2)}, u32[]{:S(2)}) collective-permute-start(bf16[512,1024]{1,0:T(8,128)(2,1)S(1)} %get-tuple-element.51), channel_id=1, source_target_pairs={{0,4},{1,9},{2,6},{3,11},{4,0},{5,13},{6,2},{7,15},{8,12},{9,1},{1... | collective-permute-start | bytes 3145736 | tf_op jit(solution)/shard_map/ppermute | solution.py:27
  27.1 3.2 %collective-permute-start.9 = (bf16[512,1024]{1,0:T(8,128)(2,1)S(1)}, bf16[512,1024]{1,0:T(8,128)(2,1)S(1)}, u32[]{:S(2)}, u32[]{:S(2)}) collective-permute-start(bf16[512,1024]{1,0:T(8,128)(2,1)S(1)} %get-tuple-element.50), channel_id=1, source_target_pairs={{0,2},{1,17},{2,4},{3,19},{4,6},{5,21},{6,0},{7,23},{8,10},{9,25},... | collective-permute-start | bytes 3145736 | tf_op jit(solution)/shard_map/ppermute | solution.py:27
  30.3 5.9 %collective-permute-done.5.refs_0_ = bf16[512,512]{1,0:T(8,128)(2,1)S(1)} collective-permute-done((bf16[512,512]{1,0:T(8,128)(2,1)S(1)}, bf16[512,512]{1,0:T(8,128)(2,1)S(1)}, u32[]{:S(2)}, u32[]{:S(2)}) %collective-permute-start.5) | collective-permute-done | bytes 524320 | tf_op jit(solution)/shard_map/ppermute | solution.py:27
  36.3 3.3 %collective-permute-start.6 = (bf16[512,512]{1,0:T(8,128)(2,1)S(1)}, bf16[512,512]{1,0:T(8,128)(2,1)S(1)}, u32[]{:S(2)}, u32[]{:S(2)}) collective-permute-start(bf16[512,512]{1,0:T(8,128)(2,1)S(1)} %get-tuple-element.45), channel_id=1, source_target_pairs={{0,8},{1,7},{2,10},{3,1},{4,12},{5,3},{6,14},{7,5},{8,0},{9,15},{1... | collective-permute-start | bytes 1572872 | tf_op jit(solution)/shard_map/ppermute | solution.py:27
  39.6 6.7 %collective-permute-done.4.refs_3_ = bf16[768,512]{1,0:T(8,128)(2,1)S(1)} collective-permute-done((bf16[768,512]{1,0:T(8,128)(2,1)S(1)}, bf16[768,512]{1,0:T(8,128)(2,1)S(1)}, u32[]{:S(2)}, u32[]{:S(2)}) %collective-permute-start.4) | collective-permute-done | bytes 786464 | tf_op jit(solution)/shard_map/ppermute | solution.py:27
  46.4 0.0 collective-permute-start.7
  46.4 3.8 %project.2 = (f32[256,512]{1,0:T(8,128)S(1)}, f32[256,512]{1,0:T(8,128)S(1)}, bf16[256,2048]{1,0:T(8,128)(2,1)S(1)}, bf16[256,2048]{1,0:T(8,128)(2,1)}, f32[8,128]{1,0:T(8,128)S(1)}) custom-call(s32[6]{0:T(128)S(1)} %stack.27.where, bf16[256,4096]{1,0:T(8,128)(2,1)S(1)} %get-tuple-element.36.tok_own, bf16[256,4608]{1,0:T(8,128)(2,1)S(1)} %collective-permute-done.tok_far, ...), custom_call_target="tpu_custom_call" | custom-call | flops 1 | bytes 1 | tf_op jit(solution)/shard_map/project/pallas_call | solution.py:353
  50.2 2.4 %collective-permute-done.6.source.refs_1_ = bf16[512,512]{1,0:T(8,128)(2,1)S(1)} collective-permute-done((bf16[512,512]{1,0:T(8,128)(2,1)S(1)}, bf16[512,512]{1,0:T(8,128)(2,1)S(1)}, u32[]{:S(2)}, u32[]{:S(2)}) %collective-permute-start.6) | collective-permute-done | bytes 524320 | tf_op jit(solution)/shard_map/ppermute | solution.py:27
  52.6 0.6 relay.1
  53.2 6.3 %collective-permute-start.8 = (bf16[512,512]{1,0:T(8,128)(2,1)S(1)}, bf16[512,512]{1,0:T(8,128)(2,1)S(1)}, u32[]{:S(2)}, u32[]{:S(2)}) collective-permute-start(bf16[512,512]{1,0:T(8,128)(2,1)S(1)} %relay.1), channel_id=1, source_target_pairs={{0,224},{1,225},{2,226},{3,227},{4,228},{5,229},{6,230},{7,231},{8... | collective-permute-start | bytes 1572872 | tf_op jit(solution)/shard_map/ppermute | solution.py:27
  59.6 0.0 collective-permute-done.11.refs_3_
  59.6 0.0 collective-permute-done.9.refs_1_
  59.6 1.1 %cut.1 = (bf16[256,512]{1,0:T(8,128)(2,1)S(1)}, bf16[256,512]{1,0:T(8,128)(2,1)S(1)}, bf16[256,512]{1,0:T(8,128)(2,1)S(1)}, bf16[256,512]{1,0:T(8,128)(2,1)S(1)}, f32[8,128]{1,0:T(8,128)S(1)}) custom-call(s32[6]{0:T(128)S(1)} %stack.27.where, bf16[512,1024]{1,0:T(8,128)(2,1)S(1)} %get-tuple-element.49.refs_0_, ...), custom_call_target="tpu_custom_call" | custom-call | flops 1 | bytes 1 | tf_op jit(solution)/shard_map/cut/pallas_call | solution.py:375
  60.6 1.5 %collective-permute-start.15 = (bf16[256,512]{1,0:T(8,128)(2,1)S(1)}, bf16[256,512]{1,0:T(8,128)(2,1)S(1)}, u32[]{:S(2)}, u32[]{:S(2)}) collective-permute-start(bf16[256,512]{1,0:T(8,128)(2,1)S(1)} %get-tuple-element.64), channel_id=1, source_target_pairs={{0,16},{1,3},{2,18},{3,5},{4,20},{5,7},{6,22},{7,1},{8,24},{9,11},... | collective-permute-start | bytes 786440 | tf_op jit(solution)/shard_map/ppermute | solution.py:27
  62.2 3.3 %collective-permute-start.16 = (bf16[256,512]{1,0:T(8,128)(2,1)S(1)}, bf16[256,512]{1,0:T(8,128)(2,1)S(1)}, u32[]{:S(2)}, u32[]{:S(2)}) collective-permute-start(bf16[256,512]{1,0:T(8,128)(2,1)S(1)} %get-tuple-element.65), channel_id=1, source_target_pairs={{0,8},{1,5},{2,10},{3,7},{4,12},{5,1},{6,14},{7,3},{8,0},{9,13},{1... | collective-permute-start | bytes 786440 | tf_op jit(solution)/shard_map/ppermute | solution.py:27
  65.4 1.4 %collective-permute-start.17 = (bf16[256,512]{1,0:T(8,128)(2,1)S(1)}, bf16[256,512]{1,0:T(8,128)(2,1)S(1)}, u32[]{:S(2)}, u32[]{:S(2)}) collective-permute-start(bf16[256,512]{1,0:T(8,128)(2,1)S(1)} %get-tuple-element.66), channel_id=1, source_target_pairs={{0,24},{1,7},{2,26},{3,1},{4,28},{5,3},{6,30},{7,5},{8,16},{9,15},... | collective-permute-start | bytes 786440 | tf_op jit(solution)/shard_map/ppermute | solution.py:27
  66.9 0.0 collective-permute-done.7.refs_2_
  66.9 0.0 collective-permute-start.12
  66.9 2.5 %collective-permute-done.8.refs_3_ = bf16[512,512]{1,0:T(8,128)(2,1)S(1)} collective-permute-done((bf16[512,512]{1,0:T(8,128)(2,1)S(1)}, bf16[512,512]{1,0:T(8,128)(2,1)S(1)}, u32[]{:S(2)}, u32[]{:S(2)}) %collective-permute-start.8) | collective-permute-done | bytes 524320 | tf_op jit(solution)/shard_map/ppermute | solution.py:27
  69.3 3.9 %project.3 = (f32[256,512]{1,0:T(8,128)S(1)}, f32[256,512]{1,0:T(8,128)}, bf16[256,2048]{1,0:T(8,128)(2,1)S(1)}, bf16[256,2048]{1,0:T(8,128)(2,1)}, f32[8,128]{1,0:T(8,128)S(1)}) custom-call(s32[6]{0:T(128)S(1)} %stack.27.where, bf16[256,4096]{1,0:T(8,128)(2,1)S(1)} %get-tuple-element.36.tok_own, bf16[256,4608]{1,0:T(8,128)(2,1)S(1)} %collective-permute-done.tok_far, ...), custom_call_target="tpu_custom_call" | custom-call | flops 1 | bytes 1 | tf_op jit(solution)/shard_map/project/pallas_call | solution.py:353
  73.3 0.0 collective-permute-start.13
  73.3 0.0 collective-permute-done.15.refs_1_
  73.3 0.5 collective-permute-start.14
  73.8 0.0 collective-permute-done.16.refs_2_
  73.8 0.0 collective-permute-done.17.refs_3_
  73.8 0.7 sum.1
  74.5 0.7 copy-done.2
  75.2 6.8 %all-to-all-start = ((bf16[8,32,512]{2,1,0:T(8,128)(2,1)}), bf16[8,32,512]{2,1,0:T(8,128)(2,1)S(1)}, u32[]{:S(2)}, u32[]{:S(2)}) async-start(bf16[8,32,512]{2,1,0:T(8,128)(2,1)} %bitcast.9), calls=%async_computation | async-start | bytes 524288 | tf_op jit(solution)/shard_map/all_to_all | solution.py:408
  81.9 0.0 collective-permute-done.14.refs_5_
  81.9 0.0 collective-permute-done.12.refs_2_
  82.0 1.0 %copy-done.1 = f32[256,512]{1,0:T(8,128)S(1)} copy-done((f32[256,512]{1,0:T(8,128)S(1)}, f32[256,512]{1,0:T(8,128)}, u32[]{:S(2)}) %copy-start.1) | copy-done | bytes 524312
  83.0 6.0 %finish.1 = (bf16[256,512]{1,0:T(8,128)(2,1)}, bf16[256,8192]{1,0:T(8,128)(2,1)}, f32[8,128]{1,0:T(8,128)S(1)}) custom-call(s32[6]{0:T(128)S(1)} %stack.27.where, bf16[256,8192]{1,0:T(8,128)(2,1)} %tokens.3, bf16[256,2048]{1,0:T(8,128)(2,1)S(1)} %get-tuple-element.43.refs_0_, bf16[256,2048]{1,0:T(8,128)(2,1)S(1)} %get-tuple-element.54.refs_1_, ...), custom_call_target="tpu_custom_call" | custom-call | flops 8388608 | bytes 13631488 | tf_op jit(solution)/shard_map/finish/pallas_call | solution.py:411
  89.0 5.1 %all-to-all-done.parts = bf16[8,32,512]{2,1,0:T(8,128)(2,1)S(1)} async-done(((bf16[8,32,512]{2,1,0:T(8,128)(2,1)}), bf16[8,32,512]{2,1,0:T(8,128)(2,1)S(1)}, u32[]{:S(2)}, u32[]{:S(2)}) %all-to-all-start) | async-done | bytes 262176 | tf_op jit(solution)/shard_map/all_to_all | solution.py:408
  94.1 1.2 %end.1 = f32[32,512]{1,0:T(8,128)} custom-call(s32[6]{0:T(128)S(1)} %stack.27.where, bf16[8,32,512]{2,1,0:T(8,128)(2,1)S(1)} %all-to-all-done.parts, f32[8,128]{1,0:T(8,128)S(1)} %get-tuple-element.68.after), custom_call_target="tpu_custom_call" | custom-call | flops 1 | bytes 1 | tf_op jit(solution)/shard_map/end/pallas_call | solution.py:437
  (7 shorter events, 0.0 us)
Async XLA Ops:
  5.5 4.6 %collective-permute-start = (bf16[256,4608]{1,0:T(8,128)(2,1)S(1)}, bf16[256,4608]{1,0:T(8,128)(2,1)S(1)}, u32[]{:S(2)}, u32[]{:S(2)}) collective-permute-start(bf16[256,4608]{1,0:T(8,128)(2,1)S(1)} %get-tuple-element.37), channel_id=1, source_target_pairs={{0,1},{1,0},{2,3},{3,2},{4,5},{5,4},{6,7},{7,6},{8,9},{9,8},{10,11... | collective-permute-start | bytes 7077896 | tf_op jit(solution)/shard_map/ppermute | solution.py:27
  5.6 10.5 %collective-permute-start.1 = (bf16[256,512]{1,0:T(8,128)(2,1)S(1)}, bf16[256,512]{1,0:T(8,128)(2,1)S(1)}, u32[]{:S(2)}, u32[]{:S(2)}) collective-permute-start(bf16[256,512]{1,0:T(8,128)(2,1)S(1)} %get-tuple-element.39.weight.refs_0_), channel_id=1, source_target_pairs={{0,2},{1,9},{2,4},{3,11},{4,6},{5,13},{6,0},{7,15},{8,10},{9,1},{1... | collective-permute-start | bytes 786440 | tf_op jit(solution)/shard_map/ppermute | solution.py:27
  7.9 10.6 %collective-permute-start.2 = (bf16[256,512]{1,0:T(8,128)(2,1)S(1)}, bf16[256,512]{1,0:T(8,128)(2,1)S(1)}, u32[]{:S(2)}, u32[]{:S(2)}) collective-permute-start(bf16[256,512]{1,0:T(8,128)(2,1)S(1)} %get-tuple-element.39.weight.refs_0_), channel_id=1, source_target_pairs={{0,4},{1,3},{2,6},{3,5},{4,0},{5,7},{6,2},{7,1},{8,12},{9,11},{10,... | collective-permute-start | bytes 786440 | tf_op jit(solution)/shard_map/ppermute | solution.py:27
  8.6 12.4 %collective-permute-start.3 = (bf16[256,512]{1,0:T(8,128)(2,1)S(1)}, bf16[256,512]{1,0:T(8,128)(2,1)S(1)}, u32[]{:S(2)}, u32[]{:S(2)}) collective-permute-start(bf16[256,512]{1,0:T(8,128)(2,1)S(1)} %get-tuple-element.39.weight.refs_0_), channel_id=1, source_target_pairs={{0,6},{1,15},{2,0},{3,9},{4,2},{5,11},{6,4},{7,13},{8,14},{9,7},{1... | collective-permute-start | bytes 786440 | tf_op jit(solution)/shard_map/ppermute | solution.py:27
  21.6 14.7 %collective-permute-start.5 = (bf16[512,512]{1,0:T(8,128)(2,1)S(1)}, bf16[512,512]{1,0:T(8,128)(2,1)S(1)}, u32[]{:S(2)}, u32[]{:S(2)}) collective-permute-start(bf16[512,512]{1,0:T(8,128)(2,1)S(1)} %get-tuple-element.44), channel_id=1, source_target_pairs={{0,8},{1,3},{2,10},{3,5},{4,12},{5,7},{6,14},{7,1},{8,0},{9,11},{1... | collective-permute-start | bytes 1572872 | tf_op jit(solution)/shard_map/ppermute | solution.py:27
  23.7 22.6 %collective-permute-start.4 = (bf16[768,512]{1,0:T(8,128)(2,1)S(1)}, bf16[768,512]{1,0:T(8,128)(2,1)S(1)}, u32[]{:S(2)}, u32[]{:S(2)}) collective-permute-start(bf16[768,512]{1,0:T(8,128)(2,1)S(1)} %get-tuple-element.42.refs_2_), channel_id=1, source_target_pairs={{0,32},{1,33},{2,34},{3,35},{4,36},{5,37},{6,38},{7,39},{8,40},{9,... | collective-permute-start | bytes 2359304 | tf_op jit(solution)/shard_map/ppermute | solution.py:27
  25.6 33.9 %collective-permute-start.10 = (bf16[512,1024]{1,0:T(8,128)(2,1)S(1)}, bf16[512,1024]{1,0:T(8,128)(2,1)S(1)}, u32[]{:S(2)}, u32[]{:S(2)}) collective-permute-start(bf16[512,1024]{1,0:T(8,128)(2,1)S(1)} %get-tuple-element.51), channel_id=1, source_target_pairs={{0,4},{1,9},{2,6},{3,11},{4,0},{5,13},{6,2},{7,15},{8,12},{9,1},{1... | collective-permute-start | bytes 3145736 | tf_op jit(solution)/shard_map/ppermute | solution.py:27
  27.1 32.5 %collective-permute-start.11 = (bf16[512,1024]{1,0:T(8,128)(2,1)S(1)}, bf16[512,1024]{1,0:T(8,128)(2,1)S(1)}, u32[]{:S(2)}, u32[]{:S(2)}) collective-permute-start(bf16[512,1024]{1,0:T(8,128)(2,1)S(1)} %get-tuple-element.52), channel_id=1, source_target_pairs={{0,6},{1,25},{2,0},{3,27},{4,2},{5,29},{6,4},{7,31},{8,14},{9,17},... | collective-permute-start | bytes 3145736 | tf_op jit(solution)/shard_map/ppermute | solution.py:27
  27.1 32.5 %collective-permute-start.9 = (bf16[512,1024]{1,0:T(8,128)(2,1)S(1)}, bf16[512,1024]{1,0:T(8,128)(2,1)S(1)}, u32[]{:S(2)}, u32[]{:S(2)}) collective-permute-start(bf16[512,1024]{1,0:T(8,128)(2,1)S(1)} %get-tuple-element.50), channel_id=1, source_target_pairs={{0,2},{1,17},{2,4},{3,19},{4,6},{5,21},{6,0},{7,23},{8,10},{9,25},... | collective-permute-start | bytes 3145736 | tf_op jit(solution)/shard_map/ppermute | solution.py:27
  36.3 16.4 %collective-permute-start.6 = (bf16[512,512]{1,0:T(8,128)(2,1)S(1)}, bf16[512,512]{1,0:T(8,128)(2,1)S(1)}, u32[]{:S(2)}, u32[]{:S(2)}) collective-permute-start(bf16[512,512]{1,0:T(8,128)(2,1)S(1)} %get-tuple-element.45), channel_id=1, source_target_pairs={{0,8},{1,7},{2,10},{3,1},{4,12},{5,3},{6,14},{7,5},{8,0},{9,15},{1... | collective-permute-start | bytes 1572872 | tf_op jit(solution)/shard_map/ppermute | solution.py:27
  46.4 20.5 %collective-permute-start.7 = (bf16[512,512]{1,0:T(8,128)(2,1)S(1)}, bf16[512,512]{1,0:T(8,128)(2,1)S(1)}, u32[]{:S(2)}, u32[]{:S(2)}) collective-permute-start(bf16[512,512]{1,0:T(8,128)(2,1)S(1)} %collective-permute-done.5.refs_0_), channel_id=1, source_target_pairs={{0,32},{1,33},{2,34},{3,35},{4,36},{5,37},{6,38},{7,39},{8,40},{9,... | collective-permute-start | bytes 1572872 | tf_op jit(solution)/shard_map/ppermute | solution.py:27
  53.2 16.1 %collective-permute-start.8 = (bf16[512,512]{1,0:T(8,128)(2,1)S(1)}, bf16[512,512]{1,0:T(8,128)(2,1)S(1)}, u32[]{:S(2)}, u32[]{:S(2)}) collective-permute-start(bf16[512,512]{1,0:T(8,128)(2,1)S(1)} %relay.1), channel_id=1, source_target_pairs={{0,224},{1,225},{2,226},{3,227},{4,228},{5,229},{6,230},{7,231},{8... | collective-permute-start | bytes 1572872 | tf_op jit(solution)/shard_map/ppermute | solution.py:27
  60.6 12.6 %collective-permute-start.15 = (bf16[256,512]{1,0:T(8,128)(2,1)S(1)}, bf16[256,512]{1,0:T(8,128)(2,1)S(1)}, u32[]{:S(2)}, u32[]{:S(2)}) collective-permute-start(bf16[256,512]{1,0:T(8,128)(2,1)S(1)} %get-tuple-element.64), channel_id=1, source_target_pairs={{0,16},{1,3},{2,18},{3,5},{4,20},{5,7},{6,22},{7,1},{8,24},{9,11},... | collective-permute-start | bytes 786440 | tf_op jit(solution)/shard_map/ppermute | solution.py:27
  62.2 11.6 %collective-permute-start.16 = (bf16[256,512]{1,0:T(8,128)(2,1)S(1)}, bf16[256,512]{1,0:T(8,128)(2,1)S(1)}, u32[]{:S(2)}, u32[]{:S(2)}) collective-permute-start(bf16[256,512]{1,0:T(8,128)(2,1)S(1)} %get-tuple-element.65), channel_id=1, source_target_pairs={{0,8},{1,5},{2,10},{3,7},{4,12},{5,1},{6,14},{7,3},{8,0},{9,13},{1... | collective-permute-start | bytes 786440 | tf_op jit(solution)/shard_map/ppermute | solution.py:27
  65.4 8.4 %collective-permute-start.17 = (bf16[256,512]{1,0:T(8,128)(2,1)S(1)}, bf16[256,512]{1,0:T(8,128)(2,1)S(1)}, u32[]{:S(2)}, u32[]{:S(2)}) collective-permute-start(bf16[256,512]{1,0:T(8,128)(2,1)S(1)} %get-tuple-element.66), channel_id=1, source_target_pairs={{0,24},{1,7},{2,26},{3,1},{4,28},{5,3},{6,30},{7,5},{8,16},{9,15},... | collective-permute-start | bytes 786440 | tf_op jit(solution)/shard_map/ppermute | solution.py:27
  66.9 15.1 %collective-permute-start.12 = (bf16[256,2048]{1,0:T(8,128)(2,1)}, bf16[256,2048]{1,0:T(8,128)(2,1)S(1)}, u32[]{:S(2)}, u32[]{:S(2)}) collective-permute-start(bf16[256,2048]{1,0:T(8,128)(2,1)} %get-tuple-element.55), channel_id=1, source_target_pairs={{0,1},{1,0},{2,3},{3,2},{4,5},{5,4},{6,7},{7,6},{8,9},{9,8},{10,11... | collective-permute-start | bytes 3145736 | tf_op jit(solution)/shard_map/ppermute | solution.py:27
  73.3 1.2 %copy-start = (f32[256,512]{1,0:T(8,128)}, f32[256,512]{1,0:T(8,128)S(1)}, u32[]{:S(2)}) copy-start(f32[256,512]{1,0:T(8,128)S(1)} %get-tuple-element.57.refs_4_) | copy-start | bytes 1572868
  73.3 8.7 %collective-permute-start.13 = (bf16[256,2048]{1,0:T(8,128)(2,1)}, bf16[256,2048]{1,0:T(8,128)(2,1)}, u32[]{:S(2)}, u32[]{:S(2)}) collective-permute-start(bf16[256,2048]{1,0:T(8,128)(2,1)} %get-tuple-element.56), channel_id=1, source_target_pairs={{0,1},{1,0},{2,3},{3,2},{4,5},{5,4},{6,7},{7,6},{8,9},{9,8},{10,11... | collective-permute-start | bytes 3145736 | tf_op jit(solution)/shard_map/ppermute | solution.py:27
  73.3 8.7 %collective-permute-start.14 = (f32[256,512]{1,0:T(8,128)}, f32[256,512]{1,0:T(8,128)}, u32[]{:S(2)}, u32[]{:S(2)}) collective-permute-start(f32[256,512]{1,0:T(8,128)} %get-tuple-element.58), channel_id=1, source_target_pairs={{0,1},{1,0},{2,3},{3,2},{4,5},{5,4},{6,7},{7,6},{8,9},{9,8},{10,11... | collective-permute-start | bytes 1572872 | tf_op jit(solution)/shard_map/ppermute | solution.py:27
  74.5 0.7 copy-start.2
  75.2 18.9 %all-to-all-start = ((bf16[8,32,512]{2,1,0:T(8,128)(2,1)}), bf16[8,32,512]{2,1,0:T(8,128)(2,1)S(1)}, u32[]{:S(2)}, u32[]{:S(2)}) async-start(bf16[8,32,512]{2,1,0:T(8,128)(2,1)} %bitcast.9), calls=%async_computation | async-start | bytes 524288 | tf_op jit(solution)/shard_map/all_to_all | solution.py:408
  82.0 1.0 %copy-start.1 = (f32[256,512]{1,0:T(8,128)S(1)}, f32[256,512]{1,0:T(8,128)}, u32[]{:S(2)}) copy-start(f32[256,512]{1,0:T(8,128)} %copy-done) | copy-start | bytes 1572868

commit v6 on v5

--- a/solution.py
+++ b/solution.py
@@ -235,8 +235,9 @@
         send_2[:HALF, :] = weight[...]
 
 
-def relay_kernel(where, source, after, out):
-    out[...] = source[...]
+def relay_kernel(where, source, after, out_1, out_2):
+    out_1[...] = source[:HALF, :]
+    out_2[...] = source[HALF:, :]
 
 
 def project_kernel(first, where, tok_own, tok_far, kg_own, *refs):
@@ -246,9 +247,9 @@
         key_own[...] = jnp.zeros_like(key_own)
         key_far[...] = jnp.zeros_like(key_far)
     else:
-        key_own[...] = refs[4][...]
-        key_far[...] = refs[5][...]
-    pieces = [ref.at[row : row + HALF, :] for ref in refs[:4] for row in range(0, ref.shape[0], HALF)]
+        key_own[...] = refs[5][...]
+        key_far[...] = refs[6][...]
+    pieces = [ref.at[row : row + HALF, :] for ref in refs[: 5 if first else 4] for row in range(0, ref.shape[0], HALF)]
     if first == 0:
         pieces = [pieces[index] for index in (0, 2, 3, 4, 1, 5, 6, 7)]
     for index, piece in enumerate(pieces):
@@ -363,11 +364,11 @@
     key_1, key_far_1, grad_1, grad_far_1, early_mark = project(
         0, keep, tok_far, kg, weight, weight_other, near_rows, along_z(near_rows, 1)
     )
-    relayed = call(
+    relayed_1, relayed_2 = call(
         relay_kernel,
         "relay",
-        arr((512, 512)),
-        dict(in_specs=[smem(), vmem(), anywhere()], out_specs=vmem()),
+        [arr((HALF, 512))] * 2,
+        flat(1, 2, 1),
         8,
         2**18,
         2**20,
@@ -389,7 +390,8 @@
         got_1,
         got_2,
         along_z(got_1, 1),
-        along_z(relayed, -1),
+        along_z(relayed_1, 1),
+        along_z(relayed_2, -1),
         key_1,
         key_far_1,
         cut_mark,

time: 95.6 us -> 98.2 us (1.027)
  the two profiles are of different devices: /device:TPU:6 before, /device:TPU:1 now
where the time goes in v6:
time: 98.2 us; the launch traced here: 97.8 us
  waiting for transfers between devices  34.9 us (36%)
  starting transfers between devices  34.6 us (35%)
  Pallas kernels  25.7 us (26%)
  local copies, waits for them, and re-layouts  1.8 us (2%)
    ppermute x19, waiting for transfers between devices, permute(): return lax.ppermute(array, AXES, pairs)  29.7 us
    ppermute x19, starting transfers between devices, permute(): return lax.ppermute(array, AXES, pairs)  29.5 us
    pallas_call x2, Pallas kernels, project(): call(functools.partial(project_kernel, first), 'project', [arr((256, 512)...  7.74 us
    pallas_call x1, Pallas kernels, on_device(): call(finish_kernel, 'finish', [arr((256, 512)), arr((256, 8192)), MARK],...  6 us
    all_to_all x1, waiting for transfers between devices, on_device(): lax.all_to_all(plane.reshape(NZ, 32, BLK), 'z', split_axis=0, concat_axis...  5.29 us
    all_to_all x1, starting transfers between devices, on_device(): lax.all_to_all(plane.reshape(NZ, 32, BLK), 'z', split_axis=0, concat_axis...  5.1 us
    pallas_call x1, Pallas kernels, on_device(): call(prep_kernel, 'prep', [arr((256, 4608)), arr((256, 4096)), arr((256,...  4.78 us
    pallas_call x1, Pallas kernels, on_device(): call(functools.partial(partial_kernel, range(4)), 'partial', [arr((512, 1...  2.98 us
  transfers between devices with their start and end apart: 20, of which 8 were waited for; matrix products, arithmetic and copies ran while one was open for 0% of the time, Pallas kernels for 19%

profile of v6, /device:TPU:1, one launch (start us, length us, event | category | flops | bytes accessed | tf_op | source)
XLA Modules:
  0.0 97.8 jit_solution(5164557359556554039)
XLA Ops:
  0.6 0.1 stack.27.where
  0.7 4.8 %prep.1 = (bf16[256,4608]{1,0:T(8,128)(2,1)S(1)}, bf16[256,4096]{1,0:T(8,128)(2,1)S(1)}, bf16[256,512]{1,0:T(8,128)(2,1)S(1)}, f32[256,128]{1,0:T(8,128)S(1)}, b...) custom-call(s32[6]{0:T(128)S(1)} %stack.27.where, bf16[256,8192]{1,0:T(8,128)(2,1)} %tokens.3, ...), custom_call_target="tpu_custom_call" | custom-call | flops 1 | bytes 1 | tf_op jit(solution)/shard_map/prep/pallas_call | solution.py:301
  5.5 3.3 %collective-permute-start = (bf16[256,4608]{1,0:T(8,128)(2,1)S(1)}, bf16[256,4608]{1,0:T(8,128)(2,1)S(1)}, u32[]{:S(2)}, u32[]{:S(2)}) collective-permute-start(bf16[256,4608]{1,0:T(8,128)(2,1)S(1)} %get-tuple-element.39), channel_id=1, source_target_pairs={{0,1},{1,0},{2,3},{3,2},{4,5},{5,4},{6,7},{7,6},{8,9},{9,8},{10,11... | collective-permute-start | bytes 7077896 | tf_op jit(solution)/shard_map/ppermute | solution.py:27
  8.8 1.2 %collective-permute-start.1 = (bf16[256,512]{1,0:T(8,128)(2,1)S(1)}, bf16[256,512]{1,0:T(8,128)(2,1)S(1)}, u32[]{:S(2)}, u32[]{:S(2)}) collective-permute-start(bf16[256,512]{1,0:T(8,128)(2,1)S(1)} %get-tuple-element.41.weight.refs_0_), channel_id=1, source_target_pairs={{0,2},{1,9},{2,4},{3,11},{4,6},{5,13},{6,0},{7,15},{8,10},{9,1},{1... | collective-permute-start | bytes 786440 | tf_op jit(solution)/shard_map/ppermute | solution.py:27
  10.0 1.2 %collective-permute-start.2 = (bf16[256,512]{1,0:T(8,128)(2,1)S(1)}, bf16[256,512]{1,0:T(8,128)(2,1)S(1)}, u32[]{:S(2)}, u32[]{:S(2)}) collective-permute-start(bf16[256,512]{1,0:T(8,128)(2,1)S(1)} %get-tuple-element.41.weight.refs_0_), channel_id=1, source_target_pairs={{0,4},{1,3},{2,6},{3,5},{4,0},{5,7},{6,2},{7,1},{8,12},{9,11},{10,... | collective-permute-start | bytes 786440 | tf_op jit(solution)/shard_map/ppermute | solution.py:27
  11.2 3.0 %collective-permute-start.3 = (bf16[256,512]{1,0:T(8,128)(2,1)S(1)}, bf16[256,512]{1,0:T(8,128)(2,1)S(1)}, u32[]{:S(2)}, u32[]{:S(2)}) collective-permute-start(bf16[256,512]{1,0:T(8,128)(2,1)S(1)} %get-tuple-element.41.weight.refs_0_), channel_id=1, source_target_pairs={{0,6},{1,15},{2,0},{3,9},{4,2},{5,11},{6,4},{7,13},{8,14},{9,7},{1... | collective-permute-start | bytes 786440 | tf_op jit(solution)/shard_map/ppermute | solution.py:27
  14.2 0.0 collective-permute-done.tok_far
  14.2 3.0 %partial.1 = (bf16[512,1024]{1,0:T(8,128)(2,1)S(1)}, bf16[512,1024]{1,0:T(8,128)(2,1)S(1)}, bf16[512,1024]{1,0:T(8,128)(2,1)S(1)}, bf16[512,1024]{1,0:T(8,128)(2,1)S(1)}, f32[8,128]{1,0:T(8,128)S(1)}) custom-call(s32[6]{0:T(128)S(1)} %stack.27.where, bf16[256,4096]{1,0:T(8,128)(2,1)S(1)} %get-tuple-element.38.tok_own, ...), custom_call_target="tpu_custom_call" | custom-call | flops 1 | bytes 1 | tf_op jit(solution)/shard_map/partial/pallas_call | solution.py:330
  17.2 4.2 %collective-permute-done.2.near_2 = bf16[256,512]{1,0:T(8,128)(2,1)S(1)} collective-permute-done((bf16[256,512]{1,0:T(8,128)(2,1)S(1)}, bf16[256,512]{1,0:T(8,128)(2,1)S(1)}, u32[]{:S(2)}, u32[]{:S(2)}) %collective-permute-start.2) | collective-permute-done | bytes 262176 | tf_op jit(solution)/shard_map/ppermute | solution.py:27
  21.4 0.3 collective-permute-done.3.near_3
  21.7 0.7 pick.1
  22.4 3.3 %collective-permute-start.5 = (bf16[512,512]{1,0:T(8,128)(2,1)S(1)}, bf16[512,512]{1,0:T(8,128)(2,1)S(1)}, u32[]{:S(2)}, u32[]{:S(2)}) collective-permute-start(bf16[512,512]{1,0:T(8,128)(2,1)S(1)} %get-tuple-element.46), channel_id=1, source_target_pairs={{0,8},{1,3},{2,10},{3,5},{4,12},{5,7},{6,14},{7,1},{8,0},{9,11},{1... | collective-permute-start | bytes 1572872 | tf_op jit(solution)/shard_map/ppermute | solution.py:27
  25.7 0.4 collective-permute-start.10
  26.1 1.6 %collective-permute-start.4 = (bf16[768,512]{1,0:T(8,128)(2,1)S(1)}, bf16[768,512]{1,0:T(8,128)(2,1)S(1)}, u32[]{:S(2)}, u32[]{:S(2)}) collective-permute-start(bf16[768,512]{1,0:T(8,128)(2,1)S(1)} %get-tuple-element.44.refs_2_), channel_id=1, source_target_pairs={{0,32},{1,33},{2,34},{3,35},{4,36},{5,37},{6,38},{7,39},{8,40},{9,... | collective-permute-start | bytes 2359304 | tf_op jit(solution)/shard_map/ppermute | solution.py:27
  27.7 1.6 %collective-permute-start.11 = (bf16[512,1024]{1,0:T(8,128)(2,1)S(1)}, bf16[512,1024]{1,0:T(8,128)(2,1)S(1)}, u32[]{:S(2)}, u32[]{:S(2)}) collective-permute-start(bf16[512,1024]{1,0:T(8,128)(2,1)S(1)} %get-tuple-element.55), channel_id=1, source_target_pairs={{0,4},{1,9},{2,6},{3,11},{4,0},{5,13},{6,2},{7,15},{8,12},{9,1},{1... | collective-permute-start | bytes 3145736 | tf_op jit(solution)/shard_map/ppermute | solution.py:27
  29.3 0.8 collective-permute-start.12
  30.1 6.3 %collective-permute-done.5.refs_0_ = bf16[512,512]{1,0:T(8,128)(2,1)S(1)} collective-permute-done((bf16[512,512]{1,0:T(8,128)(2,1)S(1)}, bf16[512,512]{1,0:T(8,128)(2,1)S(1)}, u32[]{:S(2)}, u32[]{:S(2)}) %collective-permute-start.5) | collective-permute-done | bytes 524320 | tf_op jit(solution)/shard_map/ppermute | solution.py:27
  36.4 1.6 %collective-permute-start.6 = (bf16[512,512]{1,0:T(8,128)(2,1)S(1)}, bf16[512,512]{1,0:T(8,128)(2,1)S(1)}, u32[]{:S(2)}, u32[]{:S(2)}) collective-permute-start(bf16[512,512]{1,0:T(8,128)(2,1)S(1)} %get-tuple-element.47), channel_id=1, source_target_pairs={{0,8},{1,7},{2,10},{3,1},{4,12},{5,3},{6,14},{7,5},{8,0},{9,15},{1... | collective-permute-start | bytes 1572872 | tf_op jit(solution)/shard_map/ppermute | solution.py:27
  38.0 10.9 %collective-permute-done.4.refs_3_ = bf16[768,512]{1,0:T(8,128)(2,1)S(1)} collective-permute-done((bf16[768,512]{1,0:T(8,128)(2,1)S(1)}, bf16[768,512]{1,0:T(8,128)(2,1)S(1)}, u32[]{:S(2)}, u32[]{:S(2)}) %collective-permute-start.4) | collective-permute-done | bytes 786464 | tf_op jit(solution)/shard_map/ppermute | solution.py:27
  48.9 0.0 collective-permute-start.7
  48.9 3.8 %project.2 = (f32[256,512]{1,0:T(8,128)S(1)}, f32[256,512]{1,0:T(8,128)S(1)}, bf16[256,2048]{1,0:T(8,128)(2,1)S(1)}, bf16[256,2048]{1,0:T(8,128)(2,1)}, f32[8,128]{1,0:T(8,128)S(1)}) custom-call(s32[6]{0:T(128)S(1)} %stack.27.where, bf16[256,4096]{1,0:T(8,128)(2,1)S(1)} %get-tuple-element.38.tok_own, bf16[256,4608]{1,0:T(8,128)(2,1)S(1)} %collective-permute-done.tok_far, ...), custom_call_target="tpu_custom_call" | custom-call | flops 1 | bytes 1 | tf_op jit(solution)/shard_map/project/pallas_call | solution.py:354
  52.8 1.1 %collective-permute-done.6.source.refs_1_ = bf16[512,512]{1,0:T(8,128)(2,1)S(1)} collective-permute-done((bf16[512,512]{1,0:T(8,128)(2,1)S(1)}, bf16[512,512]{1,0:T(8,128)(2,1)S(1)}, u32[]{:S(2)}, u32[]{:S(2)}) %collective-permute-start.6) | collective-permute-done | bytes 524320 | tf_op jit(solution)/shard_map/ppermute | solution.py:27
  53.9 0.6 relay.1
  54.5 1.7 %collective-permute-start.8 = (bf16[256,512]{1,0:T(8,128)(2,1)S(1)}, bf16[256,512]{1,0:T(8,128)(2,1)S(1)}, u32[]{:S(2)}, u32[]{:S(2)}) collective-permute-start(bf16[256,512]{1,0:T(8,128)(2,1)S(1)} %get-tuple-element.49), channel_id=1, source_target_pairs={{0,32},{1,33},{2,34},{3,35},{4,36},{5,37},{6,38},{7,39},{8,40},{9,... | collective-permute-start | bytes 786440 | tf_op jit(solution)/shard_map/ppermute | solution.py:27
  56.2 6.3 %collective-permute-done.10.refs_1_ = bf16[512,1024]{1,0:T(8,128)(2,1)S(1)} collective-permute-done((bf16[512,1024]{1,0:T(8,128)(2,1)S(1)}, bf16[512,1024]{1,0:T(8,128)(2,1)S(1)}, u32[]{:S(2)}, u32[]{:S(2)}) %collective-permute-start.10) | collective-permute-done | bytes 1048608 | tf_op jit(solution)/shard_map/ppermute | solution.py:27
  62.5 3.9 %collective-permute-start.9 = (bf16[256,512]{1,0:T(8,128)(2,1)S(1)}, bf16[256,512]{1,0:T(8,128)(2,1)S(1)}, u32[]{:S(2)}, u32[]{:S(2)}) collective-permute-start(bf16[256,512]{1,0:T(8,128)(2,1)S(1)} %get-tuple-element.50), channel_id=1, source_target_pairs={{0,224},{1,225},{2,226},{3,227},{4,228},{5,229},{6,230},{7,231},{8... | collective-permute-start | bytes 786440 | tf_op jit(solution)/shard_map/ppermute | solution.py:27
  66.4 0.0 collective-permute-done.11.refs_2_
  66.4 0.0 collective-permute-done.12.refs_3_
  66.4 1.1 %cut.1 = (bf16[256,512]{1,0:T(8,128)(2,1)S(1)}, bf16[256,512]{1,0:T(8,128)(2,1)S(1)}, bf16[256,512]{1,0:T(8,128)(2,1)S(1)}, bf16[256,512]{1,0:T(8,128)(2,1)S(1)}, f32[8,128]{1,0:T(8,128)S(1)}) custom-call(s32[6]{0:T(128)S(1)} %stack.27.where, bf16[512,1024]{1,0:T(8,128)(2,1)S(1)} %get-tuple-element.53.refs_0_, ...), custom_call_target="tpu_custom_call" | custom-call | flops 1 | bytes 1 | tf_op jit(solution)/shard_map/cut/pallas_call | solution.py:376
  67.5 1.3 %collective-permute-start.16 = (bf16[256,512]{1,0:T(8,128)(2,1)S(1)}, bf16[256,512]{1,0:T(8,128)(2,1)S(1)}, u32[]{:S(2)}, u32[]{:S(2)}) collective-permute-start(bf16[256,512]{1,0:T(8,128)(2,1)S(1)} %get-tuple-element.68), channel_id=1, source_target_pairs={{0,16},{1,3},{2,18},{3,5},{4,20},{5,7},{6,22},{7,1},{8,24},{9,11},... | collective-permute-start | bytes 786440 | tf_op jit(solution)/shard_map/ppermute | solution.py:27
  68.8 2.4 %collective-permute-start.17 = (bf16[256,512]{1,0:T(8,128)(2,1)S(1)}, bf16[256,512]{1,0:T(8,128)(2,1)S(1)}, u32[]{:S(2)}, u32[]{:S(2)}) collective-permute-start(bf16[256,512]{1,0:T(8,128)(2,1)S(1)} %get-tuple-element.69), channel_id=1, source_target_pairs={{0,8},{1,5},{2,10},{3,7},{4,12},{5,1},{6,14},{7,3},{8,0},{9,13},{1... | collective-permute-start | bytes 786440 | tf_op jit(solution)/shard_map/ppermute | solution.py:27
  71.2 0.0 collective-permute-done.8.refs_3_
  71.2 1.2 %collective-permute-start.18 = (bf16[256,512]{1,0:T(8,128)(2,1)S(1)}, bf16[256,512]{1,0:T(8,128)(2,1)S(1)}, u32[]{:S(2)}, u32[]{:S(2)}) collective-permute-start(bf16[256,512]{1,0:T(8,128)(2,1)S(1)} %get-tuple-element.70), channel_id=1, source_target_pairs={{0,24},{1,7},{2,26},{3,1},{4,28},{5,3},{6,30},{7,5},{8,16},{9,15},... | collective-permute-start | bytes 786440 | tf_op jit(solution)/shard_map/ppermute | solution.py:27
  72.3 0.5 collective-permute-start.13
  72.9 3.9 %project.3 = (f32[256,512]{1,0:T(8,128)S(1)}, f32[256,512]{1,0:T(8,128)}, bf16[256,2048]{1,0:T(8,128)(2,1)S(1)}, bf16[256,2048]{1,0:T(8,128)(2,1)}, f32[8,128]{1,0:T(8,128)S(1)}) custom-call(s32[6]{0:T(128)S(1)} %stack.27.where, bf16[256,4096]{1,0:T(8,128)(2,1)S(1)} %get-tuple-element.38.tok_own, bf16[256,4608]{1,0:T(8,128)(2,1)S(1)} %collective-permute-done.tok_far, ...), custom_call_target="tpu_custom_call" | custom-call | flops 1 | bytes 1 | tf_op jit(solution)/shard_map/project/pallas_call | solution.py:354
  76.8 0.0 collective-permute-start.14
  76.8 0.0 collective-permute-done.16.refs_1_
  76.8 0.5 collective-permute-start.15
  77.3 0.5 collective-permute-done.17.refs_2_
  77.7 0.0 collective-permute-done.18.refs_3_
  77.7 0.7 sum.1
  78.5 0.7 copy-done.2
  79.1 5.1 %all-to-all-start = ((bf16[8,32,512]{2,1,0:T(8,128)(2,1)}), bf16[8,32,512]{2,1,0:T(8,128)(2,1)S(1)}, u32[]{:S(2)}, u32[]{:S(2)}) async-start(bf16[8,32,512]{2,1,0:T(8,128)(2,1)} %bitcast.9), calls=%async_computation | async-start | bytes 524288 | tf_op jit(solution)/shard_map/all_to_all | solution.py:410
  84.2 0.0 collective-permute-done.15.refs_5_
  84.3 1.0 %copy-done.1 = f32[256,512]{1,0:T(8,128)S(1)} copy-done((f32[256,512]{1,0:T(8,128)S(1)}, f32[256,512]{1,0:T(8,128)}, u32[]{:S(2)}) %copy-start.1) | copy-done | bytes 524312
  85.3 6.0 %finish.1 = (bf16[256,512]{1,0:T(8,128)(2,1)}, bf16[256,8192]{1,0:T(8,128)(2,1)}, f32[8,128]{1,0:T(8,128)S(1)}) custom-call(s32[6]{0:T(128)S(1)} %stack.27.where, bf16[256,8192]{1,0:T(8,128)(2,1)} %tokens.3, bf16[256,2048]{1,0:T(8,128)(2,1)S(1)} %get-tuple-element.45.refs_0_, bf16[256,2048]{1,0:T(8,128)(2,1)S(1)} %get-tuple-element.58.refs_1_, ...), custom_call_target="tpu_custom_call" | custom-call | flops 8388608 | bytes 13631488 | tf_op jit(solution)/shard_map/finish/pallas_call | solution.py:413
  91.3 5.3 %all-to-all-done.parts = bf16[8,32,512]{2,1,0:T(8,128)(2,1)S(1)} async-done(((bf16[8,32,512]{2,1,0:T(8,128)(2,1)}), bf16[8,32,512]{2,1,0:T(8,128)(2,1)S(1)}, u32[]{:S(2)}, u32[]{:S(2)}) %all-to-all-start) | async-done | bytes 262176 | tf_op jit(solution)/shard_map/all_to_all | solution.py:410
  96.6 1.2 %end.1 = f32[32,512]{1,0:T(8,128)} custom-call(s32[6]{0:T(128)S(1)} %stack.27.where, bf16[8,32,512]{2,1,0:T(8,128)(2,1)S(1)} %all-to-all-done.parts, f32[8,128]{1,0:T(8,128)S(1)} %get-tuple-element.72.after), custom_call_target="tpu_custom_call" | custom-call | flops 1 | bytes 1 | tf_op jit(solution)/shard_map/end/pallas_call | solution.py:439
  (9 shorter events, 0.0 us)
Async XLA Ops:
  5.5 8.7 %collective-permute-start = (bf16[256,4608]{1,0:T(8,128)(2,1)S(1)}, bf16[256,4608]{1,0:T(8,128)(2,1)S(1)}, u32[]{:S(2)}, u32[]{:S(2)}) collective-permute-start(bf16[256,4608]{1,0:T(8,128)(2,1)S(1)} %get-tuple-element.39), channel_id=1, source_target_pairs={{0,1},{1,0},{2,3},{3,2},{4,5},{5,4},{6,7},{7,6},{8,9},{9,8},{10,11... | collective-permute-start | bytes 7077896 | tf_op jit(solution)/shard_map/ppermute | solution.py:27
  8.8 8.4 %collective-permute-start.1 = (bf16[256,512]{1,0:T(8,128)(2,1)S(1)}, bf16[256,512]{1,0:T(8,128)(2,1)S(1)}, u32[]{:S(2)}, u32[]{:S(2)}) collective-permute-start(bf16[256,512]{1,0:T(8,128)(2,1)S(1)} %get-tuple-element.41.weight.refs_0_), channel_id=1, source_target_pairs={{0,2},{1,9},{2,4},{3,11},{4,6},{5,13},{6,0},{7,15},{8,10},{9,1},{1... | collective-permute-start | bytes 786440 | tf_op jit(solution)/shard_map/ppermute | solution.py:27
  10.0 11.4 %collective-permute-start.2 = (bf16[256,512]{1,0:T(8,128)(2,1)S(1)}, bf16[256,512]{1,0:T(8,128)(2,1)S(1)}, u32[]{:S(2)}, u32[]{:S(2)}) collective-permute-start(bf16[256,512]{1,0:T(8,128)(2,1)S(1)} %get-tuple-element.41.weight.refs_0_), channel_id=1, source_target_pairs={{0,4},{1,3},{2,6},{3,5},{4,0},{5,7},{6,2},{7,1},{8,12},{9,11},{10,... | collective-permute-start | bytes 786440 | tf_op jit(solution)/shard_map/ppermute | solution.py:27
  11.2 10.5 %collective-permute-start.3 = (bf16[256,512]{1,0:T(8,128)(2,1)S(1)}, bf16[256,512]{1,0:T(8,128)(2,1)S(1)}, u32[]{:S(2)}, u32[]{:S(2)}) collective-permute-start(bf16[256,512]{1,0:T(8,128)(2,1)S(1)} %get-tuple-element.41.weight.refs_0_), channel_id=1, source_target_pairs={{0,6},{1,15},{2,0},{3,9},{4,2},{5,11},{6,4},{7,13},{8,14},{9,7},{1... | collective-permute-start | bytes 786440 | tf_op jit(solution)/shard_map/ppermute | solution.py:27
  22.4 14.0 %collective-permute-start.5 = (bf16[512,512]{1,0:T(8,128)(2,1)S(1)}, bf16[512,512]{1,0:T(8,128)(2,1)S(1)}, u32[]{:S(2)}, u32[]{:S(2)}) collective-permute-start(bf16[512,512]{1,0:T(8,128)(2,1)S(1)} %get-tuple-element.46), channel_id=1, source_target_pairs={{0,8},{1,3},{2,10},{3,5},{4,12},{5,7},{6,14},{7,1},{8,0},{9,11},{1... | collective-permute-start | bytes 1572872 | tf_op jit(solution)/shard_map/ppermute | solution.py:27
  25.7 36.8 %collective-permute-start.10 = (bf16[512,1024]{1,0:T(8,128)(2,1)S(1)}, bf16[512,1024]{1,0:T(8,128)(2,1)S(1)}, u32[]{:S(2)}, u32[]{:S(2)}) collective-permute-start(bf16[512,1024]{1,0:T(8,128)(2,1)S(1)} %get-tuple-element.54), channel_id=1, source_target_pairs={{0,2},{1,17},{2,4},{3,19},{4,6},{5,21},{6,0},{7,23},{8,10},{9,25},... | collective-permute-start | bytes 3145736 | tf_op jit(solution)/shard_map/ppermute | solution.py:27
  26.1 22.8 %collective-permute-start.4 = (bf16[768,512]{1,0:T(8,128)(2,1)S(1)}, bf16[768,512]{1,0:T(8,128)(2,1)S(1)}, u32[]{:S(2)}, u32[]{:S(2)}) collective-permute-start(bf16[768,512]{1,0:T(8,128)(2,1)S(1)} %get-tuple-element.44.refs_2_), channel_id=1, source_target_pairs={{0,32},{1,33},{2,34},{3,35},{4,36},{5,37},{6,38},{7,39},{8,40},{9,... | collective-permute-start | bytes 2359304 | tf_op jit(solution)/shard_map/ppermute | solution.py:27
  27.7 38.7 %collective-permute-start.11 = (bf16[512,1024]{1,0:T(8,128)(2,1)S(1)}, bf16[512,1024]{1,0:T(8,128)(2,1)S(1)}, u32[]{:S(2)}, u32[]{:S(2)}) collective-permute-start(bf16[512,1024]{1,0:T(8,128)(2,1)S(1)} %get-tuple-element.55), channel_id=1, source_target_pairs={{0,4},{1,9},{2,6},{3,11},{4,0},{5,13},{6,2},{7,15},{8,12},{9,1},{1... | collective-permute-start | bytes 3145736 | tf_op jit(solution)/shard_map/ppermute | solution.py:27
  29.3 37.1 %collective-permute-start.12 = (bf16[512,1024]{1,0:T(8,128)(2,1)S(1)}, bf16[512,1024]{1,0:T(8,128)(2,1)S(1)}, u32[]{:S(2)}, u32[]{:S(2)}) collective-permute-start(bf16[512,1024]{1,0:T(8,128)(2,1)S(1)} %get-tuple-element.56), channel_id=1, source_target_pairs={{0,6},{1,25},{2,0},{3,27},{4,2},{5,29},{6,4},{7,31},{8,14},{9,17},... | collective-permute-start | bytes 3145736 | tf_op jit(solution)/shard_map/ppermute | solution.py:27
  36.4 17.5 %collective-permute-start.6 = (bf16[512,512]{1,0:T(8,128)(2,1)S(1)}, bf16[512,512]{1,0:T(8,128)(2,1)S(1)}, u32[]{:S(2)}, u32[]{:S(2)}) collective-permute-start(bf16[512,512]{1,0:T(8,128)(2,1)S(1)} %get-tuple-element.47), channel_id=1, source_target_pairs={{0,8},{1,7},{2,10},{3,1},{4,12},{5,3},{6,14},{7,5},{8,0},{9,15},{1... | collective-permute-start | bytes 1572872 | tf_op jit(solution)/shard_map/ppermute | solution.py:27
  48.9 23.9 %collective-permute-start.7 = (bf16[512,512]{1,0:T(8,128)(2,1)S(1)}, bf16[512,512]{1,0:T(8,128)(2,1)S(1)}, u32[]{:S(2)}, u32[]{:S(2)}) collective-permute-start(bf16[512,512]{1,0:T(8,128)(2,1)S(1)} %collective-permute-done.5.refs_0_), channel_id=1, source_target_pairs={{0,32},{1,33},{2,34},{3,35},{4,36},{5,37},{6,38},{7,39},{8,40},{9,... | collective-permute-start | bytes 1572872 | tf_op jit(solution)/shard_map/ppermute | solution.py:27
  54.5 16.7 %collective-permute-start.8 = (bf16[256,512]{1,0:T(8,128)(2,1)S(1)}, bf16[256,512]{1,0:T(8,128)(2,1)S(1)}, u32[]{:S(2)}, u32[]{:S(2)}) collective-permute-start(bf16[256,512]{1,0:T(8,128)(2,1)S(1)} %get-tuple-element.49), channel_id=1, source_target_pairs={{0,32},{1,33},{2,34},{3,35},{4,36},{5,37},{6,38},{7,39},{8,40},{9,... | collective-permute-start | bytes 786440 | tf_op jit(solution)/shard_map/ppermute | solution.py:27
  62.5 9.8 %collective-permute-start.9 = (bf16[256,512]{1,0:T(8,128)(2,1)S(1)}, bf16[256,512]{1,0:T(8,128)(2,1)S(1)}, u32[]{:S(2)}, u32[]{:S(2)}) collective-permute-start(bf16[256,512]{1,0:T(8,128)(2,1)S(1)} %get-tuple-element.50), channel_id=1, source_target_pairs={{0,224},{1,225},{2,226},{3,227},{4,228},{5,229},{6,230},{7,231},{8... | collective-permute-start | bytes 786440 | tf_op jit(solution)/shard_map/ppermute | solution.py:27
  67.5 9.3 %collective-permute-start.16 = (bf16[256,512]{1,0:T(8,128)(2,1)S(1)}, bf16[256,512]{1,0:T(8,128)(2,1)S(1)}, u32[]{:S(2)}, u32[]{:S(2)}) collective-permute-start(bf16[256,512]{1,0:T(8,128)(2,1)S(1)} %get-tuple-element.68), channel_id=1, source_target_pairs={{0,16},{1,3},{2,18},{3,5},{4,20},{5,7},{6,22},{7,1},{8,24},{9,11},... | collective-permute-start | bytes 786440 | tf_op jit(solution)/shard_map/ppermute | solution.py:27
  68.8 9.0 %collective-permute-start.17 = (bf16[256,512]{1,0:T(8,128)(2,1)S(1)}, bf16[256,512]{1,0:T(8,128)(2,1)S(1)}, u32[]{:S(2)}, u32[]{:S(2)}) collective-permute-start(bf16[256,512]{1,0:T(8,128)(2,1)S(1)} %get-tuple-element.69), channel_id=1, source_target_pairs={{0,8},{1,5},{2,10},{3,7},{4,12},{5,1},{6,14},{7,3},{8,0},{9,13},{1... | collective-permute-start | bytes 786440 | tf_op jit(solution)/shard_map/ppermute | solution.py:27
  71.2 6.6 %collective-permute-start.18 = (bf16[256,512]{1,0:T(8,128)(2,1)S(1)}, bf16[256,512]{1,0:T(8,128)(2,1)S(1)}, u32[]{:S(2)}, u32[]{:S(2)}) collective-permute-start(bf16[256,512]{1,0:T(8,128)(2,1)S(1)} %get-tuple-element.70), channel_id=1, source_target_pairs={{0,24},{1,7},{2,26},{3,1},{4,28},{5,3},{6,30},{7,5},{8,16},{9,15},... | collective-permute-start | bytes 786440 | tf_op jit(solution)/shard_map/ppermute | solution.py:27
  72.3 11.9 %collective-permute-start.13 = (bf16[256,2048]{1,0:T(8,128)(2,1)}, bf16[256,2048]{1,0:T(8,128)(2,1)S(1)}, u32[]{:S(2)}, u32[]{:S(2)}) collective-permute-start(bf16[256,2048]{1,0:T(8,128)(2,1)} %get-tuple-element.59), channel_id=1, source_target_pairs={{0,1},{1,0},{2,3},{3,2},{4,5},{5,4},{6,7},{7,6},{8,9},{9,8},{10,11... | collective-permute-start | bytes 3145736 | tf_op jit(solution)/shard_map/ppermute | solution.py:27
  76.7 1.7 %copy-start = (f32[256,512]{1,0:T(8,128)}, f32[256,512]{1,0:T(8,128)S(1)}, u32[]{:S(2)}) copy-start(f32[256,512]{1,0:T(8,128)S(1)} %get-tuple-element.61.refs_4_) | copy-start | bytes 1572868
  76.8 7.5 %collective-permute-start.14 = (bf16[256,2048]{1,0:T(8,128)(2,1)}, bf16[256,2048]{1,0:T(8,128)(2,1)}, u32[]{:S(2)}, u32[]{:S(2)}) collective-permute-start(bf16[256,2048]{1,0:T(8,128)(2,1)} %get-tuple-element.60), channel_id=1, source_target_pairs={{0,1},{1,0},{2,3},{3,2},{4,5},{5,4},{6,7},{7,6},{8,9},{9,8},{10,11... | collective-permute-start | bytes 3145736 | tf_op jit(solution)/shard_map/ppermute | solution.py:27
  76.8 7.5 %collective-permute-start.15 = (f32[256,512]{1,0:T(8,128)}, f32[256,512]{1,0:T(8,128)}, u32[]{:S(2)}, u32[]{:S(2)}) collective-permute-start(f32[256,512]{1,0:T(8,128)} %get-tuple-element.62), channel_id=1, source_target_pairs={{0,1},{1,0},{2,3},{3,2},{4,5},{5,4},{6,7},{7,6},{8,9},{9,8},{10,11... | collective-permute-start | bytes 1572872 | tf_op jit(solution)/shard_map/ppermute | solution.py:27
  78.5 0.7 copy-start.2
  79.1 17.5 %all-to-all-start = ((bf16[8,32,512]{2,1,0:T(8,128)(2,1)}), bf16[8,32,512]{2,1,0:T(8,128)(2,1)S(1)}, u32[]{:S(2)}, u32[]{:S(2)}) async-start(bf16[8,32,512]{2,1,0:T(8,128)(2,1)} %bitcast.9), calls=%async_computation | async-start | bytes 524288 | tf_op jit(solution)/shard_map/all_to_all | solution.py:410
  84.3 1.0 %copy-start.1 = (f32[256,512]{1,0:T(8,128)S(1)}, f32[256,512]{1,0:T(8,128)}, u32[]{:S(2)}) copy-start(f32[256,512]{1,0:T(8,128)} %copy-done) | copy-start | bytes 1572868
